TPU v7x, 32 devices: a whole 2x2x4 slice. The times are simulated.
32 devices in a mesh: dp: 4 (over x, core), feat: 8 (over z, y).
Axes of the slice: x: 2, y: 2, z: 4, core: 2. Of those that a mesh axis runs over, the one named last changes fastest.
Arguments:
- features: bfloat16 [6144, 65536], P('dp', 'feat'), may hold values from -64 to 64
- weight: float32 [16, 65536], P(None, 'feat'), may hold values from -1 to 1
- labels: int32 [6144], P('dp'), may hold values from 0 to 15
- sample_weight: int32 [6144], P('dp'), may hold values from 1 to 4
Outputs:
- logit_step: float32 [6144, 16], P('dp')
- mean_loss: float32 [], replicated
All inputs are finite; a program needn't handle non-finite values.
Results may differ from a plain program's by a relative error of at most 0.014.
Values may be sent and summed in bfloat16 or wider, within the bound.
No kernel may reach another device: no remote copies, remote signals or barrier semaphores. Data moves between devices by JAX's collectives and lax.ppermute only.
A program may use at most 64 MiB of HBM per device.

v0:
```python
import functools
import math

import jax
import jax.numpy as jnp
from jax import lax
from jax.sharding import PartitionSpec as P
import jax.experimental.pallas as pl
import jax.experimental.pallas.tpu as pltpu

CG_ITERS = 4
RIDGE_COEF = 0.1
NORM_GUARD = 1e-06
LANES = 128
VMEM_LIMIT = 4 * 2**20
TURNED = 3

F32 = jnp.float32
BF16 = jnp.bfloat16
NT = (((1,), (1,)), ((), ()))
NN = (((1,), (0,)), ((), ()))


def scalar_block(values, lane):
    rows = lax.broadcasted_iota(jnp.int32, (16, LANES), 0)
    lanes = lax.broadcasted_iota(jnp.int32, (16, LANES), 1)
    block = jnp.zeros((16, LANES), F32)
    for i, value in enumerate(values):
        rest = jnp.broadcast_to(value, (16, LANES))
        for part in range(3):
            piece = rest.astype(BF16).astype(F32)
            block = jnp.where(rows == 3 * i + part, piece, block)
            rest = rest - piece
    return jnp.where(lanes == lane, block, 0.0)


def read_scalar(block, i):
    rows = lax.broadcasted_iota(jnp.int32, (16, LANES), 0)
    mine = (rows >= 3 * i) & (rows < 3 * i + 3)
    return jnp.sum(jnp.where(mine, block, 0.0), keepdims=True)


def sum_all(value):
    return jnp.sum(value, keepdims=True)


def one_row(ref):
    return jnp.concatenate([ref[i : i + 1, :] for i in range(ref.shape[0])], axis=1)


def add_up(parts):
    values = [p[...].astype(F32) for p in parts]
    while len(values) > 1:
        values = [a + b for a, b in zip(values[::2], values[1::2])]
    return values[0]


def my_core():
    return lax.rem(lax.axis_index("dp"), 2)


class Store:
    def __init__(self, rows, columns):
        self.rows, self.columns = rows, columns
        self.width = math.gcd(math.gcd(rows, columns // 2), 512)
        self.groups = min(TURNED, rows // self.width)
        self.shape = (rows * columns // self.width + self.groups * columns, self.width)

    def block(self, j):
        return pl.ds(pl.multiple_of(j * self.rows, self.width), self.rows)

    def turned(self, i, first, count):
        start = self.rows * self.columns // self.width + i * self.columns + first
        return pl.ds(pl.multiple_of(start, LANES), count)


def load_kernel(x_hbm, w_hbm, x_ref, w_ref, l_ref, sems, w_sem, *, store, ahead):
    width = store.width
    blocks = store.columns // width

    def copy(j):
        cols = pl.ds(pl.multiple_of(j * width, width), width)
        return pltpu.make_async_copy(x_hbm.at[:, cols], x_ref.at[store.block(j)], sems.at[j])

    w_copy = pltpu.make_async_copy(w_hbm, w_ref, w_sem)
    w_copy.start()
    for j in range(min(ahead, blocks)):
        copy(j).start()
    l_ref[...] = jnp.zeros(l_ref.shape, F32)
    w_copy.wait()

    @pl.loop(0, blocks)
    def _(j):
        copy(j).wait()

        @pl.when(j + ahead < blocks)
        def _():
            copy(j + ahead).start()

        first = pl.multiple_of(j * width, width)
        w = w_ref[:, pl.ds(first, width)].astype(BF16)
        for i in range(store.rows // width):
            rows = pl.ds(pl.multiple_of(j * store.rows + i * width, width), width)
            turned = x_ref[rows, :].T
            if i < store.groups:
                x_ref[store.turned(i, first, width), :] = turned
            l_ref[:, i * width : (i + 1) * width] += lax.dot_general(
                w, turned, NN, preferred_element_type=F32
            )


def column_half(c, x_ref, which, out_ref, store):
    width = store.width
    count = store.columns // 2 // width
    for i in range(count):
        block = lax.dot_general(
            c, x_ref[store.block(which * count + i), :], NN, preferred_element_type=F32
        )
        out_ref[:, i * width : (i + 1) * width] = block.astype(out_ref.dtype)


def probs_kernel(*refs, n, store):
    parts, (labels_ref, weight_ref, x_ref, p_ref, e_ref, send_ref, block_ref) = refs[:n], refs[n:]
    logits = add_up(parts)
    classes = logits.shape[0]
    top = jnp.max(logits, axis=0, keepdims=True)
    shifted = jnp.exp(logits - top)
    summed = jnp.sum(shifted, axis=0, keepdims=True)
    prob = shifted / summed
    log_total = top + jnp.log(summed)
    row_weight = one_row(weight_ref).astype(F32)
    rows = lax.broadcasted_iota(jnp.int32, logits.shape, 0)
    onehot = (rows == one_row(labels_ref)).astype(F32)
    picked = jnp.sum(logits * onehot, axis=0, keepdims=True)
    p_ref[...] = prob
    e = (row_weight * (prob - onehot)).astype(BF16)
    e_ref[...] = e
    block = scalar_block(
        (sum_all(row_weight), sum_all(row_weight * (log_total - picked))), lax.axis_index("dp")
    )
    half = store.columns // 2
    block_ref[...] = block
    send_ref[:, half:] = block.astype(BF16)
    column_half(e, x_ref, 1 - my_core(), send_ref, store)


def curvature(parts, s_prev, sc_prev, p_ref, scale_ref):
    total = add_up(parts)
    rows = p_ref.shape[1]
    block = total[:, rows:]
    u = total[:, :rows]
    res_norm = read_scalar(block, 0)
    if s_prev is None:
        beta = jnp.zeros((1, 1), F32)
        s = u
        dir_norm = res_norm
    else:
        cross = read_scalar(block, 1)
        beta = res_norm / (sc_prev[0:1, 0:1] + NORM_GUARD)
        s = u + beta * s_prev[...]
        dir_norm = res_norm + 2.0 * beta * cross + beta * beta * sc_prev[1:2, 0:1]
    prob = p_ref[...]
    mixed = jnp.sum(prob * s, axis=0, keepdims=True)
    c = (scale_ref[...] * prob * (s - mixed)).astype(BF16)
    curv = sum_all(s * c.astype(F32))
    return s, c, curv, res_norm, dir_norm, beta


def curv_kernel(*refs, n, first, store):
    parts, refs = refs[:n], refs[n:]
    s_prev, sc_prev = None, None
    if not first:
        (s_prev, sc_prev), refs = refs[:2], refs[2:]
    p_ref, scale_ref, x_ref, s_ref, c_ref, send_ref, block_ref, sc_ref = refs
    s, c, curv, res_norm, dir_norm, beta = curvature(parts, s_prev, sc_prev, p_ref, scale_ref)
    s_ref[...] = s
    c_ref[...] = c
    sc_ref[0:1, :] = jnp.broadcast_to(res_norm, (1, LANES))
    sc_ref[1:2, :] = jnp.broadcast_to(dir_norm, (1, LANES))
    sc_ref[2:3, :] = jnp.broadcast_to(beta, (1, LANES))
    sc_ref[3:, :] = jnp.zeros((5, LANES), F32)
    block = scalar_block((curv,), lax.axis_index("dp"))
    half = store.columns // 2
    block_ref[...] = block
    send_ref[:, half:] = block.astype(BF16)
    column_half(c, x_ref, 1 - my_core(), send_ref, store)


def own_columns_kernel(c_ref, block_ref, x_ref, out_ref, *, store):
    half = store.columns // 2
    out_ref[:, half:] = block_ref[...]
    column_half(c_ref[...], x_ref, my_core(), out_ref, store)


def residual_out(residual, extra, r_ref, send_ref):
    half = residual.shape[1]
    r_ref[...] = residual
    send_ref[:, :half] = residual.astype(BF16)
    send_ref[:, half:] = scalar_block((sum_all(residual * residual),) + extra, 0).astype(BF16)


def gradient_kernel(*refs, n):
    parts, (w_ref, weight_ref, r_ref, send_ref, scale_ref, loss_ref) = refs[:n], refs[n:]
    total = add_up(parts)
    half = r_ref.shape[1]
    block = total[:, half:]
    weight_total = read_scalar(block, 0)
    loss_ref[...] = jnp.broadcast_to(read_scalar(block, 1) / weight_total, loss_ref.shape)
    scale_ref[...] = one_row(weight_ref).astype(F32) / weight_total
    weight = w_ref[:, pl.ds(pl.multiple_of(my_core() * half, LANES), half)]
    residual = -(total[:, :half] / weight_total + RIDGE_COEF * weight)
    residual_out(residual, (), r_ref, send_ref)


def update_kernel(*refs, n, first):
    parts, refs = refs[:n], refs[n:]
    (r_ref, sc_ref), refs = refs[:2], refs[2:]
    if first:
        r_out, d_out, send_ref, alpha_ref = refs
        direction = r_ref[...]
    else:
        d_ref, r_out, d_out, send_ref, alpha_ref = refs
        direction = r_ref[...] + sc_ref[2:3, 0:1] * d_ref[...]
    total = add_up(parts)
    half = r_ref.shape[1]
    curv = read_scalar(total[:, half:], 0) + RIDGE_COEF * sc_ref[1:2, 0:1]
    alpha = sc_ref[0:1, 0:1] / curv
    residual = r_ref[...] - alpha * (total[:, :half] + RIDGE_COEF * direction)
    d_out[...] = direction
    alpha_ref[...] = jnp.broadcast_to(alpha, alpha_ref.shape)
    residual_out(residual, (sum_all(residual * direction),), r_out, send_ref)


def row_half(h, x_ref, which, store, i):
    half, width = store.columns // 2, store.width
    if i < store.groups:
        return lax.dot_general(
            h, x_ref[store.turned(i, which * half, half), :], NN, preferred_element_type=F32
        )
    total = jnp.zeros((h.shape[0], width), F32)
    for j in range(half // width):
        first = (which * (half // width) + j) * store.rows + i * width
        block = x_ref[pl.ds(pl.multiple_of(first, width), width), :]
        total += lax.dot_general(
            h[:, j * width : (j + 1) * width], block, NT, preferred_element_type=F32
        )
    return total


def own_rows_kernel(send_ref, x_ref, out_ref, *, store):
    half, width = store.columns // 2, store.width
    h = send_ref[:, :half]
    for i in range(store.rows // width):
        out_ref[:, i * width : (i + 1) * width] = row_half(h, x_ref, my_core(), store, i)


def mate_rows_kernel(acc_ref, mine_ref, recv_ref, x_ref, out_ref, *, store):
    half, width = store.columns // 2, store.width
    h = recv_ref[:, :half]
    block = mine_ref[:, half:].astype(F32) + recv_ref[:, half:].astype(F32)
    lane = lax.axis_index("feat")
    out_ref[:, store.rows :] = scalar_block(
        (read_scalar(block, 0), read_scalar(block, 1)), lane
    ).astype(BF16)
    for i in range(store.rows // width):
        cols = slice(i * width, (i + 1) * width)
        part = acc_ref[:, cols] + row_half(h, x_ref, 1 - my_core(), store, i)
        out_ref[:, cols] = part.astype(BF16)


def last_kernel(*refs, n):
    parts, (s_prev, sc_prev, p_ref, scale_ref, s_ref, curv_ref) = refs[:n], refs[n:]
    s, c, curv, res_norm, dir_norm, beta = curvature(parts, s_prev, sc_prev, p_ref, scale_ref)
    s_ref[...] = s
    curv_ref[0:1, :] = jnp.broadcast_to(curv, (1, LANES))
    curv_ref[1:2, :] = jnp.broadcast_to(dir_norm, (1, LANES))
    curv_ref[2:3, :] = jnp.broadcast_to(res_norm, (1, LANES))
    curv_ref[3:, :] = jnp.zeros((5, LANES), F32)


def finish_kernel(curv_ref, sc_ref, loss_ref, *refs):
    count = (len(refs) - 2) // 2
    steps, scores, (out_ref, loss_out) = refs[:count], refs[count:-2], refs[-2:]
    loss_out[0, 0] = jnp.max(loss_ref[...])
    last = sc_ref[2:3, 0:1] / (curv_ref[0:1, 0:1] + RIDGE_COEF * sc_ref[1:2, 0:1])
    total = last * scores[-1][...]
    for alpha, score in zip(steps, scores[:-1]):
        total += alpha[0:1, 0:1] * score[...]
    out_ref[...] = total


def add_kernel(*refs):
    refs[-1][...] = add_up(refs[:-1]).astype(refs[-1].dtype)


def call(kernel, name, outs, *args, pins=(), scratch=(), keep=(), out_space=pltpu.VMEM, out_specs=(), limit=VMEM_LIMIT):
    def body(*refs):
        kernel(*refs[: len(args)], *refs[len(args) + len(pins) :])

    args_pins = args + tuple(pltpu.with_memory_space_constraint(p, pltpu.VMEM) for p in pins)
    specs = [
        pl.BlockSpec(memory_space=pl.ANY if i in keep else pltpu.VMEM)
        for i in range(len(args_pins))
    ]
    return pl.pallas_call(
        body,
        out_shape=tuple(out_space(shape, dtype) for shape, dtype in outs),
        in_specs=specs,
        out_specs=tuple(pl.BlockSpec(memory_space=m) for m in out_specs or [pltpu.VMEM] * len(outs)),
        scratch_shapes=scratch,
        compiler_params=pltpu.CompilerParams(vmem_limit_bytes=limit),
        name=name,
    )(*args_pins)


def add(pins, *values, kind):
    return call(add_kernel, "add", [(values[0].shape, kind)], *values, pins=pins)[0]


def swap(value, axis, size, bit):
    return lax.ppermute(value, axis, [(i, i ^ bit) for i in range(size)])


def gather_sum(value, pins, axis, size, bits):
    kind = value.dtype
    while len(bits) > 2:
        value = add(pins, value, swap(value, axis, size, bits[0]), kind=kind)
        bits = bits[1:]
    if len(bits) == 1:
        return [value, swap(value, axis, size, bits[0])]
    a, b = bits
    return [value] + [swap(value, axis, size, k) for k in (a, b, a | b)]


def bits_of(size):
    return [1 << i for i in range(size.bit_length() - 1)]


def on_device(features, weight, labels, sample_weight, *, dp, feat):
    classes, columns = weight.shape
    rows = features.shape[0]
    half = columns // 2
    labels = labels.reshape(rows // LANES, LANES)
    row_weight = sample_weight.reshape(rows // LANES, LANES)
    across_feat = functools.partial(gather_sum, axis="feat", size=feat, bits=bits_of(feat))
    across_chips = functools.partial(gather_sum, axis="dp", size=dp, bits=bits_of(dp)[1:])

    def core_swap(value):
        return swap(value, "dp", dp, 1)

    store = Store(rows, columns)
    x, weight, logit_part = call(
        functools.partial(load_kernel, store=store, ahead=4),
        "load",
        [(store.shape, BF16), ((classes, columns), F32), ((classes, rows), F32)],
        features,
        weight,
        scratch=(pltpu.SemaphoreType.DMA((columns // store.width,)), pltpu.SemaphoreType.DMA),
        keep=(0, 1),
        limit=VMEM_LIMIT - weight.size * weight.dtype.itemsize,
    )
    x = pltpu.with_memory_space_constraint(x, pltpu.VMEM)
    pins = [x, weight]

    def column_sums(c, send, block):
        received = core_swap(send)
        (own,) = call(
            functools.partial(own_columns_kernel, store=store),
            "own_columns",
            [((classes, half + LANES), F32)],
            c,
            block,
            x,
            pins=pins,
        )
        return across_chips(add(pins, own, received, kind=BF16), pins)

    def row_sums(send):
        received = core_swap(send)
        (part,) = call(
            functools.partial(own_rows_kernel, store=store),
            "own_rows",
            [((classes, rows), F32)],
            send,
            x,
            pins=pins,
        )
        (score,) = call(
            functools.partial(mate_rows_kernel, store=store),
            "mate_rows",
            [((classes, rows + LANES), BF16)],
            part,
            send,
            received,
            x,
            pins=pins,
        )
        return across_feat(score, pins)

    curv_outs = [
        ((classes, rows), BF16),
        ((classes, half + LANES), BF16),
        ((16, LANES), F32),
    ]
    parts = across_feat(logit_part, pins)
    prob, e, send, block = call(
        functools.partial(probs_kernel, n=len(parts), store=store),
        "probs",
        [((classes, rows), F32)] + curv_outs,
        *parts,
        labels,
        row_weight,
        x,
        pins=pins,
    )
    parts = column_sums(e, send, block)
    residual, send, scale, loss = call(
        functools.partial(gradient_kernel, n=len(parts)),
        "gradient",
        [((classes, half), F32), ((classes, half + LANES), BF16), ((1, rows), F32), ((8, LANES), F32)],
        *parts,
        weight,
        row_weight,
        pins=pins,
    )
    pins[1:] = [residual]
    state, steps, scores = (), [], []
    direction = ()
    for i in range(CG_ITERS - 1):
        parts = row_sums(send)
        s, c, send, block, sc = call(
            functools.partial(curv_kernel, n=len(parts), first=i == 0, store=store),
            "curvature",
            [((classes, rows), F32)] + curv_outs + [((8, LANES), F32)],
            *parts,
            *state,
            prob,
            scale,
            x,
            pins=pins,
        )
        state = (s, sc)
        scores.append(s)
        parts = column_sums(c, send, block)
        residual, new_direction, send, alpha = call(
            functools.partial(update_kernel, n=len(parts), first=i == 0),
            "update",
            [((classes, half), F32)] * 2 + [((classes, half + LANES), BF16), ((8, LANES), F32)],
            *parts,
            residual,
            sc,
            *direction,
            pins=pins,
        )
        pins[1:] = [residual, new_direction] if i < CG_ITERS - 2 else []
        direction = (new_direction,)
        steps.append(alpha)
    parts = row_sums(send)
    s, sc = call(
        functools.partial(last_kernel, n=len(parts)),
        "last",
        [((classes, rows), F32), ((8, LANES), F32)],
        *parts,
        *state,
        prob,
        scale,
        pins=pins,
    )
    scores.append(s)
    curv = sc
    for bit in bits_of(dp):
        curv = add(pins, curv, swap(curv, "dp", dp, bit), kind=F32)
    out, loss = call(
        finish_kernel,
        "finish",
        [((classes, rows), F32), ((1, 1), F32)],
        curv,
        sc,
        loss,
        *steps,
        *scores,
        out_space=jax.ShapeDtypeStruct,
        out_specs=(pltpu.VMEM, pltpu.SMEM),
    )
    return out.T, loss.reshape(())


def solution(mesh):
    dp, feat = mesh.shape["dp"], mesh.shape["feat"]
    in_specs = (P("dp", "feat"), P(None, "feat"), P("dp"), P("dp"))
    out_specs = (P("dp", None), P())
    return jax.shard_map(
        functools.partial(on_device, dp=dp, feat=feat),
        mesh=mesh,
        in_specs=in_specs,
        out_specs=out_specs,
        check_vma=False,
    )
```

profile of v0, /device:TPU:0, one launch (start us, length us, event | category | flops | bytes accessed | tf_op | source)
XLA Modules:
  0.0 142.8 jit_solution(10251232916048882183)
XLA Ops:
  1.7 14.3 %load.1 = (bf16[49152,512]{1,0:T(8,128)(2,1)S(1)}, f32[16,8192]{1,0:T(8,128)S(1)}, f32[16,1536]{1,0:T(8,128)S(1)}) custom-call(bf16[1536,8192]{1,0:T(8,128)(2,1)} %refs_0_.1, f32[16,8192]{1,0:T(8,128)S(1)} %copy-done), custom_call_target="tpu_custom_call" | custom-call | tf_op jit(solution)/shard_map/load/pallas_call | solution.py:305
  16.0 3.0 %collective-permute-start = (f32[16,1536]{1,0:T(8,128)S(1)}, f32[16,1536]{1,0:T(8,128)S(1)}, u32[]{:S(2)}, u32[]{:S(2)}) collective-permute-start(f32[16,1536]{1,0:T(8,128)S(1)} %get-tuple-element.42.refs_0_), channel_id=1, source_target_pairs={{0,1},{1,0},{2,3},{3,2},{4,5},{5,4},{6,7},{7,6},{8,9},{9,8},{10,11... | collective-permute-start | bytes 294920 | tf_op jit(solution)/shard_map/ppermute | solution.py:321
  19.0 2.8 %collective-permute-done.refs_1_ = f32[16,1536]{1,0:T(8,128)S(1)} collective-permute-done((f32[16,1536]{1,0:T(8,128)S(1)}, f32[16,1536]{1,0:T(8,128)S(1)}, u32[]{:S(2)}, u32[]{:S(2)}) %collective-permute-start) | collective-permute-done | bytes 98336 | tf_op jit(solution)/shard_map/ppermute | solution.py:321
  21.8 4.0 %collective-permute-start.3 = (f32[16,1536]{1,0:T(8,128)S(1)}, f32[16,1536]{1,0:T(8,128)S(1)}, u32[]{:S(2)}, u32[]{:S(2)}) collective-permute-start(f32[16,1536]{1,0:T(8,128)S(1)} %add.11.refs_0_), channel_id=1, source_target_pairs={{0,6},{1,7},{2,4},{3,5},{4,2},{5,3},{6,0},{7,1},{8,14},{9,15},{10,... | collective-permute-start | bytes 294920 | tf_op jit(solution)/shard_map/ppermute | solution.py:321
  26.4 2.5 %collective-permute-done.3.refs_3_ = f32[16,1536]{1,0:T(8,128)S(1)} collective-permute-done((f32[16,1536]{1,0:T(8,128)S(1)}, f32[16,1536]{1,0:T(8,128)S(1)}, u32[]{:S(2)}, u32[]{:S(2)}) %collective-permute-start.3) | collective-permute-done | bytes 98336 | tf_op jit(solution)/shard_map/ppermute | solution.py:321
  28.9 4.1 %collective-permute-done.2.refs_2_ = f32[16,1536]{1,0:T(8,128)S(1)} collective-permute-done((f32[16,1536]{1,0:T(8,128)S(1)}, f32[16,1536]{1,0:T(8,128)S(1)}, u32[]{:S(2)}, u32[]{:S(2)}) %collective-permute-start.2) | collective-permute-done | bytes 98336 | tf_op jit(solution)/shard_map/ppermute | solution.py:321
  38.2 4.5 %collective-permute-done.5.refs_1_ = bf16[16,4224]{1,0:T(8,128)(2,1)S(1)} collective-permute-done((bf16[16,4224]{1,0:T(8,128)(2,1)S(1)}, bf16[16,4224]{1,0:T(8,128)(2,1)S(1)}, u32[]{:S(2)}, u32[]{:S(2)}) %collective-permute-start.5) | collective-permute-done | bytes 135200 | tf_op jit(solution)/shard_map/ppermute | solution.py:321
  48.1 2.7 %collective-permute-done.7.refs_1_ = bf16[16,1664]{1,0:T(8,128)(2,1)S(1)} collective-permute-done((bf16[16,1664]{1,0:T(8,128)(2,1)S(1)}, bf16[16,1664]{1,0:T(8,128)(2,1)S(1)}, u32[]{:S(2)}, u32[]{:S(2)}) %collective-permute-start.7) | collective-permute-done | bytes 53280 | tf_op jit(solution)/shard_map/ppermute | solution.py:321
  50.9 2.6 %collective-permute-start.10 = (bf16[16,1664]{1,0:T(8,128)(2,1)S(1)}, bf16[16,1664]{1,0:T(8,128)(2,1)S(1)}, u32[]{:S(2)}, u32[]{:S(2)}) collective-permute-start(bf16[16,1664]{1,0:T(8,128)(2,1)S(1)} %add.13.refs_0_), channel_id=1, source_target_pairs={{0,6},{1,7},{2,4},{3,5},{4,2},{5,3},{6,0},{7,1},{8,14},{9,15},{10,... | collective-permute-start | bytes 159752 | tf_op jit(solution)/shard_map/ppermute | solution.py:321
  63.7 4.7 %collective-permute-done.12.refs_1_ = bf16[16,4224]{1,0:T(8,128)(2,1)S(1)} collective-permute-done((bf16[16,4224]{1,0:T(8,128)(2,1)S(1)}, bf16[16,4224]{1,0:T(8,128)(2,1)S(1)}, u32[]{:S(2)}, u32[]{:S(2)}) %collective-permute-start.12) | collective-permute-done | bytes 135200 | tf_op jit(solution)/shard_map/ppermute | solution.py:321
  73.7 2.9 %collective-permute-done.14.refs_1_ = bf16[16,1664]{1,0:T(8,128)(2,1)S(1)} collective-permute-done((bf16[16,1664]{1,0:T(8,128)(2,1)S(1)}, bf16[16,1664]{1,0:T(8,128)(2,1)S(1)}, u32[]{:S(2)}, u32[]{:S(2)}) %collective-permute-start.14) | collective-permute-done | bytes 53280 | tf_op jit(solution)/shard_map/ppermute | solution.py:321
  76.6 2.4 %collective-permute-start.17 = (bf16[16,1664]{1,0:T(8,128)(2,1)S(1)}, bf16[16,1664]{1,0:T(8,128)(2,1)S(1)}, u32[]{:S(2)}, u32[]{:S(2)}) collective-permute-start(bf16[16,1664]{1,0:T(8,128)(2,1)S(1)} %add.15.refs_0_), channel_id=1, source_target_pairs={{0,6},{1,7},{2,4},{3,5},{4,2},{5,3},{6,0},{7,1},{8,14},{9,15},{10,... | collective-permute-start | bytes 159752 | tf_op jit(solution)/shard_map/ppermute | solution.py:321
  78.9 2.1 %collective-permute-start.15 = (bf16[16,1664]{1,0:T(8,128)(2,1)S(1)}, bf16[16,1664]{1,0:T(8,128)(2,1)S(1)}, u32[]{:S(2)}, u32[]{:S(2)}) collective-permute-start(bf16[16,1664]{1,0:T(8,128)(2,1)S(1)} %add.15.refs_0_), channel_id=1, source_target_pairs={{0,2},{1,3},{2,0},{3,1},{4,6},{5,7},{6,4},{7,5},{8,10},{9,11},{10,... | collective-permute-start | bytes 159752 | tf_op jit(solution)/shard_map/ppermute | solution.py:321
  84.4 1.9 %curvature.4 = (f32[16,1536]{1,0:T(8,128)S(1)}, bf16[16,1536]{1,0:T(8,128)(2,1)S(1)}, bf16[16,4224]{1,0:T(8,128)(2,1)S(1)}, f32[16,128]{1,0:T(8,128)S(1)}, f32[8,128]{1,0:T(8,128)S(1)}) custom-call(bf16[16,1664]{1,0:T(8,128)(2,1)S(1)} %add.15.refs_0_, bf16[16,1664]{1,0:T(8,128)(2,1)S(1)} %collective-permute-done.15.refs_1_, ...), custom_call_target="tpu_custom_call" | custom-call | tf_op jit(solution)/shard_map/curvature/pallas_call | solution.py:305
  86.3 1.9 %own_columns.6.refs_0_ = f32[16,4224]{1,0:T(8,128)S(1)} custom-call(bf16[16,1536]{1,0:T(8,128)(2,1)S(1)} %get-tuple-element.60.refs_0_, f32[16,128]{1,0:T(8,128)S(1)} %get-tuple-element.61.refs_1_, bf16[49152,512]{1,0:T(8,128)(2,1)S(1)} %get-tuple-element.43.refs_2_.refs_6_.refs_7_.refs_3_.refs_4_.refs_1_.refs_8_.refs_9_.refs_5_, ...), custom_call_target="tpu_custom_call" | custom-call | tf_op jit(solution)/shard_map/own_columns/pallas_call | solution.py:305
  89.8 4.5 %collective-permute-done.19.refs_1_ = bf16[16,4224]{1,0:T(8,128)(2,1)S(1)} collective-permute-done((bf16[16,4224]{1,0:T(8,128)(2,1)S(1)}, bf16[16,4224]{1,0:T(8,128)(2,1)S(1)}, u32[]{:S(2)}, u32[]{:S(2)}) %collective-permute-start.19) | collective-permute-done | bytes 135200 | tf_op jit(solution)/shard_map/ppermute | solution.py:321
  99.8 2.7 %collective-permute-done.21.refs_1_ = bf16[16,1664]{1,0:T(8,128)(2,1)S(1)} collective-permute-done((bf16[16,1664]{1,0:T(8,128)(2,1)S(1)}, bf16[16,1664]{1,0:T(8,128)(2,1)S(1)}, u32[]{:S(2)}, u32[]{:S(2)}) %collective-permute-start.21) | collective-permute-done | bytes 53280 | tf_op jit(solution)/shard_map/ppermute | solution.py:321
  102.6 2.6 %collective-permute-start.24 = (bf16[16,1664]{1,0:T(8,128)(2,1)S(1)}, bf16[16,1664]{1,0:T(8,128)(2,1)S(1)}, u32[]{:S(2)}, u32[]{:S(2)}) collective-permute-start(bf16[16,1664]{1,0:T(8,128)(2,1)S(1)} %add.17.refs_0_), channel_id=1, source_target_pairs={{0,6},{1,7},{2,4},{3,5},{4,2},{5,3},{6,0},{7,1},{8,14},{9,15},{10,... | collective-permute-start | bytes 159752 | tf_op jit(solution)/shard_map/ppermute | solution.py:321
  110.4 1.9 %curvature.5 = (f32[16,1536]{1,0:T(8,128)S(1)}, bf16[16,1536]{1,0:T(8,128)(2,1)S(1)}, bf16[16,4224]{1,0:T(8,128)(2,1)S(1)}, f32[16,128]{1,0:T(8,128)S(1)}, f32[8,128]{1,0:T(8,128)S(1)}) custom-call(bf16[16,1664]{1,0:T(8,128)(2,1)S(1)} %add.17.refs_0_, bf16[16,1664]{1,0:T(8,128)(2,1)S(1)} %collective-permute-done.22.refs_1_, ...), custom_call_target="tpu_custom_call" | custom-call | tf_op jit(solution)/shard_map/curvature/pallas_call | solution.py:305
  115.5 4.7 %collective-permute-done.26.refs_1_ = bf16[16,4224]{1,0:T(8,128)(2,1)S(1)} collective-permute-done((bf16[16,4224]{1,0:T(8,128)(2,1)S(1)}, bf16[16,4224]{1,0:T(8,128)(2,1)S(1)}, u32[]{:S(2)}, u32[]{:S(2)}) %collective-permute-start.26) | collective-permute-done | bytes 135200 | tf_op jit(solution)/shard_map/ppermute | solution.py:321
  126.0 2.9 %collective-permute-done.28.refs_1_ = bf16[16,1664]{1,0:T(8,128)(2,1)S(1)} collective-permute-done((bf16[16,1664]{1,0:T(8,128)(2,1)S(1)}, bf16[16,1664]{1,0:T(8,128)(2,1)S(1)}, u32[]{:S(2)}, u32[]{:S(2)}) %collective-permute-start.28) | collective-permute-done | bytes 53280 | tf_op jit(solution)/shard_map/ppermute | solution.py:321
  128.9 2.3 %collective-permute-start.31 = (bf16[16,1664]{1,0:T(8,128)(2,1)S(1)}, bf16[16,1664]{1,0:T(8,128)(2,1)S(1)}, u32[]{:S(2)}, u32[]{:S(2)}) collective-permute-start(bf16[16,1664]{1,0:T(8,128)(2,1)S(1)} %add.19.refs_0_), channel_id=1, source_target_pairs={{0,6},{1,7},{2,4},{3,5},{4,2},{5,3},{6,0},{7,1},{8,14},{9,15},{10,... | collective-permute-start | bytes 159752 | tf_op jit(solution)/shard_map/ppermute | solution.py:321
  131.2 2.1 %collective-permute-start.29 = (bf16[16,1664]{1,0:T(8,128)(2,1)S(1)}, bf16[16,1664]{1,0:T(8,128)(2,1)S(1)}, u32[]{:S(2)}, u32[]{:S(2)}) collective-permute-start(bf16[16,1664]{1,0:T(8,128)(2,1)S(1)} %add.19.refs_0_), channel_id=1, source_target_pairs={{0,2},{1,3},{2,0},{3,1},{4,6},{5,7},{6,4},{7,5},{8,10},{9,11},{10,... | collective-permute-start | bytes 159752 | tf_op jit(solution)/shard_map/ppermute | solution.py:321
  139.7 2.1 %collective-permute-done.33.refs_1_ = f32[8,128]{1,0:T(8,128)S(1)} collective-permute-done((f32[8,128]{1,0:T(8,128)S(1)}, f32[8,128]{1,0:T(8,128)S(1)}, u32[]{:S(2)}, u32[]{:S(2)}) %collective-permute-start.33) | collective-permute-done | bytes 4128 | tf_op jit(solution)/shard_map/ppermute | solution.py:321
  (92 shorter events, 59.7 us)
Async XLA Ops:
  16.0 5.8 %collective-permute-start = (f32[16,1536]{1,0:T(8,128)S(1)}, f32[16,1536]{1,0:T(8,128)S(1)}, u32[]{:S(2)}, u32[]{:S(2)}) collective-permute-start(f32[16,1536]{1,0:T(8,128)S(1)} %get-tuple-element.42.refs_0_), channel_id=1, source_target_pairs={{0,1},{1,0},{2,3},{3,2},{4,5},{5,4},{6,7},{7,6},{8,9},{9,8},{10,11... | collective-permute-start | bytes 294920 | tf_op jit(solution)/shard_map/ppermute | solution.py:321
  21.8 7.1 %collective-permute-start.3 = (f32[16,1536]{1,0:T(8,128)S(1)}, f32[16,1536]{1,0:T(8,128)S(1)}, u32[]{:S(2)}, u32[]{:S(2)}) collective-permute-start(f32[16,1536]{1,0:T(8,128)S(1)} %add.11.refs_0_), channel_id=1, source_target_pairs={{0,6},{1,7},{2,4},{3,5},{4,2},{5,3},{6,0},{7,1},{8,14},{9,15},{10,... | collective-permute-start | bytes 294920 | tf_op jit(solution)/shard_map/ppermute | solution.py:321
  25.8 7.2 %collective-permute-start.2 = (f32[16,1536]{1,0:T(8,128)S(1)}, f32[16,1536]{1,0:T(8,128)S(1)}, u32[]{:S(2)}, u32[]{:S(2)}) collective-permute-start(f32[16,1536]{1,0:T(8,128)S(1)} %add.11.refs_0_), channel_id=1, source_target_pairs={{0,4},{1,5},{2,6},{3,7},{4,0},{5,1},{6,2},{7,3},{8,12},{9,13},{10,... | collective-permute-start | bytes 294920 | tf_op jit(solution)/shard_map/ppermute | solution.py:321
  25.8 7.2 %collective-permute-start.1 = (f32[16,1536]{1,0:T(8,128)S(1)}, f32[16,1536]{1,0:T(8,128)S(1)}, u32[]{:S(2)}, u32[]{:S(2)}) collective-permute-start(f32[16,1536]{1,0:T(8,128)S(1)} %add.11.refs_0_), channel_id=1, source_target_pairs={{0,2},{1,3},{2,0},{3,1},{4,6},{5,7},{6,4},{7,5},{8,10},{9,11},{10,... | collective-permute-start | bytes 294920 | tf_op jit(solution)/shard_map/ppermute | solution.py:321
  36.6 6.0 %collective-permute-start.5 = (bf16[16,4224]{1,0:T(8,128)(2,1)S(1)}, bf16[16,4224]{1,0:T(8,128)(2,1)S(1)}, u32[]{:S(2)}, u32[]{:S(2)}) collective-permute-start(bf16[16,4224]{1,0:T(8,128)(2,1)S(1)} %add.12.refs_0_), channel_id=1, source_target_pairs={{0,16},{8,24},{16,0},{24,8},{1,17},{9,25},{17,1},{25,9},{2,18},{10... | collective-permute-start | bytes 405512 | tf_op jit(solution)/shard_map/ppermute | solution.py:321
  46.6 4.2 %collective-permute-start.7 = (bf16[16,1664]{1,0:T(8,128)(2,1)S(1)}, bf16[16,1664]{1,0:T(8,128)(2,1)S(1)}, u32[]{:S(2)}, u32[]{:S(2)}) collective-permute-start(bf16[16,1664]{1,0:T(8,128)(2,1)S(1)} %mate_rows.4.refs_0_), channel_id=1, source_target_pairs={{0,1},{1,0},{2,3},{3,2},{4,5},{5,4},{6,7},{7,6},{8,9},{9,8},{10,11... | collective-permute-start | bytes 159752 | tf_op jit(solution)/shard_map/ppermute | solution.py:321
  50.9 6.0 %collective-permute-start.10 = (bf16[16,1664]{1,0:T(8,128)(2,1)S(1)}, bf16[16,1664]{1,0:T(8,128)(2,1)S(1)}, u32[]{:S(2)}, u32[]{:S(2)}) collective-permute-start(bf16[16,1664]{1,0:T(8,128)(2,1)S(1)} %add.13.refs_0_), channel_id=1, source_target_pairs={{0,6},{1,7},{2,4},{3,5},{4,2},{5,3},{6,0},{7,1},{8,14},{9,15},{10,... | collective-permute-start | bytes 159752 | tf_op jit(solution)/shard_map/ppermute | solution.py:321
  53.5 5.2 %collective-permute-start.9 = (bf16[16,1664]{1,0:T(8,128)(2,1)S(1)}, bf16[16,1664]{1,0:T(8,128)(2,1)S(1)}, u32[]{:S(2)}, u32[]{:S(2)}) collective-permute-start(bf16[16,1664]{1,0:T(8,128)(2,1)S(1)} %add.13.refs_0_), channel_id=1, source_target_pairs={{0,4},{1,5},{2,6},{3,7},{4,0},{5,1},{6,2},{7,3},{8,12},{9,13},{10,... | collective-permute-start | bytes 159752 | tf_op jit(solution)/shard_map/ppermute | solution.py:321
  53.5 5.2 %collective-permute-start.8 = (bf16[16,1664]{1,0:T(8,128)(2,1)S(1)}, bf16[16,1664]{1,0:T(8,128)(2,1)S(1)}, u32[]{:S(2)}, u32[]{:S(2)}) collective-permute-start(bf16[16,1664]{1,0:T(8,128)(2,1)S(1)} %add.13.refs_0_), channel_id=1, source_target_pairs={{0,2},{1,3},{2,0},{3,1},{4,6},{5,7},{6,4},{7,5},{8,10},{9,11},{10,... | collective-permute-start | bytes 159752 | tf_op jit(solution)/shard_map/ppermute | solution.py:321
  62.3 6.0 %collective-permute-start.12 = (bf16[16,4224]{1,0:T(8,128)(2,1)S(1)}, bf16[16,4224]{1,0:T(8,128)(2,1)S(1)}, u32[]{:S(2)}, u32[]{:S(2)}) collective-permute-start(bf16[16,4224]{1,0:T(8,128)(2,1)S(1)} %add.14.refs_0_), channel_id=1, source_target_pairs={{0,16},{8,24},{16,0},{24,8},{1,17},{9,25},{17,1},{25,9},{2,18},{10... | collective-permute-start | bytes 405512 | tf_op jit(solution)/shard_map/ppermute | solution.py:321
  72.3 4.2 %collective-permute-start.14 = (bf16[16,1664]{1,0:T(8,128)(2,1)S(1)}, bf16[16,1664]{1,0:T(8,128)(2,1)S(1)}, u32[]{:S(2)}, u32[]{:S(2)}) collective-permute-start(bf16[16,1664]{1,0:T(8,128)(2,1)S(1)} %mate_rows.5.refs_0_), channel_id=1, source_target_pairs={{0,1},{1,0},{2,3},{3,2},{4,5},{5,4},{6,7},{7,6},{8,9},{9,8},{10,11... | collective-permute-start | bytes 159752 | tf_op jit(solution)/shard_map/ppermute | solution.py:321
  76.6 6.0 %collective-permute-start.17 = (bf16[16,1664]{1,0:T(8,128)(2,1)S(1)}, bf16[16,1664]{1,0:T(8,128)(2,1)S(1)}, u32[]{:S(2)}, u32[]{:S(2)}) collective-permute-start(bf16[16,1664]{1,0:T(8,128)(2,1)S(1)} %add.15.refs_0_), channel_id=1, source_target_pairs={{0,6},{1,7},{2,4},{3,5},{4,2},{5,3},{6,0},{7,1},{8,14},{9,15},{10,... | collective-permute-start | bytes 159752 | tf_op jit(solution)/shard_map/ppermute | solution.py:321
  78.9 5.4 %collective-permute-start.16 = (bf16[16,1664]{1,0:T(8,128)(2,1)S(1)}, bf16[16,1664]{1,0:T(8,128)(2,1)S(1)}, u32[]{:S(2)}, u32[]{:S(2)}) collective-permute-start(bf16[16,1664]{1,0:T(8,128)(2,1)S(1)} %add.15.refs_0_), channel_id=1, source_target_pairs={{0,4},{1,5},{2,6},{3,7},{4,0},{5,1},{6,2},{7,3},{8,12},{9,13},{10,... | collective-permute-start | bytes 159752 | tf_op jit(solution)/shard_map/ppermute | solution.py:321
  78.9 5.4 %collective-permute-start.15 = (bf16[16,1664]{1,0:T(8,128)(2,1)S(1)}, bf16[16,1664]{1,0:T(8,128)(2,1)S(1)}, u32[]{:S(2)}, u32[]{:S(2)}) collective-permute-start(bf16[16,1664]{1,0:T(8,128)(2,1)S(1)} %add.15.refs_0_), channel_id=1, source_target_pairs={{0,2},{1,3},{2,0},{3,1},{4,6},{5,7},{6,4},{7,5},{8,10},{9,11},{10,... | collective-permute-start | bytes 159752 | tf_op jit(solution)/shard_map/ppermute | solution.py:321
  88.3 6.1 %collective-permute-start.19 = (bf16[16,4224]{1,0:T(8,128)(2,1)S(1)}, bf16[16,4224]{1,0:T(8,128)(2,1)S(1)}, u32[]{:S(2)}, u32[]{:S(2)}) collective-permute-start(bf16[16,4224]{1,0:T(8,128)(2,1)S(1)} %add.16.refs_0_), channel_id=1, source_target_pairs={{0,16},{8,24},{16,0},{24,8},{1,17},{9,25},{17,1},{25,9},{2,18},{10... | collective-permute-start | bytes 405512 | tf_op jit(solution)/shard_map/ppermute | solution.py:321
  98.3 4.2 %collective-permute-start.21 = (bf16[16,1664]{1,0:T(8,128)(2,1)S(1)}, bf16[16,1664]{1,0:T(8,128)(2,1)S(1)}, u32[]{:S(2)}, u32[]{:S(2)}) collective-permute-start(bf16[16,1664]{1,0:T(8,128)(2,1)S(1)} %mate_rows.6.refs_0_), channel_id=1, source_target_pairs={{0,1},{1,0},{2,3},{3,2},{4,5},{5,4},{6,7},{7,6},{8,9},{9,8},{10,11... | collective-permute-start | bytes 159752 | tf_op jit(solution)/shard_map/ppermute | solution.py:321
  102.6 6.0 %collective-permute-start.24 = (bf16[16,1664]{1,0:T(8,128)(2,1)S(1)}, bf16[16,1664]{1,0:T(8,128)(2,1)S(1)}, u32[]{:S(2)}, u32[]{:S(2)}) collective-permute-start(bf16[16,1664]{1,0:T(8,128)(2,1)S(1)} %add.17.refs_0_), channel_id=1, source_target_pairs={{0,6},{1,7},{2,4},{3,5},{4,2},{5,3},{6,0},{7,1},{8,14},{9,15},{10,... | collective-permute-start | bytes 159752 | tf_op jit(solution)/shard_map/ppermute | solution.py:321
  105.2 5.2 %collective-permute-start.23 = (bf16[16,1664]{1,0:T(8,128)(2,1)S(1)}, bf16[16,1664]{1,0:T(8,128)(2,1)S(1)}, u32[]{:S(2)}, u32[]{:S(2)}) collective-permute-start(bf16[16,1664]{1,0:T(8,128)(2,1)S(1)} %add.17.refs_0_), channel_id=1, source_target_pairs={{0,4},{1,5},{2,6},{3,7},{4,0},{5,1},{6,2},{7,3},{8,12},{9,13},{10,... | collective-permute-start | bytes 159752 | tf_op jit(solution)/shard_map/ppermute | solution.py:321
  105.2 5.2 %collective-permute-start.22 = (bf16[16,1664]{1,0:T(8,128)(2,1)S(1)}, bf16[16,1664]{1,0:T(8,128)(2,1)S(1)}, u32[]{:S(2)}, u32[]{:S(2)}) collective-permute-start(bf16[16,1664]{1,0:T(8,128)(2,1)S(1)} %add.17.refs_0_), channel_id=1, source_target_pairs={{0,2},{1,3},{2,0},{3,1},{4,6},{5,7},{6,4},{7,5},{8,10},{9,11},{10,... | collective-permute-start | bytes 159752 | tf_op jit(solution)/shard_map/ppermute | solution.py:321
  114.1 6.1 %collective-permute-start.26 = (bf16[16,4224]{1,0:T(8,128)(2,1)S(1)}, bf16[16,4224]{1,0:T(8,128)(2,1)S(1)}, u32[]{:S(2)}, u32[]{:S(2)}) collective-permute-start(bf16[16,4224]{1,0:T(8,128)(2,1)S(1)} %add.18.refs_0_), channel_id=1, source_target_pairs={{0,16},{8,24},{16,0},{24,8},{1,17},{9,25},{17,1},{25,9},{2,18},{10... | collective-permute-start | bytes 405512 | tf_op jit(solution)/shard_map/ppermute | solution.py:321
  124.6 4.2 %collective-permute-start.28 = (bf16[16,1664]{1,0:T(8,128)(2,1)S(1)}, bf16[16,1664]{1,0:T(8,128)(2,1)S(1)}, u32[]{:S(2)}, u32[]{:S(2)}) collective-permute-start(bf16[16,1664]{1,0:T(8,128)(2,1)S(1)} %mate_rows.7.refs_0_), channel_id=1, source_target_pairs={{0,1},{1,0},{2,3},{3,2},{4,5},{5,4},{6,7},{7,6},{8,9},{9,8},{10,11... | collective-permute-start | bytes 159752 | tf_op jit(solution)/shard_map/ppermute | solution.py:321
  128.9 6.0 %collective-permute-start.31 = (bf16[16,1664]{1,0:T(8,128)(2,1)S(1)}, bf16[16,1664]{1,0:T(8,128)(2,1)S(1)}, u32[]{:S(2)}, u32[]{:S(2)}) collective-permute-start(bf16[16,1664]{1,0:T(8,128)(2,1)S(1)} %add.19.refs_0_), channel_id=1, source_target_pairs={{0,6},{1,7},{2,4},{3,5},{4,2},{5,3},{6,0},{7,1},{8,14},{9,15},{10,... | collective-permute-start | bytes 159752 | tf_op jit(solution)/shard_map/ppermute | solution.py:321
  131.2 5.4 %collective-permute-start.30 = (bf16[16,1664]{1,0:T(8,128)(2,1)S(1)}, bf16[16,1664]{1,0:T(8,128)(2,1)S(1)}, u32[]{:S(2)}, u32[]{:S(2)}) collective-permute-start(bf16[16,1664]{1,0:T(8,128)(2,1)S(1)} %add.19.refs_0_), channel_id=1, source_target_pairs={{0,4},{1,5},{2,6},{3,7},{4,0},{5,1},{6,2},{7,3},{8,12},{9,13},{10,... | collective-permute-start | bytes 159752 | tf_op jit(solution)/shard_map/ppermute | solution.py:321
  131.2 5.4 %collective-permute-start.29 = (bf16[16,1664]{1,0:T(8,128)(2,1)S(1)}, bf16[16,1664]{1,0:T(8,128)(2,1)S(1)}, u32[]{:S(2)}, u32[]{:S(2)}) collective-permute-start(bf16[16,1664]{1,0:T(8,128)(2,1)S(1)} %add.19.refs_0_), channel_id=1, source_target_pairs={{0,2},{1,3},{2,0},{3,1},{4,6},{5,7},{6,4},{7,5},{8,10},{9,11},{10,... | collective-permute-start | bytes 159752 | tf_op jit(solution)/shard_map/ppermute | solution.py:321
  (17 other events, 140.8 us)
where the time goes:
time: 143 us
  waiting for transfers between devices  55.6 us (39%)
  Pallas kernels  46.3 us (32%)
  starting transfers between devices  38.9 us (27%)
    ppermute x34, waiting for transfers between devices, swap(): return lax.ppermute(value, axis, [(i, i ^ bit) for i in range(size)])  55.6 us
    pallas_call x34, Pallas kernels, call(): pl.pallas_call(body, out_shape=tuple((out_space(shape, dtype) for shape,...  46.3 us
    ppermute x34, starting transfers between devices, swap(): return lax.ppermute(value, axis, [(i, i ^ bit) for i in range(size)])  38.9 us
  transfers between devices with their start and end apart: 34, of which 21 were waited for; matrix products, arithmetic and copies ran while one was open for 0% of the time, Pallas kernels for 10%

commit v1 on v0

--- a/solution.py
+++ b/solution.py
@@ -59,67 +59,54 @@
     return lax.rem(lax.axis_index("dp"), 2)
 
 
-class Store:
-    def __init__(self, rows, columns):
-        self.rows, self.columns = rows, columns
-        self.width = math.gcd(math.gcd(rows, columns // 2), 512)
-        self.groups = min(TURNED, rows // self.width)
-        self.shape = (rows * columns // self.width + self.groups * columns, self.width)
-
-    def block(self, j):
-        return pl.ds(pl.multiple_of(j * self.rows, self.width), self.rows)
-
-    def turned(self, i, first, count):
-        start = self.rows * self.columns // self.width + i * self.columns + first
-        return pl.ds(pl.multiple_of(start, LANES), count)
-
-
-def load_kernel(x_hbm, w_hbm, x_ref, w_ref, l_ref, sems, w_sem, *, store, ahead):
-    width = store.width
-    blocks = store.columns // width
-
-    def copy(j):
-        cols = pl.ds(pl.multiple_of(j * width, width), width)
-        return pltpu.make_async_copy(x_hbm.at[:, cols], x_ref.at[store.block(j)], sems.at[j])
+def half_of(which, half):
+    return pl.ds(pl.multiple_of(which * half, LANES), half)
+
+
+def load_kernel(x_hbm, w_hbm, x_ref, xt_ref, w_ref, l_ref, sems, w_sem, *, step, ahead):
+    rows, columns = x_ref.shape
+    chunks = rows // step
+    block = math.gcd(columns, 512)
+
+    def rows_of(i):
+        return pl.ds(pl.multiple_of(i * step, step), step)
+
+    def copy(i):
+        return pltpu.make_async_copy(x_hbm.at[rows_of(i)], x_ref.at[rows_of(i)], sems.at[i])
 
     w_copy = pltpu.make_async_copy(w_hbm, w_ref, w_sem)
     w_copy.start()
-    for j in range(min(ahead, blocks)):
-        copy(j).start()
-    l_ref[...] = jnp.zeros(l_ref.shape, F32)
+    for i in range(min(ahead, chunks)):
+        copy(i).start()
     w_copy.wait()
 
-    @pl.loop(0, blocks)
-    def _(j):
-        copy(j).wait()
-
-        @pl.when(j + ahead < blocks)
+    @pl.loop(0, chunks)
+    def _(i):
+        copy(i).wait()
+
+        @pl.when(i + ahead < chunks)
         def _():
-            copy(j + ahead).start()
-
-        first = pl.multiple_of(j * width, width)
-        w = w_ref[:, pl.ds(first, width)].astype(BF16)
-        for i in range(store.rows // width):
-            rows = pl.ds(pl.multiple_of(j * store.rows + i * width, width), width)
-            turned = x_ref[rows, :].T
-            if i < store.groups:
-                x_ref[store.turned(i, first, width), :] = turned
-            l_ref[:, i * width : (i + 1) * width] += lax.dot_general(
-                w, turned, NN, preferred_element_type=F32
-            )
-
-
-def column_half(c, x_ref, which, out_ref, store):
-    width = store.width
-    count = store.columns // 2 // width
-    for i in range(count):
-        block = lax.dot_general(
-            c, x_ref[store.block(which * count + i), :], NN, preferred_element_type=F32
-        )
-        out_ref[:, i * width : (i + 1) * width] = block.astype(out_ref.dtype)
-
-
-def probs_kernel(*refs, n, store):
+            copy(i + ahead).start()
+
+        total = jnp.zeros((w_ref.shape[0], step), F32)
+        for j in range(0, columns, block):
+            turned = x_ref[rows_of(i), j : j + block].T
+            xt_ref[j : j + block, rows_of(i)] = turned
+            w = w_ref[:, j : j + block].astype(BF16)
+            total += lax.dot_general(w, turned, NN, preferred_element_type=F32)
+        l_ref[:, rows_of(i)] = total
+
+
+def column_half(c, x_ref, which, out_ref):
+    half = x_ref.shape[1] // 2
+    width = math.gcd(half, 512)
+    for i in range(0, half, width):
+        cols = pl.ds(pl.multiple_of(which * half + i, width), width)
+        block = lax.dot_general(c, x_ref[:, cols], NN, preferred_element_type=F32)
+        out_ref[:, i : i + width] = block.astype(out_ref.dtype)
+
+
+def probs_kernel(*refs, n):
     parts, (labels_ref, weight_ref, x_ref, p_ref, e_ref, send_ref, block_ref) = refs[:n], refs[n:]
     logits = add_up(parts)
     classes = logits.shape[0]
@@ -138,10 +125,10 @@
     block = scalar_block(
         (sum_all(row_weight), sum_all(row_weight * (log_total - picked))), lax.axis_index("dp")
     )
-    half = store.columns // 2
+    half = x_ref.shape[1] // 2
     block_ref[...] = block
     send_ref[:, half:] = block.astype(BF16)
-    column_half(e, x_ref, 1 - my_core(), send_ref, store)
+    column_half(e, x_ref, 1 - my_core(), send_ref)
 
 
 def curvature(parts, s_prev, sc_prev, p_ref, scale_ref):
@@ -166,7 +153,7 @@
     return s, c, curv, res_norm, dir_norm, beta
 
 
-def curv_kernel(*refs, n, first, store):
+def curv_kernel(*refs, n, first):
     parts, refs = refs[:n], refs[n:]
     s_prev, sc_prev = None, None
     if not first:
@@ -180,21 +167,20 @@
     sc_ref[2:3, :] = jnp.broadcast_to(beta, (1, LANES))
     sc_ref[3:, :] = jnp.zeros((5, LANES), F32)
     block = scalar_block((curv,), lax.axis_index("dp"))
-    half = store.columns // 2
+    half = x_ref.shape[1] // 2
     block_ref[...] = block
     send_ref[:, half:] = block.astype(BF16)
-    column_half(c, x_ref, 1 - my_core(), send_ref, store)
-
-
-def own_columns_kernel(c_ref, block_ref, x_ref, out_ref, *, store):
-    half = store.columns // 2
+    column_half(c, x_ref, 1 - my_core(), send_ref)
+
+
+def own_columns_kernel(c_ref, block_ref, x_ref, out_ref):
+    half = x_ref.shape[1] // 2
     out_ref[:, half:] = block_ref[...]
-    column_half(c_ref[...], x_ref, my_core(), out_ref, store)
-
-
-def residual_out(residual, extra, r_ref, send_ref):
+    column_half(c_ref[...], x_ref, my_core(), out_ref)
+
+
+def residual_out(residual, extra, send_ref):
     half = residual.shape[1]
-    r_ref[...] = residual
     send_ref[:, :half] = residual.astype(BF16)
     send_ref[:, half:] = scalar_block((sum_all(residual * residual),) + extra, 0).astype(BF16)
 
@@ -209,63 +195,60 @@
     scale_ref[...] = one_row(weight_ref).astype(F32) / weight_total
     weight = w_ref[:, pl.ds(pl.multiple_of(my_core() * half, LANES), half)]
     residual = -(total[:, :half] / weight_total + RIDGE_COEF * weight)
-    residual_out(residual, (), r_ref, send_ref)
-
-
-def update_kernel(*refs, n, first):
+    r_ref[...] = residual
+    residual_out(residual, (), send_ref)
+
+
+def update_kernel(*refs, n, first, last):
     parts, refs = refs[:n], refs[n:]
     (r_ref, sc_ref), refs = refs[:2], refs[2:]
-    if first:
-        r_out, d_out, send_ref, alpha_ref = refs
-        direction = r_ref[...]
-    else:
-        d_ref, r_out, d_out, send_ref, alpha_ref = refs
-        direction = r_ref[...] + sc_ref[2:3, 0:1] * d_ref[...]
+    direction = r_ref[...]
+    if not first:
+        direction = direction + sc_ref[2:3, 0:1] * refs[0][...]
+        refs = refs[1:]
+    send_ref, alpha_ref = refs[:2]
     total = add_up(parts)
     half = r_ref.shape[1]
     curv = read_scalar(total[:, half:], 0) + RIDGE_COEF * sc_ref[1:2, 0:1]
     alpha = sc_ref[0:1, 0:1] / curv
     residual = r_ref[...] - alpha * (total[:, :half] + RIDGE_COEF * direction)
-    d_out[...] = direction
+    if not last:
+        r_out, d_out = refs[2:]
+        r_out[...] = residual
+        d_out[...] = direction
     alpha_ref[...] = jnp.broadcast_to(alpha, alpha_ref.shape)
-    residual_out(residual, (sum_all(residual * direction),), r_out, send_ref)
-
-
-def row_half(h, x_ref, which, store, i):
-    half, width = store.columns // 2, store.width
-    if i < store.groups:
-        return lax.dot_general(
-            h, x_ref[store.turned(i, which * half, half), :], NN, preferred_element_type=F32
-        )
-    total = jnp.zeros((h.shape[0], width), F32)
-    for j in range(half // width):
-        first = (which * (half // width) + j) * store.rows + i * width
-        block = x_ref[pl.ds(pl.multiple_of(first, width), width), :]
-        total += lax.dot_general(
-            h[:, j * width : (j + 1) * width], block, NT, preferred_element_type=F32
-        )
-    return total
-
-
-def own_rows_kernel(send_ref, x_ref, out_ref, *, store):
-    half, width = store.columns // 2, store.width
-    h = send_ref[:, :half]
-    for i in range(store.rows // width):
-        out_ref[:, i * width : (i + 1) * width] = row_half(h, x_ref, my_core(), store, i)
-
-
-def mate_rows_kernel(acc_ref, mine_ref, recv_ref, x_ref, out_ref, *, store):
-    half, width = store.columns // 2, store.width
+    residual_out(residual, (sum_all(residual * direction),), send_ref)
+
+
+def row_blocks(xt_ref):
+    rows = xt_ref.shape[1]
+    width = math.gcd(rows, 512)
+    return [slice(i, i + width) for i in range(0, rows, width)]
+
+
+def row_half(h, xt_ref, which, block):
+    half = xt_ref.shape[0] // 2
+    return lax.dot_general(
+        h, xt_ref[half_of(which, half), block], NN, preferred_element_type=F32
+    )
+
+
+def own_rows_kernel(send_ref, xt_ref, out_ref):
+    h = send_ref[:, : xt_ref.shape[0] // 2]
+    for block in row_blocks(xt_ref):
+        out_ref[:, block] = row_half(h, xt_ref, my_core(), block)
+
+
+def mate_rows_kernel(acc_ref, mine_ref, recv_ref, xt_ref, out_ref):
+    half, rows = xt_ref.shape[0] // 2, xt_ref.shape[1]
     h = recv_ref[:, :half]
-    block = mine_ref[:, half:].astype(F32) + recv_ref[:, half:].astype(F32)
-    lane = lax.axis_index("feat")
-    out_ref[:, store.rows :] = scalar_block(
-        (read_scalar(block, 0), read_scalar(block, 1)), lane
+    both = mine_ref[:, half:].astype(F32) + recv_ref[:, half:].astype(F32)
+    out_ref[:, rows:] = scalar_block(
+        (read_scalar(both, 0), read_scalar(both, 1)), lax.axis_index("feat")
     ).astype(BF16)
-    for i in range(store.rows // width):
-        cols = slice(i * width, (i + 1) * width)
-        part = acc_ref[:, cols] + row_half(h, x_ref, 1 - my_core(), store, i)
-        out_ref[:, cols] = part.astype(BF16)
+    for block in row_blocks(xt_ref):
+        part = acc_ref[:, block] + row_half(h, xt_ref, 1 - my_core(), block)
+        out_ref[:, block] = part.astype(BF16)
 
 
 def last_kernel(*refs, n):
@@ -297,9 +280,13 @@
     def body(*refs):
         kernel(*refs[: len(args)], *refs[len(args) + len(pins) :])
 
+    args = tuple(
+        pltpu.with_memory_space_constraint(a, pltpu.HBM) if i in keep else a
+        for i, a in enumerate(args)
+    )
     args_pins = args + tuple(pltpu.with_memory_space_constraint(p, pltpu.VMEM) for p in pins)
     specs = [
-        pl.BlockSpec(memory_space=pl.ANY if i in keep else pltpu.VMEM)
+        pl.BlockSpec(memory_space=pltpu.HBM if i in keep else pltpu.VMEM)
         for i in range(len(args_pins))
     ]
     return pl.pallas_call(
@@ -329,7 +316,7 @@
     if len(bits) == 1:
         return [value, swap(value, axis, size, bits[0])]
     a, b = bits
-    return [value] + [swap(value, axis, size, k) for k in (a, b, a | b)]
+    return [value] + [swap(value, axis, size, k) for k in (a, a | b, b)]
 
 
 def bits_of(size):
@@ -348,24 +335,28 @@
     def core_swap(value):
         return swap(value, "dp", dp, 1)
 
-    store = Store(rows, columns)
-    x, weight, logit_part = call(
-        functools.partial(load_kernel, store=store, ahead=4),
+    step = math.gcd(rows, 256)
+    x, xt, weight, logit_part = call(
+        functools.partial(load_kernel, step=step, ahead=2),
         "load",
-        [(store.shape, BF16), ((classes, columns), F32), ((classes, rows), F32)],
+        [
+            ((rows, columns), BF16),
+            ((columns, rows), BF16),
+            ((classes, columns), F32),
+            ((classes, rows), F32),
+        ],
         features,
         weight,
-        scratch=(pltpu.SemaphoreType.DMA((columns // store.width,)), pltpu.SemaphoreType.DMA),
+        scratch=(pltpu.SemaphoreType.DMA((rows // step,)), pltpu.SemaphoreType.DMA),
         keep=(0, 1),
-        limit=VMEM_LIMIT - weight.size * weight.dtype.itemsize,
-    )
-    x = pltpu.with_memory_space_constraint(x, pltpu.VMEM)
-    pins = [x, weight]
+        limit=VMEM_LIMIT,
+    )
+    pins = [x, xt, weight]
 
     def column_sums(c, send, block):
         received = core_swap(send)
         (own,) = call(
-            functools.partial(own_columns_kernel, store=store),
+            own_columns_kernel,
             "own_columns",
             [((classes, half + LANES), F32)],
             c,
@@ -378,21 +369,21 @@
     def row_sums(send):
         received = core_swap(send)
         (part,) = call(
-            functools.partial(own_rows_kernel, store=store),
+            own_rows_kernel,
             "own_rows",
             [((classes, rows), F32)],
             send,
-            x,
+            xt,
             pins=pins,
         )
         (score,) = call(
-            functools.partial(mate_rows_kernel, store=store),
+            mate_rows_kernel,
             "mate_rows",
             [((classes, rows + LANES), BF16)],
             part,
             send,
             received,
-            x,
+            xt,
             pins=pins,
         )
         return across_feat(score, pins)
@@ -404,7 +395,7 @@
     ]
     parts = across_feat(logit_part, pins)
     prob, e, send, block = call(
-        functools.partial(probs_kernel, n=len(parts), store=store),
+        functools.partial(probs_kernel, n=len(parts)),
         "probs",
         [((classes, rows), F32)] + curv_outs,
         *parts,
@@ -423,13 +414,13 @@
         row_weight,
         pins=pins,
     )
-    pins[1:] = [residual]
+    pins[2:] = [residual]
     state, steps, scores = (), [], []
     direction = ()
     for i in range(CG_ITERS - 1):
         parts = row_sums(send)
         s, c, send, block, sc = call(
-            functools.partial(curv_kernel, n=len(parts), first=i == 0, store=store),
+            functools.partial(curv_kernel, n=len(parts), first=i == 0),
             "curvature",
             [((classes, rows), F32)] + curv_outs + [((8, LANES), F32)],
             *parts,
@@ -442,18 +433,21 @@
         state = (s, sc)
         scores.append(s)
         parts = column_sums(c, send, block)
-        residual, new_direction, send, alpha = call(
-            functools.partial(update_kernel, n=len(parts), first=i == 0),
+        last = i == CG_ITERS - 2
+        send, alpha, *vectors = call(
+            functools.partial(update_kernel, n=len(parts), first=i == 0, last=last),
             "update",
-            [((classes, half), F32)] * 2 + [((classes, half + LANES), BF16), ((8, LANES), F32)],
+            [((classes, half + LANES), BF16), ((8, LANES), F32)]
+            + [((classes, half), F32)] * (0 if last else 2),
             *parts,
             residual,
             sc,
             *direction,
             pins=pins,
         )
-        pins[1:] = [residual, new_direction] if i < CG_ITERS - 2 else []
-        direction = (new_direction,)
+        pins[2:] = vectors
+        if not last:
+            residual, *direction = vectors
         steps.append(alpha)
     parts = row_sums(send)
     s, sc = call(

time: 143 us -> 137 us (0.958)
  Pallas kernels: 46.3 us -> 41.5 us
  starting transfers between devices: 38.9 us -> 36.1 us
  waiting for transfers between devices: 55.6 us -> 58.4 us
    pallas_call x34, Pallas kernels: 46.3 us -> 41.5 us  [call(): pl.pallas_call(body, out_shape=tuple((out_space(shape, dtype) for shape,...]
    ppermute x34, waiting for transfers between devices: 55.6 us -> 58.4 us  [swap(): return lax.ppermute(value, axis, [(i, i ^ bit) for i in range(size)])]
    ppermute x34, starting transfers between devices: 38.9 us -> 36.1 us  [swap(): return lax.ppermute(value, axis, [(i, i ^ bit) for i in range(size)])]
  transfers between devices with their start and end apart: 34 -> 34, of which waited for: 21 -> 22; matrix products, arithmetic and copies ran while one was open for 0% -> 0% of each run, Pallas kernels for 10% -> 10%
where the time goes in v1:
time: 137 us
  waiting for transfers between devices  58.4 us (43%)
  Pallas kernels  41.5 us (30%)
  starting transfers between devices  36.1 us (26%)
    ppermute x34, waiting for transfers between devices, swap(): return lax.ppermute(value, axis, [(i, i ^ bit) for i in range(size)])  58.4 us
    pallas_call x34, Pallas kernels, call(): pl.pallas_call(body, out_shape=tuple((out_space(shape, dtype) for shape,...  41.5 us
    ppermute x34, starting transfers between devices, swap(): return lax.ppermute(value, axis, [(i, i ^ bit) for i in range(size)])  36.1 us
  transfers between devices with their start and end apart: 34, of which 22 were waited for; matrix products, arithmetic and copies ran while one was open for 0% of the time, Pallas kernels for 10%

profile of v1, /device:TPU:0, one launch (start us, length us, event | category | flops | bytes accessed | tf_op | source)
XLA Modules:
  0.0 137.0 jit_solution(12348904527143093098)
XLA Ops:
  0.6 10.2 %load.1 = (bf16[1536,8192]{1,0:T(8,128)(2,1)S(1)}, bf16[8192,1536]{1,0:T(8,128)(2,1)S(1)}, f32[16,8192]{1,0:T(8,128)S(1)}, f32[16,1536]{1,0:T(8,128)S(1)}) custom-call(bf16[1536,8192]{1,0:T(8,128)(2,1)} %refs_0_.1, f32[16,8192]{1,0:T(8,128)} %refs_1_.1), custom_call_target="tpu_custom_call" | custom-call | tf_op jit(solution)/shard_map/load/pallas_call | solution.py:292
  10.8 3.0 %collective-permute-start = (f32[16,1536]{1,0:T(8,128)S(1)}, f32[16,1536]{1,0:T(8,128)S(1)}, u32[]{:S(2)}, u32[]{:S(2)}) collective-permute-start(f32[16,1536]{1,0:T(8,128)S(1)} %get-tuple-element.43.refs_0_), channel_id=1, source_target_pairs={{0,1},{1,0},{2,3},{3,2},{4,5},{5,4},{6,7},{7,6},{8,9},{9,8},{10,11... | collective-permute-start | bytes 294920 | tf_op jit(solution)/shard_map/ppermute | solution.py:308
  13.8 2.8 %collective-permute-done.refs_1_ = f32[16,1536]{1,0:T(8,128)S(1)} collective-permute-done((f32[16,1536]{1,0:T(8,128)S(1)}, f32[16,1536]{1,0:T(8,128)S(1)}, u32[]{:S(2)}, u32[]{:S(2)}) %collective-permute-start) | collective-permute-done | bytes 98336 | tf_op jit(solution)/shard_map/ppermute | solution.py:308
  16.7 3.0 %collective-permute-start.3 = (f32[16,1536]{1,0:T(8,128)S(1)}, f32[16,1536]{1,0:T(8,128)S(1)}, u32[]{:S(2)}, u32[]{:S(2)}) collective-permute-start(f32[16,1536]{1,0:T(8,128)S(1)} %add.11.refs_0_), channel_id=1, source_target_pairs={{0,4},{1,5},{2,6},{3,7},{4,0},{5,1},{6,2},{7,3},{8,12},{9,13},{10,... | collective-permute-start | bytes 294920 | tf_op jit(solution)/shard_map/ppermute | solution.py:308
  21.2 5.5 %collective-permute-done.3.refs_3_ = f32[16,1536]{1,0:T(8,128)S(1)} collective-permute-done((f32[16,1536]{1,0:T(8,128)S(1)}, f32[16,1536]{1,0:T(8,128)S(1)}, u32[]{:S(2)}, u32[]{:S(2)}) %collective-permute-start.3) | collective-permute-done | bytes 98336 | tf_op jit(solution)/shard_map/ppermute | solution.py:308
  27.1 1.8 %probs.1 = (f32[16,1536]{1,0:T(8,128)S(1)}, bf16[16,1536]{1,0:T(8,128)(2,1)S(1)}, bf16[16,4224]{1,0:T(8,128)(2,1)S(1)}, f32[16,128]{1,0:T(8,128)S(1)}) custom-call(f32[16,1536]{1,0:T(8,128)S(1)} %add.11.refs_0_, f32[16,1536]{1,0:T(8,128)S(1)} %collective-permute-done.1.refs_1_, f32[16,1536]{1,0:T(8,128)S(1)} %collective-permute-done.2.refs_2_, ...), custom_call_target="tpu_custom_call" | custom-call | tf_op jit(solution)/shard_map/probs/pallas_call | solution.py:292
  32.3 4.5 %collective-permute-done.5.refs_1_ = bf16[16,4224]{1,0:T(8,128)(2,1)S(1)} collective-permute-done((bf16[16,4224]{1,0:T(8,128)(2,1)S(1)}, bf16[16,4224]{1,0:T(8,128)(2,1)S(1)}, u32[]{:S(2)}, u32[]{:S(2)}) %collective-permute-start.5) | collective-permute-done | bytes 135200 | tf_op jit(solution)/shard_map/ppermute | solution.py:308
  42.3 2.7 %collective-permute-done.7.refs_1_ = bf16[16,1664]{1,0:T(8,128)(2,1)S(1)} collective-permute-done((bf16[16,1664]{1,0:T(8,128)(2,1)S(1)}, bf16[16,1664]{1,0:T(8,128)(2,1)S(1)}, u32[]{:S(2)}, u32[]{:S(2)}) %collective-permute-start.7) | collective-permute-done | bytes 53280 | tf_op jit(solution)/shard_map/ppermute | solution.py:308
  45.0 3.1 %collective-permute-start.10 = (bf16[16,1664]{1,0:T(8,128)(2,1)S(1)}, bf16[16,1664]{1,0:T(8,128)(2,1)S(1)}, u32[]{:S(2)}, u32[]{:S(2)}) collective-permute-start(bf16[16,1664]{1,0:T(8,128)(2,1)S(1)} %add.13.refs_0_), channel_id=1, source_target_pairs={{0,4},{1,5},{2,6},{3,7},{4,0},{5,1},{6,2},{7,3},{8,12},{9,13},{10,... | collective-permute-start | bytes 159752 | tf_op jit(solution)/shard_map/ppermute | solution.py:308
  48.8 2.6 %collective-permute-done.10.refs_3_ = bf16[16,1664]{1,0:T(8,128)(2,1)S(1)} collective-permute-done((bf16[16,1664]{1,0:T(8,128)(2,1)S(1)}, bf16[16,1664]{1,0:T(8,128)(2,1)S(1)}, u32[]{:S(2)}, u32[]{:S(2)}) %collective-permute-start.10) | collective-permute-done | bytes 53280 | tf_op jit(solution)/shard_map/ppermute | solution.py:308
  51.4 2.7 %collective-permute-done.9.refs_2_ = bf16[16,1664]{1,0:T(8,128)(2,1)S(1)} collective-permute-done((bf16[16,1664]{1,0:T(8,128)(2,1)S(1)}, bf16[16,1664]{1,0:T(8,128)(2,1)S(1)}, u32[]{:S(2)}, u32[]{:S(2)}) %collective-permute-start.9) | collective-permute-done | bytes 53280 | tf_op jit(solution)/shard_map/ppermute | solution.py:308
  54.1 1.8 %curvature.3 = (f32[16,1536]{1,0:T(8,128)S(1)}, bf16[16,1536]{1,0:T(8,128)(2,1)S(1)}, bf16[16,4224]{1,0:T(8,128)(2,1)S(1)}, f32[16,128]{1,0:T(8,128)S(1)}, f32[8,128]{1,0:T(8,128)S(1)}) custom-call(bf16[16,1664]{1,0:T(8,128)(2,1)S(1)} %add.13.refs_0_, bf16[16,1664]{1,0:T(8,128)(2,1)S(1)} %collective-permute-done.8.refs_1_, ...), custom_call_target="tpu_custom_call" | custom-call | tf_op jit(solution)/shard_map/curvature/pallas_call | solution.py:292
  59.2 4.5 %collective-permute-done.12.refs_1_ = bf16[16,4224]{1,0:T(8,128)(2,1)S(1)} collective-permute-done((bf16[16,4224]{1,0:T(8,128)(2,1)S(1)}, bf16[16,4224]{1,0:T(8,128)(2,1)S(1)}, u32[]{:S(2)}, u32[]{:S(2)}) %collective-permute-start.12) | collective-permute-done | bytes 135200 | tf_op jit(solution)/shard_map/ppermute | solution.py:308
  69.2 2.7 %collective-permute-done.14.refs_1_ = bf16[16,1664]{1,0:T(8,128)(2,1)S(1)} collective-permute-done((bf16[16,1664]{1,0:T(8,128)(2,1)S(1)}, bf16[16,1664]{1,0:T(8,128)(2,1)S(1)}, u32[]{:S(2)}, u32[]{:S(2)}) %collective-permute-start.14) | collective-permute-done | bytes 53280 | tf_op jit(solution)/shard_map/ppermute | solution.py:308
  75.5 2.7 %collective-permute-done.17.refs_3_ = bf16[16,1664]{1,0:T(8,128)(2,1)S(1)} collective-permute-done((bf16[16,1664]{1,0:T(8,128)(2,1)S(1)}, bf16[16,1664]{1,0:T(8,128)(2,1)S(1)}, u32[]{:S(2)}, u32[]{:S(2)}) %collective-permute-start.17) | collective-permute-done | bytes 53280 | tf_op jit(solution)/shard_map/ppermute | solution.py:308
  79.2 1.9 %curvature.4 = (f32[16,1536]{1,0:T(8,128)S(1)}, bf16[16,1536]{1,0:T(8,128)(2,1)S(1)}, bf16[16,4224]{1,0:T(8,128)(2,1)S(1)}, f32[16,128]{1,0:T(8,128)S(1)}, f32[8,128]{1,0:T(8,128)S(1)}) custom-call(bf16[16,1664]{1,0:T(8,128)(2,1)S(1)} %add.15.refs_0_, bf16[16,1664]{1,0:T(8,128)(2,1)S(1)} %collective-permute-done.15.refs_1_, ...), custom_call_target="tpu_custom_call" | custom-call | tf_op jit(solution)/shard_map/curvature/pallas_call | solution.py:292
  84.5 4.5 %collective-permute-done.19.refs_1_ = bf16[16,4224]{1,0:T(8,128)(2,1)S(1)} collective-permute-done((bf16[16,4224]{1,0:T(8,128)(2,1)S(1)}, bf16[16,4224]{1,0:T(8,128)(2,1)S(1)}, u32[]{:S(2)}, u32[]{:S(2)}) %collective-permute-start.19) | collective-permute-done | bytes 135200 | tf_op jit(solution)/shard_map/ppermute | solution.py:308
  94.5 2.7 %collective-permute-done.21.refs_1_ = bf16[16,1664]{1,0:T(8,128)(2,1)S(1)} collective-permute-done((bf16[16,1664]{1,0:T(8,128)(2,1)S(1)}, bf16[16,1664]{1,0:T(8,128)(2,1)S(1)}, u32[]{:S(2)}, u32[]{:S(2)}) %collective-permute-start.21) | collective-permute-done | bytes 53280 | tf_op jit(solution)/shard_map/ppermute | solution.py:308
  100.8 3.1 %collective-permute-done.24.refs_3_ = bf16[16,1664]{1,0:T(8,128)(2,1)S(1)} collective-permute-done((bf16[16,1664]{1,0:T(8,128)(2,1)S(1)}, bf16[16,1664]{1,0:T(8,128)(2,1)S(1)}, u32[]{:S(2)}, u32[]{:S(2)}) %collective-permute-start.24) | collective-permute-done | bytes 53280 | tf_op jit(solution)/shard_map/ppermute | solution.py:308
  105.0 1.9 %curvature.5 = (f32[16,1536]{1,0:T(8,128)S(1)}, bf16[16,1536]{1,0:T(8,128)(2,1)S(1)}, bf16[16,4224]{1,0:T(8,128)(2,1)S(1)}, f32[16,128]{1,0:T(8,128)S(1)}, f32[8,128]{1,0:T(8,128)S(1)}) custom-call(bf16[16,1664]{1,0:T(8,128)(2,1)S(1)} %add.17.refs_0_, bf16[16,1664]{1,0:T(8,128)(2,1)S(1)} %collective-permute-done.22.refs_1_, ...), custom_call_target="tpu_custom_call" | custom-call | tf_op jit(solution)/shard_map/curvature/pallas_call | solution.py:292
  110.3 4.5 %collective-permute-done.26.refs_1_ = bf16[16,4224]{1,0:T(8,128)(2,1)S(1)} collective-permute-done((bf16[16,4224]{1,0:T(8,128)(2,1)S(1)}, bf16[16,4224]{1,0:T(8,128)(2,1)S(1)}, u32[]{:S(2)}, u32[]{:S(2)}) %collective-permute-start.26) | collective-permute-done | bytes 135200 | tf_op jit(solution)/shard_map/ppermute | solution.py:308
  120.4 2.7 %collective-permute-done.28.refs_1_ = bf16[16,1664]{1,0:T(8,128)(2,1)S(1)} collective-permute-done((bf16[16,1664]{1,0:T(8,128)(2,1)S(1)}, bf16[16,1664]{1,0:T(8,128)(2,1)S(1)}, u32[]{:S(2)}, u32[]{:S(2)}) %collective-permute-start.28) | collective-permute-done | bytes 53280 | tf_op jit(solution)/shard_map/ppermute | solution.py:308
  126.6 3.1 %collective-permute-done.31.refs_3_ = bf16[16,1664]{1,0:T(8,128)(2,1)S(1)} collective-permute-done((bf16[16,1664]{1,0:T(8,128)(2,1)S(1)}, bf16[16,1664]{1,0:T(8,128)(2,1)S(1)}, u32[]{:S(2)}, u32[]{:S(2)}) %collective-permute-start.31) | collective-permute-done | bytes 53280 | tf_op jit(solution)/shard_map/ppermute | solution.py:308
  134.0 2.1 %collective-permute-done.33.refs_1_ = f32[8,128]{1,0:T(8,128)S(1)} collective-permute-done((f32[8,128]{1,0:T(8,128)S(1)}, f32[8,128]{1,0:T(8,128)S(1)}, u32[]{:S(2)}, u32[]{:S(2)}) %collective-permute-start.33) | collective-permute-done | bytes 4128 | tf_op jit(solution)/shard_map/ppermute | solution.py:308
  (86 shorter events, 55.9 us)
Async XLA Ops:
  10.8 5.8 %collective-permute-start = (f32[16,1536]{1,0:T(8,128)S(1)}, f32[16,1536]{1,0:T(8,128)S(1)}, u32[]{:S(2)}, u32[]{:S(2)}) collective-permute-start(f32[16,1536]{1,0:T(8,128)S(1)} %get-tuple-element.43.refs_0_), channel_id=1, source_target_pairs={{0,1},{1,0},{2,3},{3,2},{4,5},{5,4},{6,7},{7,6},{8,9},{9,8},{10,11... | collective-permute-start | bytes 294920 | tf_op jit(solution)/shard_map/ppermute | solution.py:308
  16.7 10.1 %collective-permute-start.3 = (f32[16,1536]{1,0:T(8,128)S(1)}, f32[16,1536]{1,0:T(8,128)S(1)}, u32[]{:S(2)}, u32[]{:S(2)}) collective-permute-start(f32[16,1536]{1,0:T(8,128)S(1)} %add.11.refs_0_), channel_id=1, source_target_pairs={{0,4},{1,5},{2,6},{3,7},{4,0},{5,1},{6,2},{7,3},{8,12},{9,13},{10,... | collective-permute-start | bytes 294920 | tf_op jit(solution)/shard_map/ppermute | solution.py:308
  19.6 7.1 %collective-permute-start.2 = (f32[16,1536]{1,0:T(8,128)S(1)}, f32[16,1536]{1,0:T(8,128)S(1)}, u32[]{:S(2)}, u32[]{:S(2)}) collective-permute-start(f32[16,1536]{1,0:T(8,128)S(1)} %add.11.refs_0_), channel_id=1, source_target_pairs={{0,6},{1,7},{2,4},{3,5},{4,2},{5,3},{6,0},{7,1},{8,14},{9,15},{10,... | collective-permute-start | bytes 294920 | tf_op jit(solution)/shard_map/ppermute | solution.py:308
  21.0 6.2 %collective-permute-start.1 = (f32[16,1536]{1,0:T(8,128)S(1)}, f32[16,1536]{1,0:T(8,128)S(1)}, u32[]{:S(2)}, u32[]{:S(2)}) collective-permute-start(f32[16,1536]{1,0:T(8,128)S(1)} %add.11.refs_0_), channel_id=1, source_target_pairs={{0,2},{1,3},{2,0},{3,1},{4,6},{5,7},{6,4},{7,5},{8,10},{9,11},{10,... | collective-permute-start | bytes 294920 | tf_op jit(solution)/shard_map/ppermute | solution.py:308
  30.8 6.0 %collective-permute-start.5 = (bf16[16,4224]{1,0:T(8,128)(2,1)S(1)}, bf16[16,4224]{1,0:T(8,128)(2,1)S(1)}, u32[]{:S(2)}, u32[]{:S(2)}) collective-permute-start(bf16[16,4224]{1,0:T(8,128)(2,1)S(1)} %add.12.refs_0_), channel_id=1, source_target_pairs={{0,16},{8,24},{16,0},{24,8},{1,17},{9,25},{17,1},{25,9},{2,18},{10... | collective-permute-start | bytes 405512 | tf_op jit(solution)/shard_map/ppermute | solution.py:308
  40.8 4.2 %collective-permute-start.7 = (bf16[16,1664]{1,0:T(8,128)(2,1)S(1)}, bf16[16,1664]{1,0:T(8,128)(2,1)S(1)}, u32[]{:S(2)}, u32[]{:S(2)}) collective-permute-start(bf16[16,1664]{1,0:T(8,128)(2,1)S(1)} %mate_rows.4.refs_0_), channel_id=1, source_target_pairs={{0,1},{1,0},{2,3},{3,2},{4,5},{5,4},{6,7},{7,6},{8,9},{9,8},{10,11... | collective-permute-start | bytes 159752 | tf_op jit(solution)/shard_map/ppermute | solution.py:308
  45.0 6.4 %collective-permute-start.10 = (bf16[16,1664]{1,0:T(8,128)(2,1)S(1)}, bf16[16,1664]{1,0:T(8,128)(2,1)S(1)}, u32[]{:S(2)}, u32[]{:S(2)}) collective-permute-start(bf16[16,1664]{1,0:T(8,128)(2,1)S(1)} %add.13.refs_0_), channel_id=1, source_target_pairs={{0,4},{1,5},{2,6},{3,7},{4,0},{5,1},{6,2},{7,3},{8,12},{9,13},{10,... | collective-permute-start | bytes 159752 | tf_op jit(solution)/shard_map/ppermute | solution.py:308
  48.2 5.9 %collective-permute-start.9 = (bf16[16,1664]{1,0:T(8,128)(2,1)S(1)}, bf16[16,1664]{1,0:T(8,128)(2,1)S(1)}, u32[]{:S(2)}, u32[]{:S(2)}) collective-permute-start(bf16[16,1664]{1,0:T(8,128)(2,1)S(1)} %add.13.refs_0_), channel_id=1, source_target_pairs={{0,6},{1,7},{2,4},{3,5},{4,2},{5,3},{6,0},{7,1},{8,14},{9,15},{10,... | collective-permute-start | bytes 159752 | tf_op jit(solution)/shard_map/ppermute | solution.py:308
  48.8 5.3 %collective-permute-start.8 = (bf16[16,1664]{1,0:T(8,128)(2,1)S(1)}, bf16[16,1664]{1,0:T(8,128)(2,1)S(1)}, u32[]{:S(2)}, u32[]{:S(2)}) collective-permute-start(bf16[16,1664]{1,0:T(8,128)(2,1)S(1)} %add.13.refs_0_), channel_id=1, source_target_pairs={{0,2},{1,3},{2,0},{3,1},{4,6},{5,7},{6,4},{7,5},{8,10},{9,11},{10,... | collective-permute-start | bytes 159752 | tf_op jit(solution)/shard_map/ppermute | solution.py:308
  57.7 6.0 %collective-permute-start.12 = (bf16[16,4224]{1,0:T(8,128)(2,1)S(1)}, bf16[16,4224]{1,0:T(8,128)(2,1)S(1)}, u32[]{:S(2)}, u32[]{:S(2)}) collective-permute-start(bf16[16,4224]{1,0:T(8,128)(2,1)S(1)} %add.14.refs_0_), channel_id=1, source_target_pairs={{0,16},{8,24},{16,0},{24,8},{1,17},{9,25},{17,1},{25,9},{2,18},{10... | collective-permute-start | bytes 405512 | tf_op jit(solution)/shard_map/ppermute | solution.py:308
  67.7 4.2 %collective-permute-start.14 = (bf16[16,1664]{1,0:T(8,128)(2,1)S(1)}, bf16[16,1664]{1,0:T(8,128)(2,1)S(1)}, u32[]{:S(2)}, u32[]{:S(2)}) collective-permute-start(bf16[16,1664]{1,0:T(8,128)(2,1)S(1)} %mate_rows.5.refs_0_), channel_id=1, source_target_pairs={{0,1},{1,0},{2,3},{3,2},{4,5},{5,4},{6,7},{7,6},{8,9},{9,8},{10,11... | collective-permute-start | bytes 159752 | tf_op jit(solution)/shard_map/ppermute | solution.py:308
  72.0 6.2 %collective-permute-start.17 = (bf16[16,1664]{1,0:T(8,128)(2,1)S(1)}, bf16[16,1664]{1,0:T(8,128)(2,1)S(1)}, u32[]{:S(2)}, u32[]{:S(2)}) collective-permute-start(bf16[16,1664]{1,0:T(8,128)(2,1)S(1)} %add.15.refs_0_), channel_id=1, source_target_pairs={{0,4},{1,5},{2,6},{3,7},{4,0},{5,1},{6,2},{7,3},{8,12},{9,13},{10,... | collective-permute-start | bytes 159752 | tf_op jit(solution)/shard_map/ppermute | solution.py:308
  73.2 6.0 %collective-permute-start.16 = (bf16[16,1664]{1,0:T(8,128)(2,1)S(1)}, bf16[16,1664]{1,0:T(8,128)(2,1)S(1)}, u32[]{:S(2)}, u32[]{:S(2)}) collective-permute-start(bf16[16,1664]{1,0:T(8,128)(2,1)S(1)} %add.15.refs_0_), channel_id=1, source_target_pairs={{0,6},{1,7},{2,4},{3,5},{4,2},{5,3},{6,0},{7,1},{8,14},{9,15},{10,... | collective-permute-start | bytes 159752 | tf_op jit(solution)/shard_map/ppermute | solution.py:308
  74.2 5.0 %collective-permute-start.15 = (bf16[16,1664]{1,0:T(8,128)(2,1)S(1)}, bf16[16,1664]{1,0:T(8,128)(2,1)S(1)}, u32[]{:S(2)}, u32[]{:S(2)}) collective-permute-start(bf16[16,1664]{1,0:T(8,128)(2,1)S(1)} %add.15.refs_0_), channel_id=1, source_target_pairs={{0,2},{1,3},{2,0},{3,1},{4,6},{5,7},{6,4},{7,5},{8,10},{9,11},{10,... | collective-permute-start | bytes 159752 | tf_op jit(solution)/shard_map/ppermute | solution.py:308
  82.9 6.1 %collective-permute-start.19 = (bf16[16,4224]{1,0:T(8,128)(2,1)S(1)}, bf16[16,4224]{1,0:T(8,128)(2,1)S(1)}, u32[]{:S(2)}, u32[]{:S(2)}) collective-permute-start(bf16[16,4224]{1,0:T(8,128)(2,1)S(1)} %add.16.refs_0_), channel_id=1, source_target_pairs={{0,16},{8,24},{16,0},{24,8},{1,17},{9,25},{17,1},{25,9},{2,18},{10... | collective-permute-start | bytes 405512 | tf_op jit(solution)/shard_map/ppermute | solution.py:308
  93.0 4.2 %collective-permute-start.21 = (bf16[16,1664]{1,0:T(8,128)(2,1)S(1)}, bf16[16,1664]{1,0:T(8,128)(2,1)S(1)}, u32[]{:S(2)}, u32[]{:S(2)}) collective-permute-start(bf16[16,1664]{1,0:T(8,128)(2,1)S(1)} %mate_rows.6.refs_0_), channel_id=1, source_target_pairs={{0,1},{1,0},{2,3},{3,2},{4,5},{5,4},{6,7},{7,6},{8,9},{9,8},{10,11... | collective-permute-start | bytes 159752 | tf_op jit(solution)/shard_map/ppermute | solution.py:308
  97.2 6.7 %collective-permute-start.24 = (bf16[16,1664]{1,0:T(8,128)(2,1)S(1)}, bf16[16,1664]{1,0:T(8,128)(2,1)S(1)}, u32[]{:S(2)}, u32[]{:S(2)}) collective-permute-start(bf16[16,1664]{1,0:T(8,128)(2,1)S(1)} %add.17.refs_0_), channel_id=1, source_target_pairs={{0,4},{1,5},{2,6},{3,7},{4,0},{5,1},{6,2},{7,3},{8,12},{9,13},{10,... | collective-permute-start | bytes 159752 | tf_op jit(solution)/shard_map/ppermute | solution.py:308
  99.0 6.0 %collective-permute-start.23 = (bf16[16,1664]{1,0:T(8,128)(2,1)S(1)}, bf16[16,1664]{1,0:T(8,128)(2,1)S(1)}, u32[]{:S(2)}, u32[]{:S(2)}) collective-permute-start(bf16[16,1664]{1,0:T(8,128)(2,1)S(1)} %add.17.refs_0_), channel_id=1, source_target_pairs={{0,6},{1,7},{2,4},{3,5},{4,2},{5,3},{6,0},{7,1},{8,14},{9,15},{10,... | collective-permute-start | bytes 159752 | tf_op jit(solution)/shard_map/ppermute | solution.py:308
  100.2 4.8 %collective-permute-start.22 = (bf16[16,1664]{1,0:T(8,128)(2,1)S(1)}, bf16[16,1664]{1,0:T(8,128)(2,1)S(1)}, u32[]{:S(2)}, u32[]{:S(2)}) collective-permute-start(bf16[16,1664]{1,0:T(8,128)(2,1)S(1)} %add.17.refs_0_), channel_id=1, source_target_pairs={{0,2},{1,3},{2,0},{3,1},{4,6},{5,7},{6,4},{7,5},{8,10},{9,11},{10,... | collective-permute-start | bytes 159752 | tf_op jit(solution)/shard_map/ppermute | solution.py:308
  108.7 6.1 %collective-permute-start.26 = (bf16[16,4224]{1,0:T(8,128)(2,1)S(1)}, bf16[16,4224]{1,0:T(8,128)(2,1)S(1)}, u32[]{:S(2)}, u32[]{:S(2)}) collective-permute-start(bf16[16,4224]{1,0:T(8,128)(2,1)S(1)} %add.18.refs_0_), channel_id=1, source_target_pairs={{0,16},{8,24},{16,0},{24,8},{1,17},{9,25},{17,1},{25,9},{2,18},{10... | collective-permute-start | bytes 405512 | tf_op jit(solution)/shard_map/ppermute | solution.py:308
  118.8 4.2 %collective-permute-start.28 = (bf16[16,1664]{1,0:T(8,128)(2,1)S(1)}, bf16[16,1664]{1,0:T(8,128)(2,1)S(1)}, u32[]{:S(2)}, u32[]{:S(2)}) collective-permute-start(bf16[16,1664]{1,0:T(8,128)(2,1)S(1)} %mate_rows.7.refs_0_), channel_id=1, source_target_pairs={{0,1},{1,0},{2,3},{3,2},{4,5},{5,4},{6,7},{7,6},{8,9},{9,8},{10,11... | collective-permute-start | bytes 159752 | tf_op jit(solution)/shard_map/ppermute | solution.py:308
  123.1 6.7 %collective-permute-start.31 = (bf16[16,1664]{1,0:T(8,128)(2,1)S(1)}, bf16[16,1664]{1,0:T(8,128)(2,1)S(1)}, u32[]{:S(2)}, u32[]{:S(2)}) collective-permute-start(bf16[16,1664]{1,0:T(8,128)(2,1)S(1)} %add.19.refs_0_), channel_id=1, source_target_pairs={{0,4},{1,5},{2,6},{3,7},{4,0},{5,1},{6,2},{7,3},{8,12},{9,13},{10,... | collective-permute-start | bytes 159752 | tf_op jit(solution)/shard_map/ppermute | solution.py:308
  124.4 6.1 %collective-permute-start.30 = (bf16[16,1664]{1,0:T(8,128)(2,1)S(1)}, bf16[16,1664]{1,0:T(8,128)(2,1)S(1)}, u32[]{:S(2)}, u32[]{:S(2)}) collective-permute-start(bf16[16,1664]{1,0:T(8,128)(2,1)S(1)} %add.19.refs_0_), channel_id=1, source_target_pairs={{0,6},{1,7},{2,4},{3,5},{4,2},{5,3},{6,0},{7,1},{8,14},{9,15},{10,... | collective-permute-start | bytes 159752 | tf_op jit(solution)/shard_map/ppermute | solution.py:308
  126.1 4.8 %collective-permute-start.29 = (bf16[16,1664]{1,0:T(8,128)(2,1)S(1)}, bf16[16,1664]{1,0:T(8,128)(2,1)S(1)}, u32[]{:S(2)}, u32[]{:S(2)}) collective-permute-start(bf16[16,1664]{1,0:T(8,128)(2,1)S(1)} %add.19.refs_0_), channel_id=1, source_target_pairs={{0,2},{1,3},{2,0},{3,1},{4,6},{5,7},{6,4},{7,5},{8,10},{9,11},{10,... | collective-permute-start | bytes 159752 | tf_op jit(solution)/shard_map/ppermute | solution.py:308
  (14 other events, 67.2 us)

commit v2 on v1

--- a/solution.py
+++ b/solution.py
@@ -59,10 +59,6 @@
     return lax.rem(lax.axis_index("dp"), 2)
 
 
-def half_of(which, half):
-    return pl.ds(pl.multiple_of(which * half, LANES), half)
-
-
 def load_kernel(x_hbm, w_hbm, x_ref, xt_ref, w_ref, l_ref, sems, w_sem, *, step, ahead):
     rows, columns = x_ref.shape
     chunks = rows // step
@@ -97,17 +93,25 @@
         l_ref[:, rows_of(i)] = total
 
 
-def column_half(c, x_ref, which, out_ref):
-    half = x_ref.shape[1] // 2
-    width = math.gcd(half, 512)
-    for i in range(0, half, width):
-        cols = pl.ds(pl.multiple_of(which * half + i, width), width)
+def column_part(c, x_ref, which, part, out_ref):
+    size = x_ref.shape[1] // 4
+    width = math.gcd(size, 512)
+    for i in range(0, size, width):
+        cols = pl.ds(pl.multiple_of((2 * which + part) * size + i, LANES), width)
         block = lax.dot_general(c, x_ref[:, cols], NN, preferred_element_type=F32)
         out_ref[:, i : i + width] = block.astype(out_ref.dtype)
 
 
+def send_columns(c, x_ref, block, send0_ref, send1_ref):
+    size = x_ref.shape[1] // 4
+    send0_ref[:, size:] = block.astype(BF16)
+    column_part(c, x_ref, 1 - my_core(), 0, send0_ref)
+    column_part(c, x_ref, 1 - my_core(), 1, send1_ref)
+
+
 def probs_kernel(*refs, n):
-    parts, (labels_ref, weight_ref, x_ref, p_ref, e_ref, send_ref, block_ref) = refs[:n], refs[n:]
+    parts, refs = refs[:n], refs[n:]
+    labels_ref, weight_ref, x_ref, p_ref, e_ref, send0_ref, send1_ref, block_ref = refs
     logits = add_up(parts)
     classes = logits.shape[0]
     top = jnp.max(logits, axis=0, keepdims=True)
@@ -125,10 +129,8 @@
     block = scalar_block(
         (sum_all(row_weight), sum_all(row_weight * (log_total - picked))), lax.axis_index("dp")
     )
-    half = x_ref.shape[1] // 2
     block_ref[...] = block
-    send_ref[:, half:] = block.astype(BF16)
-    column_half(e, x_ref, 1 - my_core(), send_ref)
+    send_columns(e, x_ref, block, send0_ref, send1_ref)
 
 
 def curvature(parts, s_prev, sc_prev, p_ref, scale_ref):
@@ -158,7 +160,7 @@
     s_prev, sc_prev = None, None
     if not first:
         (s_prev, sc_prev), refs = refs[:2], refs[2:]
-    p_ref, scale_ref, x_ref, s_ref, c_ref, send_ref, block_ref, sc_ref = refs
+    p_ref, scale_ref, x_ref, s_ref, c_ref, send0_ref, send1_ref, block_ref, sc_ref = refs
     s, c, curv, res_norm, dir_norm, beta = curvature(parts, s_prev, sc_prev, p_ref, scale_ref)
     s_ref[...] = s
     c_ref[...] = c
@@ -167,57 +169,85 @@
     sc_ref[2:3, :] = jnp.broadcast_to(beta, (1, LANES))
     sc_ref[3:, :] = jnp.zeros((5, LANES), F32)
     block = scalar_block((curv,), lax.axis_index("dp"))
-    half = x_ref.shape[1] // 2
     block_ref[...] = block
-    send_ref[:, half:] = block.astype(BF16)
-    column_half(c, x_ref, 1 - my_core(), send_ref)
-
-
-def own_columns_kernel(c_ref, block_ref, x_ref, out_ref):
-    half = x_ref.shape[1] // 2
-    out_ref[:, half:] = block_ref[...]
-    column_half(c_ref[...], x_ref, my_core(), out_ref)
-
-
-def residual_out(residual, extra, send_ref):
-    half = residual.shape[1]
-    send_ref[:, :half] = residual.astype(BF16)
-    send_ref[:, half:] = scalar_block((sum_all(residual * residual),) + extra, 0).astype(BF16)
-
-
-def gradient_kernel(*refs, n):
-    parts, (w_ref, weight_ref, r_ref, send_ref, scale_ref, loss_ref) = refs[:n], refs[n:]
+    send_columns(c, x_ref, block, send0_ref, send1_ref)
+
+
+def own_columns_kernel(*refs, part):
+    c_ref, x_ref, out_ref = refs[0], refs[-2], refs[-1]
+    if part == 0:
+        out_ref[:, x_ref.shape[1] // 4 :] = refs[1][...]
+    column_part(c_ref[...], x_ref, my_core(), part, out_ref)
+
+
+def residual_out(residual, sums, aux_ref, send_ref):
+    size = residual.shape[1]
+    send_ref[:, :size] = residual.astype(BF16)
+    if aux_ref is not None:
+        for i, value in enumerate(sums):
+            aux_ref[i : i + 1, :] = jnp.broadcast_to(value, (1, LANES))
+    else:
+        send_ref[:, size:] = scalar_block(sums, 0).astype(BF16)
+
+
+def own_weight(w_ref, part, size):
+    return w_ref[:, pl.ds(pl.multiple_of((2 * my_core() + part) * size, LANES), size)]
+
+
+def gradient0_kernel(*refs, n):
+    parts, (w_ref, weight_ref, r_ref, send_ref, aux_ref, scale_ref, loss_ref) = refs[:n], refs[n:]
     total = add_up(parts)
-    half = r_ref.shape[1]
-    block = total[:, half:]
+    size = r_ref.shape[1]
+    block = total[:, size:]
     weight_total = read_scalar(block, 0)
     loss_ref[...] = jnp.broadcast_to(read_scalar(block, 1) / weight_total, loss_ref.shape)
     scale_ref[...] = one_row(weight_ref).astype(F32) / weight_total
-    weight = w_ref[:, pl.ds(pl.multiple_of(my_core() * half, LANES), half)]
-    residual = -(total[:, :half] / weight_total + RIDGE_COEF * weight)
+    residual = -(total[:, :size] / weight_total + RIDGE_COEF * own_weight(w_ref, 0, size))
     r_ref[...] = residual
-    residual_out(residual, (), send_ref)
-
-
-def update_kernel(*refs, n, first, last):
+    aux_ref[...] = jnp.zeros(aux_ref.shape, F32)
+    residual_out(residual, (sum_all(residual * residual), weight_total), aux_ref, send_ref)
+
+
+def gradient1_kernel(*refs, n):
+    parts, (w_ref, aux_ref, r_ref, send_ref) = refs[:n], refs[n:]
+    total = add_up(parts)
+    size = r_ref.shape[1]
+    residual = -(total / aux_ref[1:2, 0:1] + RIDGE_COEF * own_weight(w_ref, 1, size))
+    r_ref[...] = residual
+    residual_out(residual, (aux_ref[0:1, 0:1] + sum_all(residual * residual),), None, send_ref)
+
+
+def update_kernel(*refs, n, part, first, last):
     parts, refs = refs[:n], refs[n:]
-    (r_ref, sc_ref), refs = refs[:2], refs[2:]
+    (r_ref, sc_ref, aux_ref), refs = refs[:3], refs[3:]
     direction = r_ref[...]
     if not first:
         direction = direction + sc_ref[2:3, 0:1] * refs[0][...]
         refs = refs[1:]
-    send_ref, alpha_ref = refs[:2]
+    if part == 0:
+        send_ref, out_ref = refs[:2]
+        refs = refs[2:]
+    else:
+        send_ref, refs = refs[0], refs[1:]
     total = add_up(parts)
-    half = r_ref.shape[1]
-    curv = read_scalar(total[:, half:], 0) + RIDGE_COEF * sc_ref[1:2, 0:1]
-    alpha = sc_ref[0:1, 0:1] / curv
-    residual = r_ref[...] - alpha * (total[:, :half] + RIDGE_COEF * direction)
+    size = direction.shape[1]
+    if part == 0:
+        curv = read_scalar(total[:, size:], 0) + RIDGE_COEF * sc_ref[1:2, 0:1]
+        alpha = sc_ref[0:1, 0:1] / curv
+    else:
+        alpha = aux_ref[2:3, 0:1]
+    residual = r_ref[...] - alpha * (total[:, :size] + RIDGE_COEF * direction)
     if not last:
-        r_out, d_out = refs[2:]
+        r_out, d_out = refs
         r_out[...] = residual
         d_out[...] = direction
-    alpha_ref[...] = jnp.broadcast_to(alpha, alpha_ref.shape)
-    residual_out(residual, (sum_all(residual * direction),), send_ref)
+    sums = (sum_all(residual * residual), sum_all(residual * direction))
+    if part == 0:
+        out_ref[...] = jnp.zeros(out_ref.shape, F32)
+        residual_out(residual, sums + (alpha,), out_ref, send_ref)
+    else:
+        sums = tuple(aux_ref[i : i + 1, 0:1] + value for i, value in enumerate(sums))
+        residual_out(residual, sums, None, send_ref)
 
 
 def row_blocks(xt_ref):
@@ -226,28 +256,37 @@
     return [slice(i, i + width) for i in range(0, rows, width)]
 
 
-def row_half(h, xt_ref, which, block):
-    half = xt_ref.shape[0] // 2
-    return lax.dot_general(
-        h, xt_ref[half_of(which, half), block], NN, preferred_element_type=F32
-    )
-
-
-def own_rows_kernel(send_ref, xt_ref, out_ref):
-    h = send_ref[:, : xt_ref.shape[0] // 2]
+def row_part(h, xt_ref, which, part, block):
+    size = xt_ref.shape[0] // 4
+    at = pl.ds(pl.multiple_of((2 * which + part) * size, LANES), size)
+    return lax.dot_general(h, xt_ref[at, block], NN, preferred_element_type=F32)
+
+
+def rows0_kernel(mine0_ref, xt_ref, out_ref):
+    h = mine0_ref[...]
     for block in row_blocks(xt_ref):
-        out_ref[:, block] = row_half(h, xt_ref, my_core(), block)
-
-
-def mate_rows_kernel(acc_ref, mine_ref, recv_ref, xt_ref, out_ref):
-    half, rows = xt_ref.shape[0] // 2, xt_ref.shape[1]
-    h = recv_ref[:, :half]
-    both = mine_ref[:, half:].astype(F32) + recv_ref[:, half:].astype(F32)
+        out_ref[:, block] = row_part(h, xt_ref, my_core(), 0, block)
+
+
+def rows1_kernel(acc_ref, mine1_ref, recv0_ref, xt_ref, out_ref):
+    mine, mate = mine1_ref[:, : xt_ref.shape[0] // 4], recv0_ref[...]
+    for block in row_blocks(xt_ref):
+        out_ref[:, block] = (
+            acc_ref[:, block]
+            + row_part(mine, xt_ref, my_core(), 1, block)
+            + row_part(mate, xt_ref, 1 - my_core(), 0, block)
+        )
+
+
+def rows2_kernel(acc_ref, mine1_ref, recv1_ref, xt_ref, out_ref):
+    size, rows = xt_ref.shape[0] // 4, xt_ref.shape[1]
+    h = recv1_ref[:, :size]
+    both = mine1_ref[:, size:].astype(F32) + recv1_ref[:, size:].astype(F32)
     out_ref[:, rows:] = scalar_block(
         (read_scalar(both, 0), read_scalar(both, 1)), lax.axis_index("feat")
     ).astype(BF16)
     for block in row_blocks(xt_ref):
-        part = acc_ref[:, block] + row_half(h, xt_ref, 1 - my_core(), block)
+        part = acc_ref[:, block] + row_part(h, xt_ref, 1 - my_core(), 1, block)
         out_ref[:, block] = part.astype(BF16)
 
 
@@ -261,14 +300,16 @@
     curv_ref[3:, :] = jnp.zeros((5, LANES), F32)
 
 
-def finish_kernel(curv_ref, sc_ref, loss_ref, *refs):
+def finish_kernel(*refs, n):
+    parts, (sc_ref, loss_ref), refs = refs[:n], refs[n : n + 2], refs[n + 2 :]
+    curv = add_up(parts)
     count = (len(refs) - 2) // 2
     steps, scores, (out_ref, loss_out) = refs[:count], refs[count:-2], refs[-2:]
     loss_out[0, 0] = jnp.max(loss_ref[...])
-    last = sc_ref[2:3, 0:1] / (curv_ref[0:1, 0:1] + RIDGE_COEF * sc_ref[1:2, 0:1])
+    last = sc_ref[2:3, 0:1] / (curv[0:1, 0:1] + RIDGE_COEF * sc_ref[1:2, 0:1])
     total = last * scores[-1][...]
     for alpha, score in zip(steps, scores[:-1]):
-        total += alpha[0:1, 0:1] * score[...]
+        total += alpha[2:3, 0:1] * score[...]
     out_ref[...] = total
 
 
@@ -310,6 +351,12 @@
 
 def gather_sum(value, pins, axis, size, bits):
     kind = value.dtype
+    if len(bits) > 2:
+        a, b = bits[:2]
+        value = add(
+            pins, value, *[swap(value, axis, size, k) for k in (b, a, a | b)], kind=kind
+        )
+        bits = bits[2:]
     while len(bits) > 2:
         value = add(pins, value, swap(value, axis, size, bits[0]), kind=kind)
         bits = bits[1:]
@@ -326,7 +373,7 @@
 def on_device(features, weight, labels, sample_weight, *, dp, feat):
     classes, columns = weight.shape
     rows = features.shape[0]
-    half = columns // 2
+    size = columns // 4
     labels = labels.reshape(rows // LANES, LANES)
     row_weight = sample_weight.reshape(rows // LANES, LANES)
     across_feat = functools.partial(gather_sum, axis="feat", size=feat, bits=bits_of(feat))
@@ -353,36 +400,39 @@
     )
     pins = [x, xt, weight]
 
-    def column_sums(c, send, block):
-        received = core_swap(send)
-        (own,) = call(
-            own_columns_kernel,
-            "own_columns",
-            [((classes, half + LANES), F32)],
-            c,
-            block,
-            x,
-            pins=pins,
-        )
-        return across_chips(add(pins, own, received, kind=BF16), pins)
-
-    def row_sums(send):
-        received = core_swap(send)
-        (part,) = call(
-            own_rows_kernel,
-            "own_rows",
-            [((classes, rows), F32)],
-            send,
-            xt,
-            pins=pins,
-        )
+    def column_sums(c, send0, send1, block):
+        received0, received1 = core_swap(send0), core_swap(send1)
+        sums = []
+        for part, received, extra in ((0, received0, (block,)), (1, received1, ())):
+            (own,) = call(
+                functools.partial(own_columns_kernel, part=part),
+                "own_columns",
+                [((classes, size + LANES * len(extra)), F32)],
+                c,
+                *extra,
+                x,
+                pins=pins,
+            )
+            sums.append(across_chips(add(pins, own, received, kind=BF16), pins))
+        return sums
+
+    full = [((classes, rows), F32)]
+
+    def first_rows(send0):
+        received0 = core_swap(send0)
+        (acc,) = call(rows0_kernel, "rows_0", full, send0, xt, pins=pins)
+        return acc, received0
+
+    def row_sums(acc, received0, send1):
+        received1 = core_swap(send1)
+        (acc,) = call(rows1_kernel, "rows_1", full, acc, send1, received0, xt, pins=pins)
         (score,) = call(
-            mate_rows_kernel,
-            "mate_rows",
+            rows2_kernel,
+            "rows_2",
             [((classes, rows + LANES), BF16)],
-            part,
-            send,
-            received,
+            acc,
+            send1,
+            received1,
             xt,
             pins=pins,
         )
@@ -390,11 +440,13 @@
 
     curv_outs = [
         ((classes, rows), BF16),
-        ((classes, half + LANES), BF16),
+        ((classes, size + LANES), BF16),
+        ((classes, size), BF16),
         ((16, LANES), F32),
     ]
+    aux_out = ((8, LANES), F32)
     parts = across_feat(logit_part, pins)
-    prob, e, send, block = call(
+    prob, e, send0, send1, block = call(
         functools.partial(probs_kernel, n=len(parts)),
         "probs",
         [((classes, rows), F32)] + curv_outs,
@@ -404,22 +456,33 @@
         x,
         pins=pins,
     )
-    parts = column_sums(e, send, block)
-    residual, send, scale, loss = call(
-        functools.partial(gradient_kernel, n=len(parts)),
-        "gradient",
-        [((classes, half), F32), ((classes, half + LANES), BF16), ((1, rows), F32), ((8, LANES), F32)],
-        *parts,
+    parts0, parts1 = column_sums(e, send0, send1, block)
+    residual0, send0, aux, scale, loss = call(
+        functools.partial(gradient0_kernel, n=len(parts0)),
+        "gradient_0",
+        [((classes, size), F32), ((classes, size), BF16), aux_out, ((1, rows), F32), aux_out],
+        *parts0,
         weight,
         row_weight,
         pins=pins,
     )
-    pins[2:] = [residual]
+    acc, received0 = first_rows(send0)
+    residual1, send1 = call(
+        functools.partial(gradient1_kernel, n=len(parts1)),
+        "gradient_1",
+        [((classes, size), F32), ((classes, size + LANES), BF16)],
+        *parts1,
+        weight,
+        aux,
+        pins=pins + [acc, received0],
+    )
+    residuals = [residual0, residual1]
+    directions = [(), ()]
+    pins[2:] = residuals
     state, steps, scores = (), [], []
-    direction = ()
     for i in range(CG_ITERS - 1):
-        parts = row_sums(send)
-        s, c, send, block, sc = call(
+        parts = row_sums(acc, received0, send1)
+        s, c, send0, send1, block, sc = call(
             functools.partial(curv_kernel, n=len(parts), first=i == 0),
             "curvature",
             [((classes, rows), F32)] + curv_outs + [((8, LANES), F32)],
@@ -432,24 +495,38 @@
         )
         state = (s, sc)
         scores.append(s)
-        parts = column_sums(c, send, block)
+        both = column_sums(c, send0, send1, block)
         last = i == CG_ITERS - 2
-        send, alpha, *vectors = call(
-            functools.partial(update_kernel, n=len(parts), first=i == 0, last=last),
-            "update",
-            [((classes, half + LANES), BF16), ((8, LANES), F32)]
-            + [((classes, half), F32)] * (0 if last else 2),
-            *parts,
-            residual,
+        vectors = [((classes, size), F32)] * (0 if last else 2)
+        send0, aux, *first_half = call(
+            functools.partial(update_kernel, n=len(both[0]), part=0, first=i == 0, last=last),
+            "update_0",
+            [((classes, size), BF16), aux_out] + vectors,
+            *both[0],
+            residuals[0],
             sc,
-            *direction,
+            sc,
+            *directions[0],
             pins=pins,
         )
-        pins[2:] = vectors
+        acc, received0 = first_rows(send0)
+        send1, *second_half = call(
+            functools.partial(update_kernel, n=len(both[1]), part=1, first=i == 0, last=last),
+            "update_1",
+            [((classes, size + LANES), BF16)] + vectors,
+            *both[1],
+            residuals[1],
+            sc,
+            aux,
+            *directions[1],
+            pins=pins + [acc, received0],
+        )
+        steps.append(aux)
         if not last:
-            residual, *direction = vectors
-        steps.append(alpha)
-    parts = row_sums(send)
+            residuals = [first_half[0], second_half[0]]
+            directions = [first_half[1:], second_half[1:]]
+        pins[2:] = first_half + second_half
+    parts = row_sums(acc, received0, send1)
     s, sc = call(
         functools.partial(last_kernel, n=len(parts)),
         "last",
@@ -461,14 +538,12 @@
         pins=pins,
     )
     scores.append(s)
-    curv = sc
-    for bit in bits_of(dp):
-        curv = add(pins, curv, swap(curv, "dp", dp, bit), kind=F32)
+    parts = gather_sum(sc, pins, "dp", dp, bits_of(dp))
     out, loss = call(
-        finish_kernel,
+        functools.partial(finish_kernel, n=len(parts)),
         "finish",
         [((classes, rows), F32), ((1, 1), F32)],
-        curv,
+        *parts,
         sc,
         loss,
         *steps,

time: 137 us -> 133 us (0.971)
  waiting for transfers between devices: 58.4 us -> 45.9 us
  starting transfers between devices: 36.1 us -> 42.8 us
  Pallas kernels: 41.5 us -> 43.3 us
    ppermute x34 -> x47, waiting for transfers between devices: 58.4 us -> 45.9 us  [swap(): return lax.ppermute(value, axis, [(i, i ^ bit) for i in range(size)])]
    ppermute x34 -> x47, starting transfers between devices: 36.1 us -> 42.8 us  [swap(): return lax.ppermute(value, axis, [(i, i ^ bit) for i in range(size)])]
    pallas_call x34 -> x48, Pallas kernels: 41.5 us -> 43.3 us  [call(): pl.pallas_call(body, out_shape=tuple((out_space(shape, dtype) for shape,...]
  transfers between devices with their start and end apart: 34 -> 47, of which waited for: 22 -> 38; matrix products, arithmetic and copies ran while one was open for 0% -> 0% of each run, Pallas kernels for 10% -> 15%
where the time goes in v2:
time: 133 us
  waiting for transfers between devices  45.9 us (35%)
  Pallas kernels  43.3 us (33%)
  starting transfers between devices  42.8 us (32%)
    ppermute x47, waiting for transfers between devices, swap(): return lax.ppermute(value, axis, [(i, i ^ bit) for i in range(size)])  45.9 us
    pallas_call x48, Pallas kernels, call(): pl.pallas_call(body, out_shape=tuple((out_space(shape, dtype) for shape,...  43.3 us
    ppermute x47, starting transfers between devices, swap(): return lax.ppermute(value, axis, [(i, i ^ bit) for i in range(size)])  42.8 us
  transfers between devices with their start and end apart: 47, of which 38 were waited for; matrix products, arithmetic and copies ran while one was open for 0% of the time, Pallas kernels for 15%

profile of v2, /device:TPU:0, one launch (start us, length us, event | category | flops | bytes accessed | tf_op | source)
XLA Modules:
  0.0 133.1 jit_solution(5146507379919917137)
XLA Ops:
  0.6 10.2 %load.1 = (bf16[1536,8192]{1,0:T(8,128)(2,1)S(1)}, bf16[8192,1536]{1,0:T(8,128)(2,1)S(1)}, f32[16,8192]{1,0:T(8,128)S(1)}, f32[16,1536]{1,0:T(8,128)S(1)}) custom-call(bf16[1536,8192]{1,0:T(8,128)(2,1)} %refs_0_.1, f32[16,8192]{1,0:T(8,128)} %refs_1_.1), custom_call_target="tpu_custom_call" | custom-call | tf_op jit(solution)/shard_map/load/pallas_call | solution.py:333
  10.8 4.0 %collective-permute-start.2 = (f32[16,1536]{1,0:T(8,128)S(1)}, f32[16,1536]{1,0:T(8,128)S(1)}, u32[]{:S(2)}, u32[]{:S(2)}) collective-permute-start(f32[16,1536]{1,0:T(8,128)S(1)} %get-tuple-element.56.refs_0_), channel_id=1, source_target_pairs={{0,3},{1,2},{2,1},{3,0},{4,7},{5,6},{6,5},{7,4},{8,11},{9,10},{10,... | collective-permute-start | bytes 294920 | tf_op jit(solution)/shard_map/ppermute | solution.py:349
  15.5 2.5 %collective-permute-done.2.refs_3_ = f32[16,1536]{1,0:T(8,128)S(1)} collective-permute-done((f32[16,1536]{1,0:T(8,128)S(1)}, f32[16,1536]{1,0:T(8,128)S(1)}, u32[]{:S(2)}, u32[]{:S(2)}) %collective-permute-start.2) | collective-permute-done | bytes 98336 | tf_op jit(solution)/shard_map/ppermute | solution.py:349
  18.0 1.7 %collective-permute-done.1.refs_2_ = f32[16,1536]{1,0:T(8,128)S(1)} collective-permute-done((f32[16,1536]{1,0:T(8,128)S(1)}, f32[16,1536]{1,0:T(8,128)S(1)}, u32[]{:S(2)}, u32[]{:S(2)}) %collective-permute-start.1) | collective-permute-done | bytes 98336 | tf_op jit(solution)/shard_map/ppermute | solution.py:349
  20.0 2.7 %collective-permute-start.3 = (f32[16,1536]{1,0:T(8,128)S(1)}, f32[16,1536]{1,0:T(8,128)S(1)}, u32[]{:S(2)}, u32[]{:S(2)}) collective-permute-start(f32[16,1536]{1,0:T(8,128)S(1)} %add.13.refs_0_), channel_id=1, source_target_pairs={{0,4},{1,5},{2,6},{3,7},{4,0},{5,1},{6,2},{7,3},{8,12},{9,13},{10,... | collective-permute-start | bytes 294920 | tf_op jit(solution)/shard_map/ppermute | solution.py:349
  22.7 4.9 %collective-permute-done.3.refs_1_ = f32[16,1536]{1,0:T(8,128)S(1)} collective-permute-done((f32[16,1536]{1,0:T(8,128)S(1)}, f32[16,1536]{1,0:T(8,128)S(1)}, u32[]{:S(2)}, u32[]{:S(2)}) %collective-permute-start.3) | collective-permute-done | bytes 98336 | tf_op jit(solution)/shard_map/ppermute | solution.py:349
  27.5 1.8 %probs.1 = (f32[16,1536]{1,0:T(8,128)S(1)}, bf16[16,1536]{1,0:T(8,128)(2,1)S(1)}, bf16[16,2176]{1,0:T(8,128)(2,1)S(1)}, bf16[16,2048]{1,0:T(8,128)(2,1)S(1)}, f32[16,128]{1,0:T(8,128)S(1)}) custom-call(f32[16,1536]{1,0:T(8,128)S(1)} %add.13.refs_0_, f32[16,1536]{1,0:T(8,128)S(1)} %collective-permute-done.3.refs_1_, s32[12,128]{1,0:T(8,128)S(1)} %bitcast.6, ...), custom_call_target="tpu_custom_call" | custom-call | tf_op jit(solution)/shard_map/probs/pallas_call | solution.py:333
  38.1 1.7 %rows_1.4.refs_0_ = f32[16,1536]{1,0:T(8,128)S(1)} custom-call(f32[16,1536]{1,0:T(8,128)S(1)} %rows_0.4.refs_7_.refs_0_, bf16[16,2176]{1,0:T(8,128)(2,1)S(1)} %get-tuple-element.66.refs_1_, bf16[16,2048]{1,0:T(8,128)(2,1)S(1)} %collective-permute-done.8.refs_8_.refs_2_, ...), custom_call_target="tpu_custom_call" | custom-call | tf_op jit(solution)/shard_map/rows_1/pallas_call | solution.py:333
  44.3 2.0 %collective-permute-done.12.refs_3_ = bf16[16,1664]{1,0:T(8,128)(2,1)S(1)} collective-permute-done((bf16[16,1664]{1,0:T(8,128)(2,1)S(1)}, bf16[16,1664]{1,0:T(8,128)(2,1)S(1)}, u32[]{:S(2)}, u32[]{:S(2)}) %collective-permute-start.12) | collective-permute-done | bytes 53280 | tf_op jit(solution)/shard_map/ppermute | solution.py:349
  46.8 3.4 %collective-permute-start.13 = (bf16[16,1664]{1,0:T(8,128)(2,1)S(1)}, bf16[16,1664]{1,0:T(8,128)(2,1)S(1)}, u32[]{:S(2)}, u32[]{:S(2)}) collective-permute-start(bf16[16,1664]{1,0:T(8,128)(2,1)S(1)} %add.16.refs_0_), channel_id=1, source_target_pairs={{0,4},{1,5},{2,6},{3,7},{4,0},{5,1},{6,2},{7,3},{8,12},{9,13},{10,... | collective-permute-start | bytes 159752 | tf_op jit(solution)/shard_map/ppermute | solution.py:349
  50.3 2.1 %collective-permute-done.13.refs_1_ = bf16[16,1664]{1,0:T(8,128)(2,1)S(1)} collective-permute-done((bf16[16,1664]{1,0:T(8,128)(2,1)S(1)}, bf16[16,1664]{1,0:T(8,128)(2,1)S(1)}, u32[]{:S(2)}, u32[]{:S(2)}) %collective-permute-start.13) | collective-permute-done | bytes 53280 | tf_op jit(solution)/shard_map/ppermute | solution.py:349
  52.4 1.8 %curvature.3 = (f32[16,1536]{1,0:T(8,128)S(1)}, bf16[16,1536]{1,0:T(8,128)(2,1)S(1)}, bf16[16,2176]{1,0:T(8,128)(2,1)S(1)}, bf16[16,2048]{1,0:T(8,128)(2,1)S(1)}...) custom-call(bf16[16,1664]{1,0:T(8,128)(2,1)S(1)} %add.16.refs_0_, bf16[16,1664]{1,0:T(8,128)(2,1)S(1)} %collective-permute-done.13.refs_1_, ...), custom_call_target="tpu_custom_call" | custom-call | tf_op jit(solution)/shard_map/curvature/pallas_call | solution.py:333
  62.0 1.7 %rows_1.5.refs_0_ = f32[16,1536]{1,0:T(8,128)S(1)} custom-call(f32[16,1536]{1,0:T(8,128)S(1)} %rows_0.5.refs_9_.refs_0_, bf16[16,2176]{1,0:T(8,128)(2,1)S(1)} %get-tuple-element.78.refs_1_, bf16[16,2048]{1,0:T(8,128)(2,1)S(1)} %collective-permute-done.18.refs_10_.refs_2_, ...), custom_call_target="tpu_custom_call" | custom-call | tf_op jit(solution)/shard_map/rows_1/pallas_call | solution.py:333
  71.7 1.9 %collective-permute-start.23 = (bf16[16,1664]{1,0:T(8,128)(2,1)S(1)}, bf16[16,1664]{1,0:T(8,128)(2,1)S(1)}, u32[]{:S(2)}, u32[]{:S(2)}) collective-permute-start(bf16[16,1664]{1,0:T(8,128)(2,1)S(1)} %add.19.refs_0_), channel_id=1, source_target_pairs={{0,4},{1,5},{2,6},{3,7},{4,0},{5,1},{6,2},{7,3},{8,12},{9,13},{10,... | collective-permute-start | bytes 159752 | tf_op jit(solution)/shard_map/ppermute | solution.py:349
  73.6 3.8 %collective-permute-done.23.refs_1_ = bf16[16,1664]{1,0:T(8,128)(2,1)S(1)} collective-permute-done((bf16[16,1664]{1,0:T(8,128)(2,1)S(1)}, bf16[16,1664]{1,0:T(8,128)(2,1)S(1)}, u32[]{:S(2)}, u32[]{:S(2)}) %collective-permute-start.23) | collective-permute-done | bytes 53280 | tf_op jit(solution)/shard_map/ppermute | solution.py:349
  77.4 1.9 %curvature.4 = (f32[16,1536]{1,0:T(8,128)S(1)}, bf16[16,1536]{1,0:T(8,128)(2,1)S(1)}, bf16[16,2176]{1,0:T(8,128)(2,1)S(1)}, bf16[16,2048]{1,0:T(8,128)(2,1)S(1)}...) custom-call(bf16[16,1664]{1,0:T(8,128)(2,1)S(1)} %add.19.refs_0_, bf16[16,1664]{1,0:T(8,128)(2,1)S(1)} %collective-permute-done.23.refs_1_, ...), custom_call_target="tpu_custom_call" | custom-call | tf_op jit(solution)/shard_map/curvature/pallas_call | solution.py:333
  88.1 1.7 %rows_1.6.refs_0_ = f32[16,1536]{1,0:T(8,128)S(1)} custom-call(f32[16,1536]{1,0:T(8,128)S(1)} %rows_0.6.refs_12_.refs_0_, bf16[16,2176]{1,0:T(8,128)(2,1)S(1)} %get-tuple-element.91.refs_1_, bf16[16,2048]{1,0:T(8,128)(2,1)S(1)} %collective-permute-done.28.refs_13_.refs_2_, ...), custom_call_target="tpu_custom_call" | custom-call | tf_op jit(solution)/shard_map/rows_1/pallas_call | solution.py:333
  94.3 2.0 %collective-permute-done.32.refs_3_ = bf16[16,1664]{1,0:T(8,128)(2,1)S(1)} collective-permute-done((bf16[16,1664]{1,0:T(8,128)(2,1)S(1)}, bf16[16,1664]{1,0:T(8,128)(2,1)S(1)}, u32[]{:S(2)}, u32[]{:S(2)}) %collective-permute-start.32) | collective-permute-done | bytes 53280 | tf_op jit(solution)/shard_map/ppermute | solution.py:349
  96.8 3.0 %collective-permute-start.33 = (bf16[16,1664]{1,0:T(8,128)(2,1)S(1)}, bf16[16,1664]{1,0:T(8,128)(2,1)S(1)}, u32[]{:S(2)}, u32[]{:S(2)}) collective-permute-start(bf16[16,1664]{1,0:T(8,128)(2,1)S(1)} %add.22.refs_0_), channel_id=1, source_target_pairs={{0,4},{1,5},{2,6},{3,7},{4,0},{5,1},{6,2},{7,3},{8,12},{9,13},{10,... | collective-permute-start | bytes 159752 | tf_op jit(solution)/shard_map/ppermute | solution.py:349
  99.8 2.1 %collective-permute-done.33.refs_1_ = bf16[16,1664]{1,0:T(8,128)(2,1)S(1)} collective-permute-done((bf16[16,1664]{1,0:T(8,128)(2,1)S(1)}, bf16[16,1664]{1,0:T(8,128)(2,1)S(1)}, u32[]{:S(2)}, u32[]{:S(2)}) %collective-permute-start.33) | collective-permute-done | bytes 53280 | tf_op jit(solution)/shard_map/ppermute | solution.py:349
  101.9 1.9 %curvature.5 = (f32[16,1536]{1,0:T(8,128)S(1)}, bf16[16,1536]{1,0:T(8,128)(2,1)S(1)}, bf16[16,2176]{1,0:T(8,128)(2,1)S(1)}, bf16[16,2048]{1,0:T(8,128)(2,1)S(1)}...) custom-call(bf16[16,1664]{1,0:T(8,128)(2,1)S(1)} %add.22.refs_0_, bf16[16,1664]{1,0:T(8,128)(2,1)S(1)} %collective-permute-done.33.refs_1_, ...), custom_call_target="tpu_custom_call" | custom-call | tf_op jit(solution)/shard_map/curvature/pallas_call | solution.py:333
  111.7 1.7 %rows_1.7.refs_0_ = f32[16,1536]{1,0:T(8,128)S(1)} custom-call(f32[16,1536]{1,0:T(8,128)S(1)} %rows_0.7.refs_12_.refs_0_, bf16[16,2176]{1,0:T(8,128)(2,1)S(1)} %update_1.5.refs_1_, bf16[16,2048]{1,0:T(8,128)(2,1)S(1)} %collective-permute-done.38.refs_13_.refs_2_, ...), custom_call_target="tpu_custom_call" | custom-call | tf_op jit(solution)/shard_map/rows_1/pallas_call | solution.py:333
  114.4 2.0 %collective-permute-start.42 = (bf16[16,1664]{1,0:T(8,128)(2,1)S(1)}, bf16[16,1664]{1,0:T(8,128)(2,1)S(1)}, u32[]{:S(2)}, u32[]{:S(2)}) collective-permute-start(bf16[16,1664]{1,0:T(8,128)(2,1)S(1)} %rows_2.7.refs_0_), channel_id=1, source_target_pairs={{0,3},{1,2},{2,1},{3,0},{4,7},{5,6},{6,5},{7,4},{8,11},{9,10},{10,... | collective-permute-start | bytes 159752 | tf_op jit(solution)/shard_map/ppermute | solution.py:349
  123.3 3.9 %collective-permute-done.43.refs_1_ = bf16[16,1664]{1,0:T(8,128)(2,1)S(1)} collective-permute-done((bf16[16,1664]{1,0:T(8,128)(2,1)S(1)}, bf16[16,1664]{1,0:T(8,128)(2,1)S(1)}, u32[]{:S(2)}, u32[]{:S(2)}) %collective-permute-start.43) | collective-permute-done | bytes 53280 | tf_op jit(solution)/shard_map/ppermute | solution.py:349
  (146 shorter events, 65.4 us)
Async XLA Ops:
  10.8 7.2 %collective-permute-start.2 = (f32[16,1536]{1,0:T(8,128)S(1)}, f32[16,1536]{1,0:T(8,128)S(1)}, u32[]{:S(2)}, u32[]{:S(2)}) collective-permute-start(f32[16,1536]{1,0:T(8,128)S(1)} %get-tuple-element.56.refs_0_), channel_id=1, source_target_pairs={{0,3},{1,2},{2,1},{3,0},{4,7},{5,6},{6,5},{7,4},{8,11},{9,10},{10,... | collective-permute-start | bytes 294920 | tf_op jit(solution)/shard_map/ppermute | solution.py:349
  14.8 4.9 %collective-permute-start.1 = (f32[16,1536]{1,0:T(8,128)S(1)}, f32[16,1536]{1,0:T(8,128)S(1)}, u32[]{:S(2)}, u32[]{:S(2)}) collective-permute-start(f32[16,1536]{1,0:T(8,128)S(1)} %get-tuple-element.56.refs_0_), channel_id=1, source_target_pairs={{0,1},{1,0},{2,3},{3,2},{4,5},{5,4},{6,7},{7,6},{8,9},{9,8},{10,11... | collective-permute-start | bytes 294920 | tf_op jit(solution)/shard_map/ppermute | solution.py:349
  15.4 4.6 %collective-permute-start = (f32[16,1536]{1,0:T(8,128)S(1)}, f32[16,1536]{1,0:T(8,128)S(1)}, u32[]{:S(2)}, u32[]{:S(2)}) collective-permute-start(f32[16,1536]{1,0:T(8,128)S(1)} %get-tuple-element.56.refs_0_), channel_id=1, source_target_pairs={{0,2},{1,3},{2,0},{3,1},{4,6},{5,7},{6,4},{7,5},{8,10},{9,11},{10,... | collective-permute-start | bytes 294920 | tf_op jit(solution)/shard_map/ppermute | solution.py:349
  20.0 7.5 %collective-permute-start.3 = (f32[16,1536]{1,0:T(8,128)S(1)}, f32[16,1536]{1,0:T(8,128)S(1)}, u32[]{:S(2)}, u32[]{:S(2)}) collective-permute-start(f32[16,1536]{1,0:T(8,128)S(1)} %add.13.refs_0_), channel_id=1, source_target_pairs={{0,4},{1,5},{2,6},{3,7},{4,0},{5,1},{6,2},{7,3},{8,12},{9,13},{10,... | collective-permute-start | bytes 294920 | tf_op jit(solution)/shard_map/ppermute | solution.py:349
  30.6 4.4 %collective-permute-start.5 = (bf16[16,2176]{1,0:T(8,128)(2,1)S(1)}, bf16[16,2176]{1,0:T(8,128)(2,1)S(1)}, u32[]{:S(2)}, u32[]{:S(2)}) collective-permute-start(bf16[16,2176]{1,0:T(8,128)(2,1)S(1)} %add.14.refs_0_), channel_id=1, source_target_pairs={{0,16},{8,24},{16,0},{24,8},{1,17},{9,25},{17,1},{25,9},{2,18},{10... | collective-permute-start | bytes 208904 | tf_op jit(solution)/shard_map/ppermute | solution.py:349
  33.5 4.3 %collective-permute-start.7 = (bf16[16,2048]{1,0:T(8,128)(2,1)S(1)}, bf16[16,2048]{1,0:T(8,128)(2,1)S(1)}, u32[]{:S(2)}, u32[]{:S(2)}) collective-permute-start(bf16[16,2048]{1,0:T(8,128)(2,1)S(1)} %add.15.refs_0_), channel_id=1, source_target_pairs={{0,16},{8,24},{16,0},{24,8},{1,17},{9,25},{17,1},{25,9},{2,18},{10... | collective-permute-start | bytes 196616 | tf_op jit(solution)/shard_map/ppermute | solution.py:349
  40.8 5.5 %collective-permute-start.12 = (bf16[16,1664]{1,0:T(8,128)(2,1)S(1)}, bf16[16,1664]{1,0:T(8,128)(2,1)S(1)}, u32[]{:S(2)}, u32[]{:S(2)}) collective-permute-start(bf16[16,1664]{1,0:T(8,128)(2,1)S(1)} %rows_2.4.refs_0_), channel_id=1, source_target_pairs={{0,3},{1,2},{2,1},{3,0},{4,7},{5,6},{6,5},{7,4},{8,11},{9,10},{10,... | collective-permute-start | bytes 159752 | tf_op jit(solution)/shard_map/ppermute | solution.py:349
  41.4 5.1 %collective-permute-start.11 = (bf16[16,1664]{1,0:T(8,128)(2,1)S(1)}, bf16[16,1664]{1,0:T(8,128)(2,1)S(1)}, u32[]{:S(2)}, u32[]{:S(2)}) collective-permute-start(bf16[16,1664]{1,0:T(8,128)(2,1)S(1)} %rows_2.4.refs_0_), channel_id=1, source_target_pairs={{0,1},{1,0},{2,3},{3,2},{4,5},{5,4},{6,7},{7,6},{8,9},{9,8},{10,11... | collective-permute-start | bytes 159752 | tf_op jit(solution)/shard_map/ppermute | solution.py:349
  46.8 5.6 %collective-permute-start.13 = (bf16[16,1664]{1,0:T(8,128)(2,1)S(1)}, bf16[16,1664]{1,0:T(8,128)(2,1)S(1)}, u32[]{:S(2)}, u32[]{:S(2)}) collective-permute-start(bf16[16,1664]{1,0:T(8,128)(2,1)S(1)} %add.16.refs_0_), channel_id=1, source_target_pairs={{0,4},{1,5},{2,6},{3,7},{4,0},{5,1},{6,2},{7,3},{8,12},{9,13},{10,... | collective-permute-start | bytes 159752 | tf_op jit(solution)/shard_map/ppermute | solution.py:349
  55.4 4.4 %collective-permute-start.15 = (bf16[16,2176]{1,0:T(8,128)(2,1)S(1)}, bf16[16,2176]{1,0:T(8,128)(2,1)S(1)}, u32[]{:S(2)}, u32[]{:S(2)}) collective-permute-start(bf16[16,2176]{1,0:T(8,128)(2,1)S(1)} %add.17.refs_0_), channel_id=1, source_target_pairs={{0,16},{8,24},{16,0},{24,8},{1,17},{9,25},{17,1},{25,9},{2,18},{10... | collective-permute-start | bytes 208904 | tf_op jit(solution)/shard_map/ppermute | solution.py:349
  57.3 4.3 %collective-permute-start.17 = (bf16[16,2048]{1,0:T(8,128)(2,1)S(1)}, bf16[16,2048]{1,0:T(8,128)(2,1)S(1)}, u32[]{:S(2)}, u32[]{:S(2)}) collective-permute-start(bf16[16,2048]{1,0:T(8,128)(2,1)S(1)} %add.18.refs_0_), channel_id=1, source_target_pairs={{0,16},{8,24},{16,0},{24,8},{1,17},{9,25},{17,1},{25,9},{2,18},{10... | collective-permute-start | bytes 196616 | tf_op jit(solution)/shard_map/ppermute | solution.py:349
  64.9 5.2 %collective-permute-start.22 = (bf16[16,1664]{1,0:T(8,128)(2,1)S(1)}, bf16[16,1664]{1,0:T(8,128)(2,1)S(1)}, u32[]{:S(2)}, u32[]{:S(2)}) collective-permute-start(bf16[16,1664]{1,0:T(8,128)(2,1)S(1)} %rows_2.5.refs_0_), channel_id=1, source_target_pairs={{0,3},{1,2},{2,1},{3,0},{4,7},{5,6},{6,5},{7,4},{8,11},{9,10},{10,... | collective-permute-start | bytes 159752 | tf_op jit(solution)/shard_map/ppermute | solution.py:349
  66.4 4.7 %collective-permute-start.21 = (bf16[16,1664]{1,0:T(8,128)(2,1)S(1)}, bf16[16,1664]{1,0:T(8,128)(2,1)S(1)}, u32[]{:S(2)}, u32[]{:S(2)}) collective-permute-start(bf16[16,1664]{1,0:T(8,128)(2,1)S(1)} %rows_2.5.refs_0_), channel_id=1, source_target_pairs={{0,1},{1,0},{2,3},{3,2},{4,5},{5,4},{6,7},{7,6},{8,9},{9,8},{10,11... | collective-permute-start | bytes 159752 | tf_op jit(solution)/shard_map/ppermute | solution.py:349
  71.7 5.7 %collective-permute-start.23 = (bf16[16,1664]{1,0:T(8,128)(2,1)S(1)}, bf16[16,1664]{1,0:T(8,128)(2,1)S(1)}, u32[]{:S(2)}, u32[]{:S(2)}) collective-permute-start(bf16[16,1664]{1,0:T(8,128)(2,1)S(1)} %add.19.refs_0_), channel_id=1, source_target_pairs={{0,4},{1,5},{2,6},{3,7},{4,0},{5,1},{6,2},{7,3},{8,12},{9,13},{10,... | collective-permute-start | bytes 159752 | tf_op jit(solution)/shard_map/ppermute | solution.py:349
  80.6 4.4 %collective-permute-start.25 = (bf16[16,2176]{1,0:T(8,128)(2,1)S(1)}, bf16[16,2176]{1,0:T(8,128)(2,1)S(1)}, u32[]{:S(2)}, u32[]{:S(2)}) collective-permute-start(bf16[16,2176]{1,0:T(8,128)(2,1)S(1)} %add.20.refs_0_), channel_id=1, source_target_pairs={{0,16},{8,24},{16,0},{24,8},{1,17},{9,25},{17,1},{25,9},{2,18},{10... | collective-permute-start | bytes 208904 | tf_op jit(solution)/shard_map/ppermute | solution.py:349
  83.4 4.3 %collective-permute-start.27 = (bf16[16,2048]{1,0:T(8,128)(2,1)S(1)}, bf16[16,2048]{1,0:T(8,128)(2,1)S(1)}, u32[]{:S(2)}, u32[]{:S(2)}) collective-permute-start(bf16[16,2048]{1,0:T(8,128)(2,1)S(1)} %add.21.refs_0_), channel_id=1, source_target_pairs={{0,16},{8,24},{16,0},{24,8},{1,17},{9,25},{17,1},{25,9},{2,18},{10... | collective-permute-start | bytes 196616 | tf_op jit(solution)/shard_map/ppermute | solution.py:349
  90.8 5.5 %collective-permute-start.32 = (bf16[16,1664]{1,0:T(8,128)(2,1)S(1)}, bf16[16,1664]{1,0:T(8,128)(2,1)S(1)}, u32[]{:S(2)}, u32[]{:S(2)}) collective-permute-start(bf16[16,1664]{1,0:T(8,128)(2,1)S(1)} %rows_2.6.refs_0_), channel_id=1, source_target_pairs={{0,3},{1,2},{2,1},{3,0},{4,7},{5,6},{6,5},{7,4},{8,11},{9,10},{10,... | collective-permute-start | bytes 159752 | tf_op jit(solution)/shard_map/ppermute | solution.py:349
  91.4 5.1 %collective-permute-start.31 = (bf16[16,1664]{1,0:T(8,128)(2,1)S(1)}, bf16[16,1664]{1,0:T(8,128)(2,1)S(1)}, u32[]{:S(2)}, u32[]{:S(2)}) collective-permute-start(bf16[16,1664]{1,0:T(8,128)(2,1)S(1)} %rows_2.6.refs_0_), channel_id=1, source_target_pairs={{0,1},{1,0},{2,3},{3,2},{4,5},{5,4},{6,7},{7,6},{8,9},{9,8},{10,11... | collective-permute-start | bytes 159752 | tf_op jit(solution)/shard_map/ppermute | solution.py:349
  96.8 5.1 %collective-permute-start.33 = (bf16[16,1664]{1,0:T(8,128)(2,1)S(1)}, bf16[16,1664]{1,0:T(8,128)(2,1)S(1)}, u32[]{:S(2)}, u32[]{:S(2)}) collective-permute-start(bf16[16,1664]{1,0:T(8,128)(2,1)S(1)} %add.22.refs_0_), channel_id=1, source_target_pairs={{0,4},{1,5},{2,6},{3,7},{4,0},{5,1},{6,2},{7,3},{8,12},{9,13},{10,... | collective-permute-start | bytes 159752 | tf_op jit(solution)/shard_map/ppermute | solution.py:349
  105.1 4.4 %collective-permute-start.35 = (bf16[16,2176]{1,0:T(8,128)(2,1)S(1)}, bf16[16,2176]{1,0:T(8,128)(2,1)S(1)}, u32[]{:S(2)}, u32[]{:S(2)}) collective-permute-start(bf16[16,2176]{1,0:T(8,128)(2,1)S(1)} %add.23.refs_0_), channel_id=1, source_target_pairs={{0,16},{8,24},{16,0},{24,8},{1,17},{9,25},{17,1},{25,9},{2,18},{10... | collective-permute-start | bytes 208904 | tf_op jit(solution)/shard_map/ppermute | solution.py:349
  107.0 4.3 %collective-permute-start.37 = (bf16[16,2048]{1,0:T(8,128)(2,1)S(1)}, bf16[16,2048]{1,0:T(8,128)(2,1)S(1)}, u32[]{:S(2)}, u32[]{:S(2)}) collective-permute-start(bf16[16,2048]{1,0:T(8,128)(2,1)S(1)} %add.24.refs_0_), channel_id=1, source_target_pairs={{0,16},{8,24},{16,0},{24,8},{1,17},{9,25},{17,1},{25,9},{2,18},{10... | collective-permute-start | bytes 196616 | tf_op jit(solution)/shard_map/ppermute | solution.py:349
  114.4 5.2 %collective-permute-start.42 = (bf16[16,1664]{1,0:T(8,128)(2,1)S(1)}, bf16[16,1664]{1,0:T(8,128)(2,1)S(1)}, u32[]{:S(2)}, u32[]{:S(2)}) collective-permute-start(bf16[16,1664]{1,0:T(8,128)(2,1)S(1)} %rows_2.7.refs_0_), channel_id=1, source_target_pairs={{0,3},{1,2},{2,1},{3,0},{4,7},{5,6},{6,5},{7,4},{8,11},{9,10},{10,... | collective-permute-start | bytes 159752 | tf_op jit(solution)/shard_map/ppermute | solution.py:349
  116.4 4.3 %collective-permute-start.41 = (bf16[16,1664]{1,0:T(8,128)(2,1)S(1)}, bf16[16,1664]{1,0:T(8,128)(2,1)S(1)}, u32[]{:S(2)}, u32[]{:S(2)}) collective-permute-start(bf16[16,1664]{1,0:T(8,128)(2,1)S(1)} %rows_2.7.refs_0_), channel_id=1, source_target_pairs={{0,1},{1,0},{2,3},{3,2},{4,5},{5,4},{6,7},{7,6},{8,9},{9,8},{10,11... | collective-permute-start | bytes 159752 | tf_op jit(solution)/shard_map/ppermute | solution.py:349
  121.6 5.5 %collective-permute-start.43 = (bf16[16,1664]{1,0:T(8,128)(2,1)S(1)}, bf16[16,1664]{1,0:T(8,128)(2,1)S(1)}, u32[]{:S(2)}, u32[]{:S(2)}) collective-permute-start(bf16[16,1664]{1,0:T(8,128)(2,1)S(1)} %add.25.refs_0_), channel_id=1, source_target_pairs={{0,4},{1,5},{2,6},{3,7},{4,0},{5,1},{6,2},{7,3},{8,12},{9,13},{10,... | collective-permute-start | bytes 159752 | tf_op jit(solution)/shard_map/ppermute | solution.py:349
  (37 other events, 247.6 us)

commit v3 on v2

--- a/solution.py
+++ b/solution.py
@@ -102,16 +102,18 @@
         out_ref[:, i : i + width] = block.astype(out_ref.dtype)
 
 
-def send_columns(c, x_ref, block, send0_ref, send1_ref):
-    size = x_ref.shape[1] // 4
-    send0_ref[:, size:] = block.astype(BF16)
+def send_columns(c, x_ref, block, send0_ref):
+    send0_ref[:, x_ref.shape[1] // 4 :] = block.astype(BF16)
     column_part(c, x_ref, 1 - my_core(), 0, send0_ref)
-    column_part(c, x_ref, 1 - my_core(), 1, send1_ref)
+
+
+def mate_columns_kernel(c_ref, x_ref, send1_ref):
+    column_part(c_ref[...], x_ref, 1 - my_core(), 1, send1_ref)
 
 
 def probs_kernel(*refs, n):
     parts, refs = refs[:n], refs[n:]
-    labels_ref, weight_ref, x_ref, p_ref, e_ref, send0_ref, send1_ref, block_ref = refs
+    labels_ref, weight_ref, x_ref, p_ref, e_ref, send0_ref, block_ref = refs
     logits = add_up(parts)
     classes = logits.shape[0]
     top = jnp.max(logits, axis=0, keepdims=True)
@@ -130,7 +132,7 @@
         (sum_all(row_weight), sum_all(row_weight * (log_total - picked))), lax.axis_index("dp")
     )
     block_ref[...] = block
-    send_columns(e, x_ref, block, send0_ref, send1_ref)
+    send_columns(e, x_ref, block, send0_ref)
 
 
 def curvature(parts, s_prev, sc_prev, p_ref, scale_ref):
@@ -160,7 +162,7 @@
     s_prev, sc_prev = None, None
     if not first:
         (s_prev, sc_prev), refs = refs[:2], refs[2:]
-    p_ref, scale_ref, x_ref, s_ref, c_ref, send0_ref, send1_ref, block_ref, sc_ref = refs
+    p_ref, scale_ref, x_ref, s_ref, c_ref, send0_ref, block_ref, sc_ref = refs
     s, c, curv, res_norm, dir_norm, beta = curvature(parts, s_prev, sc_prev, p_ref, scale_ref)
     s_ref[...] = s
     c_ref[...] = c
@@ -170,7 +172,7 @@
     sc_ref[3:, :] = jnp.zeros((5, LANES), F32)
     block = scalar_block((curv,), lax.axis_index("dp"))
     block_ref[...] = block
-    send_columns(c, x_ref, block, send0_ref, send1_ref)
+    send_columns(c, x_ref, block, send0_ref)
 
 
 def own_columns_kernel(*refs, part):
@@ -400,10 +402,14 @@
     )
     pins = [x, xt, weight]
 
-    def column_sums(c, send0, send1, block):
-        received0, received1 = core_swap(send0), core_swap(send1)
+    def column_sums(c, send0, block):
+        received0 = core_swap(send0)
+        (send1,) = call(
+            mate_columns_kernel, "mate_columns", [((classes, size), BF16)], c, x, pins=pins
+        )
+        received1 = core_swap(send1)
         sums = []
-        for part, received, extra in ((0, received0, (block,)), (1, received1, ())):
+        for part, received, extra, after in ((0, received0, (block,), [send1]), (1, received1, (), [])):
             (own,) = call(
                 functools.partial(own_columns_kernel, part=part),
                 "own_columns",
@@ -411,7 +417,7 @@
                 c,
                 *extra,
                 x,
-                pins=pins,
+                pins=pins + after,
             )
             sums.append(across_chips(add(pins, own, received, kind=BF16), pins))
         return sums
@@ -441,12 +447,11 @@
     curv_outs = [
         ((classes, rows), BF16),
         ((classes, size + LANES), BF16),
-        ((classes, size), BF16),
         ((16, LANES), F32),
     ]
     aux_out = ((8, LANES), F32)
     parts = across_feat(logit_part, pins)
-    prob, e, send0, send1, block = call(
+    prob, e, send0, block = call(
         functools.partial(probs_kernel, n=len(parts)),
         "probs",
         [((classes, rows), F32)] + curv_outs,
@@ -456,7 +461,7 @@
         x,
         pins=pins,
     )
-    parts0, parts1 = column_sums(e, send0, send1, block)
+    parts0, parts1 = column_sums(e, send0, block)
     residual0, send0, aux, scale, loss = call(
         functools.partial(gradient0_kernel, n=len(parts0)),
         "gradient_0",
@@ -482,7 +487,7 @@
     state, steps, scores = (), [], []
     for i in range(CG_ITERS - 1):
         parts = row_sums(acc, received0, send1)
-        s, c, send0, send1, block, sc = call(
+        s, c, send0, block, sc = call(
             functools.partial(curv_kernel, n=len(parts), first=i == 0),
             "curvature",
             [((classes, rows), F32)] + curv_outs + [((8, LANES), F32)],
@@ -495,7 +500,7 @@
         )
         state = (s, sc)
         scores.append(s)
-        both = column_sums(c, send0, send1, block)
+        both = column_sums(c, send0, block)
         last = i == CG_ITERS - 2
         vectors = [((classes, size), F32)] * (0 if last else 2)
         send0, aux, *first_half = call(

time: 133 us -> 132 us (level)
  waiting for transfers between devices: 45.9 us -> 43.8 us
    ppermute x47, waiting for transfers between devices: 45.9 us -> 43.8 us  [swap(): return lax.ppermute(value, axis, [(i, i ^ bit) for i in range(size)])]
    pallas_call x48 -> x52, Pallas kernels: 43.3 us -> 43.6 us  [call(): pl.pallas_call(body, out_shape=tuple((out_space(shape, dtype) for shape,...]
  transfers between devices with their start and end apart: 47 -> 47, of which waited for: 38 -> 34; matrix products, arithmetic and copies ran while one was open for 0% -> 0% of each run, Pallas kernels for 15% -> 17%
where the time goes in v3:
time: 132 us
  starting transfers between devices  43.8 us (33%)
  waiting for transfers between devices  43.8 us (33%)
  Pallas kernels  43.6 us (33%)
    ppermute x47, starting transfers between devices, swap(): return lax.ppermute(value, axis, [(i, i ^ bit) for i in range(size)])  43.8 us
    ppermute x47, waiting for transfers between devices, swap(): return lax.ppermute(value, axis, [(i, i ^ bit) for i in range(size)])  43.8 us
    pallas_call x52, Pallas kernels, call(): pl.pallas_call(body, out_shape=tuple((out_space(shape, dtype) for shape,...  43.6 us
  transfers between devices with their start and end apart: 47, of which 34 were waited for; matrix products, arithmetic and copies ran while one was open for 0% of the time, Pallas kernels for 17%

profile of v3, /device:TPU:0, one launch (start us, length us, event | category | flops | bytes accessed | tf_op | source)
XLA Modules:
  0.0 132.3 jit_solution(12004547785198144410)
XLA Ops:
  0.6 10.2 %load.1 = (bf16[1536,8192]{1,0:T(8,128)(2,1)S(1)}, bf16[8192,1536]{1,0:T(8,128)(2,1)S(1)}, f32[16,8192]{1,0:T(8,128)S(1)}, f32[16,1536]{1,0:T(8,128)S(1)}) custom-call(bf16[1536,8192]{1,0:T(8,128)(2,1)} %refs_0_.1, f32[16,8192]{1,0:T(8,128)} %refs_1_.1), custom_call_target="tpu_custom_call" | custom-call | tf_op jit(solution)/shard_map/load/pallas_call | solution.py:335
  10.8 4.0 %collective-permute-start.2 = (f32[16,1536]{1,0:T(8,128)S(1)}, f32[16,1536]{1,0:T(8,128)S(1)}, u32[]{:S(2)}, u32[]{:S(2)}) collective-permute-start(f32[16,1536]{1,0:T(8,128)S(1)} %get-tuple-element.52.refs_0_), channel_id=1, source_target_pairs={{0,3},{1,2},{2,1},{3,0},{4,7},{5,6},{6,5},{7,4},{8,11},{9,10},{10,... | collective-permute-start | bytes 294920 | tf_op jit(solution)/shard_map/ppermute | solution.py:351
  15.5 2.5 %collective-permute-done.2.refs_3_ = f32[16,1536]{1,0:T(8,128)S(1)} collective-permute-done((f32[16,1536]{1,0:T(8,128)S(1)}, f32[16,1536]{1,0:T(8,128)S(1)}, u32[]{:S(2)}, u32[]{:S(2)}) %collective-permute-start.2) | collective-permute-done | bytes 98336 | tf_op jit(solution)/shard_map/ppermute | solution.py:351
  18.1 1.7 %collective-permute-done.1.refs_2_ = f32[16,1536]{1,0:T(8,128)S(1)} collective-permute-done((f32[16,1536]{1,0:T(8,128)S(1)}, f32[16,1536]{1,0:T(8,128)S(1)}, u32[]{:S(2)}, u32[]{:S(2)}) %collective-permute-start.1) | collective-permute-done | bytes 98336 | tf_op jit(solution)/shard_map/ppermute | solution.py:351
  20.0 2.7 %collective-permute-start.3 = (f32[16,1536]{1,0:T(8,128)S(1)}, f32[16,1536]{1,0:T(8,128)S(1)}, u32[]{:S(2)}, u32[]{:S(2)}) collective-permute-start(f32[16,1536]{1,0:T(8,128)S(1)} %add.13.refs_0_), channel_id=1, source_target_pairs={{0,4},{1,5},{2,6},{3,7},{4,0},{5,1},{6,2},{7,3},{8,12},{9,13},{10,... | collective-permute-start | bytes 294920 | tf_op jit(solution)/shard_map/ppermute | solution.py:351
  22.7 4.9 %collective-permute-done.3.refs_1_ = f32[16,1536]{1,0:T(8,128)S(1)} collective-permute-done((f32[16,1536]{1,0:T(8,128)S(1)}, f32[16,1536]{1,0:T(8,128)S(1)}, u32[]{:S(2)}, u32[]{:S(2)}) %collective-permute-start.3) | collective-permute-done | bytes 98336 | tf_op jit(solution)/shard_map/ppermute | solution.py:351
  38.0 1.7 %rows_1.4.refs_0_ = f32[16,1536]{1,0:T(8,128)S(1)} custom-call(f32[16,1536]{1,0:T(8,128)S(1)} %rows_0.4.refs_7_.refs_0_, bf16[16,2176]{1,0:T(8,128)(2,1)S(1)} %get-tuple-element.61.refs_1_, bf16[16,2048]{1,0:T(8,128)(2,1)S(1)} %collective-permute-done.8.refs_8_.refs_2_, ...), custom_call_target="tpu_custom_call" | custom-call | tf_op jit(solution)/shard_map/rows_1/pallas_call | solution.py:335
  42.5 1.7 %collective-permute-start.10 = (bf16[16,1664]{1,0:T(8,128)(2,1)S(1)}, bf16[16,1664]{1,0:T(8,128)(2,1)S(1)}, u32[]{:S(2)}, u32[]{:S(2)}) collective-permute-start(bf16[16,1664]{1,0:T(8,128)(2,1)S(1)} %rows_2.4.refs_0_), channel_id=1, source_target_pairs={{0,2},{1,3},{2,0},{3,1},{4,6},{5,7},{6,4},{7,5},{8,10},{9,11},{10,... | collective-permute-start | bytes 159752 | tf_op jit(solution)/shard_map/ppermute | solution.py:351
  44.2 2.0 %collective-permute-done.12.refs_3_ = bf16[16,1664]{1,0:T(8,128)(2,1)S(1)} collective-permute-done((bf16[16,1664]{1,0:T(8,128)(2,1)S(1)}, bf16[16,1664]{1,0:T(8,128)(2,1)S(1)}, u32[]{:S(2)}, u32[]{:S(2)}) %collective-permute-start.12) | collective-permute-done | bytes 53280 | tf_op jit(solution)/shard_map/ppermute | solution.py:351
  46.7 3.4 %collective-permute-start.13 = (bf16[16,1664]{1,0:T(8,128)(2,1)S(1)}, bf16[16,1664]{1,0:T(8,128)(2,1)S(1)}, u32[]{:S(2)}, u32[]{:S(2)}) collective-permute-start(bf16[16,1664]{1,0:T(8,128)(2,1)S(1)} %add.16.refs_0_), channel_id=1, source_target_pairs={{0,4},{1,5},{2,6},{3,7},{4,0},{5,1},{6,2},{7,3},{8,12},{9,13},{10,... | collective-permute-start | bytes 159752 | tf_op jit(solution)/shard_map/ppermute | solution.py:351
  50.1 2.1 %collective-permute-done.13.refs_1_ = bf16[16,1664]{1,0:T(8,128)(2,1)S(1)} collective-permute-done((bf16[16,1664]{1,0:T(8,128)(2,1)S(1)}, bf16[16,1664]{1,0:T(8,128)(2,1)S(1)}, u32[]{:S(2)}, u32[]{:S(2)}) %collective-permute-start.13) | collective-permute-done | bytes 53280 | tf_op jit(solution)/shard_map/ppermute | solution.py:351
  61.9 1.7 %rows_1.5.refs_0_ = f32[16,1536]{1,0:T(8,128)S(1)} custom-call(f32[16,1536]{1,0:T(8,128)S(1)} %rows_0.5.refs_9_.refs_0_, bf16[16,2176]{1,0:T(8,128)(2,1)S(1)} %get-tuple-element.72.refs_1_, bf16[16,2048]{1,0:T(8,128)(2,1)S(1)} %collective-permute-done.18.refs_10_.refs_2_, ...), custom_call_target="tpu_custom_call" | custom-call | tf_op jit(solution)/shard_map/rows_1/pallas_call | solution.py:335
  64.6 1.7 %collective-permute-start.22 = (bf16[16,1664]{1,0:T(8,128)(2,1)S(1)}, bf16[16,1664]{1,0:T(8,128)(2,1)S(1)}, u32[]{:S(2)}, u32[]{:S(2)}) collective-permute-start(bf16[16,1664]{1,0:T(8,128)(2,1)S(1)} %rows_2.5.refs_0_), channel_id=1, source_target_pairs={{0,3},{1,2},{2,1},{3,0},{4,7},{5,6},{6,5},{7,4},{8,11},{9,10},{10,... | collective-permute-start | bytes 159752 | tf_op jit(solution)/shard_map/ppermute | solution.py:351
  68.3 1.7 %collective-permute-done.22.refs_3_ = bf16[16,1664]{1,0:T(8,128)(2,1)S(1)} collective-permute-done((bf16[16,1664]{1,0:T(8,128)(2,1)S(1)}, bf16[16,1664]{1,0:T(8,128)(2,1)S(1)}, u32[]{:S(2)}, u32[]{:S(2)}) %collective-permute-start.22) | collective-permute-done | bytes 53280 | tf_op jit(solution)/shard_map/ppermute | solution.py:351
  71.6 1.8 %collective-permute-start.23 = (bf16[16,1664]{1,0:T(8,128)(2,1)S(1)}, bf16[16,1664]{1,0:T(8,128)(2,1)S(1)}, u32[]{:S(2)}, u32[]{:S(2)}) collective-permute-start(bf16[16,1664]{1,0:T(8,128)(2,1)S(1)} %add.19.refs_0_), channel_id=1, source_target_pairs={{0,4},{1,5},{2,6},{3,7},{4,0},{5,1},{6,2},{7,3},{8,12},{9,13},{10,... | collective-permute-start | bytes 159752 | tf_op jit(solution)/shard_map/ppermute | solution.py:351
  73.5 3.8 %collective-permute-done.23.refs_1_ = bf16[16,1664]{1,0:T(8,128)(2,1)S(1)} collective-permute-done((bf16[16,1664]{1,0:T(8,128)(2,1)S(1)}, bf16[16,1664]{1,0:T(8,128)(2,1)S(1)}, u32[]{:S(2)}, u32[]{:S(2)}) %collective-permute-start.23) | collective-permute-done | bytes 53280 | tf_op jit(solution)/shard_map/ppermute | solution.py:351
  87.6 1.7 %rows_1.6.refs_0_ = f32[16,1536]{1,0:T(8,128)S(1)} custom-call(f32[16,1536]{1,0:T(8,128)S(1)} %rows_0.6.refs_12_.refs_0_, bf16[16,2176]{1,0:T(8,128)(2,1)S(1)} %get-tuple-element.84.refs_1_, bf16[16,2048]{1,0:T(8,128)(2,1)S(1)} %collective-permute-done.28.refs_13_.refs_2_, ...), custom_call_target="tpu_custom_call" | custom-call | tf_op jit(solution)/shard_map/rows_1/pallas_call | solution.py:335
  92.1 1.7 %collective-permute-start.30 = (bf16[16,1664]{1,0:T(8,128)(2,1)S(1)}, bf16[16,1664]{1,0:T(8,128)(2,1)S(1)}, u32[]{:S(2)}, u32[]{:S(2)}) collective-permute-start(bf16[16,1664]{1,0:T(8,128)(2,1)S(1)} %rows_2.6.refs_0_), channel_id=1, source_target_pairs={{0,2},{1,3},{2,0},{3,1},{4,6},{5,7},{6,4},{7,5},{8,10},{9,11},{10,... | collective-permute-start | bytes 159752 | tf_op jit(solution)/shard_map/ppermute | solution.py:351
  93.8 2.0 %collective-permute-done.32.refs_3_ = bf16[16,1664]{1,0:T(8,128)(2,1)S(1)} collective-permute-done((bf16[16,1664]{1,0:T(8,128)(2,1)S(1)}, bf16[16,1664]{1,0:T(8,128)(2,1)S(1)}, u32[]{:S(2)}, u32[]{:S(2)}) %collective-permute-start.32) | collective-permute-done | bytes 53280 | tf_op jit(solution)/shard_map/ppermute | solution.py:351
  96.3 3.0 %collective-permute-start.33 = (bf16[16,1664]{1,0:T(8,128)(2,1)S(1)}, bf16[16,1664]{1,0:T(8,128)(2,1)S(1)}, u32[]{:S(2)}, u32[]{:S(2)}) collective-permute-start(bf16[16,1664]{1,0:T(8,128)(2,1)S(1)} %add.22.refs_0_), channel_id=1, source_target_pairs={{0,4},{1,5},{2,6},{3,7},{4,0},{5,1},{6,2},{7,3},{8,12},{9,13},{10,... | collective-permute-start | bytes 159752 | tf_op jit(solution)/shard_map/ppermute | solution.py:351
  99.3 2.1 %collective-permute-done.33.refs_1_ = bf16[16,1664]{1,0:T(8,128)(2,1)S(1)} collective-permute-done((bf16[16,1664]{1,0:T(8,128)(2,1)S(1)}, bf16[16,1664]{1,0:T(8,128)(2,1)S(1)}, u32[]{:S(2)}, u32[]{:S(2)}) %collective-permute-start.33) | collective-permute-done | bytes 53280 | tf_op jit(solution)/shard_map/ppermute | solution.py:351
  111.2 1.7 %rows_1.7.refs_0_ = f32[16,1536]{1,0:T(8,128)S(1)} custom-call(f32[16,1536]{1,0:T(8,128)S(1)} %rows_0.7.refs_12_.refs_0_, bf16[16,2176]{1,0:T(8,128)(2,1)S(1)} %update_1.5.refs_1_, bf16[16,2048]{1,0:T(8,128)(2,1)S(1)} %collective-permute-done.38.refs_13_.refs_2_, ...), custom_call_target="tpu_custom_call" | custom-call | tf_op jit(solution)/shard_map/rows_1/pallas_call | solution.py:335
  113.9 2.0 %collective-permute-start.42 = (bf16[16,1664]{1,0:T(8,128)(2,1)S(1)}, bf16[16,1664]{1,0:T(8,128)(2,1)S(1)}, u32[]{:S(2)}, u32[]{:S(2)}) collective-permute-start(bf16[16,1664]{1,0:T(8,128)(2,1)S(1)} %rows_2.7.refs_0_), channel_id=1, source_target_pairs={{0,3},{1,2},{2,1},{3,0},{4,7},{5,6},{6,5},{7,4},{8,11},{9,10},{10,... | collective-permute-start | bytes 159752 | tf_op jit(solution)/shard_map/ppermute | solution.py:351
  122.8 3.9 %collective-permute-done.43.refs_1_ = bf16[16,1664]{1,0:T(8,128)(2,1)S(1)} collective-permute-done((bf16[16,1664]{1,0:T(8,128)(2,1)S(1)}, bf16[16,1664]{1,0:T(8,128)(2,1)S(1)}, u32[]{:S(2)}, u32[]{:S(2)}) %collective-permute-start.43) | collective-permute-done | bytes 53280 | tf_op jit(solution)/shard_map/ppermute | solution.py:351
  (146 shorter events, 65.3 us)
Async XLA Ops:
  10.8 7.2 %collective-permute-start.2 = (f32[16,1536]{1,0:T(8,128)S(1)}, f32[16,1536]{1,0:T(8,128)S(1)}, u32[]{:S(2)}, u32[]{:S(2)}) collective-permute-start(f32[16,1536]{1,0:T(8,128)S(1)} %get-tuple-element.52.refs_0_), channel_id=1, source_target_pairs={{0,3},{1,2},{2,1},{3,0},{4,7},{5,6},{6,5},{7,4},{8,11},{9,10},{10,... | collective-permute-start | bytes 294920 | tf_op jit(solution)/shard_map/ppermute | solution.py:351
  14.9 4.9 %collective-permute-start.1 = (f32[16,1536]{1,0:T(8,128)S(1)}, f32[16,1536]{1,0:T(8,128)S(1)}, u32[]{:S(2)}, u32[]{:S(2)}) collective-permute-start(f32[16,1536]{1,0:T(8,128)S(1)} %get-tuple-element.52.refs_0_), channel_id=1, source_target_pairs={{0,1},{1,0},{2,3},{3,2},{4,5},{5,4},{6,7},{7,6},{8,9},{9,8},{10,11... | collective-permute-start | bytes 294920 | tf_op jit(solution)/shard_map/ppermute | solution.py:351
  15.4 4.6 %collective-permute-start = (f32[16,1536]{1,0:T(8,128)S(1)}, f32[16,1536]{1,0:T(8,128)S(1)}, u32[]{:S(2)}, u32[]{:S(2)}) collective-permute-start(f32[16,1536]{1,0:T(8,128)S(1)} %get-tuple-element.52.refs_0_), channel_id=1, source_target_pairs={{0,2},{1,3},{2,0},{3,1},{4,6},{5,7},{6,4},{7,5},{8,10},{9,11},{10,... | collective-permute-start | bytes 294920 | tf_op jit(solution)/shard_map/ppermute | solution.py:351
  20.0 7.5 %collective-permute-start.3 = (f32[16,1536]{1,0:T(8,128)S(1)}, f32[16,1536]{1,0:T(8,128)S(1)}, u32[]{:S(2)}, u32[]{:S(2)}) collective-permute-start(f32[16,1536]{1,0:T(8,128)S(1)} %add.13.refs_0_), channel_id=1, source_target_pairs={{0,4},{1,5},{2,6},{3,7},{4,0},{5,1},{6,2},{7,3},{8,12},{9,13},{10,... | collective-permute-start | bytes 294920 | tf_op jit(solution)/shard_map/ppermute | solution.py:351
  30.5 4.6 %collective-permute-start.5 = (bf16[16,2176]{1,0:T(8,128)(2,1)S(1)}, bf16[16,2176]{1,0:T(8,128)(2,1)S(1)}, u32[]{:S(2)}, u32[]{:S(2)}) collective-permute-start(bf16[16,2176]{1,0:T(8,128)(2,1)S(1)} %add.14.refs_0_), channel_id=1, source_target_pairs={{0,16},{8,24},{16,0},{24,8},{1,17},{9,25},{17,1},{25,9},{2,18},{10... | collective-permute-start | bytes 208904 | tf_op jit(solution)/shard_map/ppermute | solution.py:351
  33.3 4.3 %collective-permute-start.7 = (bf16[16,2048]{1,0:T(8,128)(2,1)S(1)}, bf16[16,2048]{1,0:T(8,128)(2,1)S(1)}, u32[]{:S(2)}, u32[]{:S(2)}) collective-permute-start(bf16[16,2048]{1,0:T(8,128)(2,1)S(1)} %add.15.refs_0_), channel_id=1, source_target_pairs={{0,16},{8,24},{16,0},{24,8},{1,17},{9,25},{17,1},{25,9},{2,18},{10... | collective-permute-start | bytes 196616 | tf_op jit(solution)/shard_map/ppermute | solution.py:351
  40.7 5.5 %collective-permute-start.12 = (bf16[16,1664]{1,0:T(8,128)(2,1)S(1)}, bf16[16,1664]{1,0:T(8,128)(2,1)S(1)}, u32[]{:S(2)}, u32[]{:S(2)}) collective-permute-start(bf16[16,1664]{1,0:T(8,128)(2,1)S(1)} %rows_2.4.refs_0_), channel_id=1, source_target_pairs={{0,3},{1,2},{2,1},{3,0},{4,7},{5,6},{6,5},{7,4},{8,11},{9,10},{10,... | collective-permute-start | bytes 159752 | tf_op jit(solution)/shard_map/ppermute | solution.py:351
  41.2 5.1 %collective-permute-start.11 = (bf16[16,1664]{1,0:T(8,128)(2,1)S(1)}, bf16[16,1664]{1,0:T(8,128)(2,1)S(1)}, u32[]{:S(2)}, u32[]{:S(2)}) collective-permute-start(bf16[16,1664]{1,0:T(8,128)(2,1)S(1)} %rows_2.4.refs_0_), channel_id=1, source_target_pairs={{0,1},{1,0},{2,3},{3,2},{4,5},{5,4},{6,7},{7,6},{8,9},{9,8},{10,11... | collective-permute-start | bytes 159752 | tf_op jit(solution)/shard_map/ppermute | solution.py:351
  46.7 5.6 %collective-permute-start.13 = (bf16[16,1664]{1,0:T(8,128)(2,1)S(1)}, bf16[16,1664]{1,0:T(8,128)(2,1)S(1)}, u32[]{:S(2)}, u32[]{:S(2)}) collective-permute-start(bf16[16,1664]{1,0:T(8,128)(2,1)S(1)} %add.16.refs_0_), channel_id=1, source_target_pairs={{0,4},{1,5},{2,6},{3,7},{4,0},{5,1},{6,2},{7,3},{8,12},{9,13},{10,... | collective-permute-start | bytes 159752 | tf_op jit(solution)/shard_map/ppermute | solution.py:351
  55.1 4.6 %collective-permute-start.15 = (bf16[16,2176]{1,0:T(8,128)(2,1)S(1)}, bf16[16,2176]{1,0:T(8,128)(2,1)S(1)}, u32[]{:S(2)}, u32[]{:S(2)}) collective-permute-start(bf16[16,2176]{1,0:T(8,128)(2,1)S(1)} %add.17.refs_0_), channel_id=1, source_target_pairs={{0,16},{8,24},{16,0},{24,8},{1,17},{9,25},{17,1},{25,9},{2,18},{10... | collective-permute-start | bytes 208904 | tf_op jit(solution)/shard_map/ppermute | solution.py:351
  57.2 4.3 %collective-permute-start.17 = (bf16[16,2048]{1,0:T(8,128)(2,1)S(1)}, bf16[16,2048]{1,0:T(8,128)(2,1)S(1)}, u32[]{:S(2)}, u32[]{:S(2)}) collective-permute-start(bf16[16,2048]{1,0:T(8,128)(2,1)S(1)} %add.18.refs_0_), channel_id=1, source_target_pairs={{0,16},{8,24},{16,0},{24,8},{1,17},{9,25},{17,1},{25,9},{2,18},{10... | collective-permute-start | bytes 196616 | tf_op jit(solution)/shard_map/ppermute | solution.py:351
  64.6 5.3 %collective-permute-start.22 = (bf16[16,1664]{1,0:T(8,128)(2,1)S(1)}, bf16[16,1664]{1,0:T(8,128)(2,1)S(1)}, u32[]{:S(2)}, u32[]{:S(2)}) collective-permute-start(bf16[16,1664]{1,0:T(8,128)(2,1)S(1)} %rows_2.5.refs_0_), channel_id=1, source_target_pairs={{0,3},{1,2},{2,1},{3,0},{4,7},{5,6},{6,5},{7,4},{8,11},{9,10},{10,... | collective-permute-start | bytes 159752 | tf_op jit(solution)/shard_map/ppermute | solution.py:351
  66.3 4.7 %collective-permute-start.21 = (bf16[16,1664]{1,0:T(8,128)(2,1)S(1)}, bf16[16,1664]{1,0:T(8,128)(2,1)S(1)}, u32[]{:S(2)}, u32[]{:S(2)}) collective-permute-start(bf16[16,1664]{1,0:T(8,128)(2,1)S(1)} %rows_2.5.refs_0_), channel_id=1, source_target_pairs={{0,1},{1,0},{2,3},{3,2},{4,5},{5,4},{6,7},{7,6},{8,9},{9,8},{10,11... | collective-permute-start | bytes 159752 | tf_op jit(solution)/shard_map/ppermute | solution.py:351
  71.6 5.7 %collective-permute-start.23 = (bf16[16,1664]{1,0:T(8,128)(2,1)S(1)}, bf16[16,1664]{1,0:T(8,128)(2,1)S(1)}, u32[]{:S(2)}, u32[]{:S(2)}) collective-permute-start(bf16[16,1664]{1,0:T(8,128)(2,1)S(1)} %add.19.refs_0_), channel_id=1, source_target_pairs={{0,4},{1,5},{2,6},{3,7},{4,0},{5,1},{6,2},{7,3},{8,12},{9,13},{10,... | collective-permute-start | bytes 159752 | tf_op jit(solution)/shard_map/ppermute | solution.py:351
  80.3 4.7 %collective-permute-start.25 = (bf16[16,2176]{1,0:T(8,128)(2,1)S(1)}, bf16[16,2176]{1,0:T(8,128)(2,1)S(1)}, u32[]{:S(2)}, u32[]{:S(2)}) collective-permute-start(bf16[16,2176]{1,0:T(8,128)(2,1)S(1)} %add.20.refs_0_), channel_id=1, source_target_pairs={{0,16},{8,24},{16,0},{24,8},{1,17},{9,25},{17,1},{25,9},{2,18},{10... | collective-permute-start | bytes 208904 | tf_op jit(solution)/shard_map/ppermute | solution.py:351
  82.9 4.3 %collective-permute-start.27 = (bf16[16,2048]{1,0:T(8,128)(2,1)S(1)}, bf16[16,2048]{1,0:T(8,128)(2,1)S(1)}, u32[]{:S(2)}, u32[]{:S(2)}) collective-permute-start(bf16[16,2048]{1,0:T(8,128)(2,1)S(1)} %add.21.refs_0_), channel_id=1, source_target_pairs={{0,16},{8,24},{16,0},{24,8},{1,17},{9,25},{17,1},{25,9},{2,18},{10... | collective-permute-start | bytes 196616 | tf_op jit(solution)/shard_map/ppermute | solution.py:351
  90.3 5.5 %collective-permute-start.32 = (bf16[16,1664]{1,0:T(8,128)(2,1)S(1)}, bf16[16,1664]{1,0:T(8,128)(2,1)S(1)}, u32[]{:S(2)}, u32[]{:S(2)}) collective-permute-start(bf16[16,1664]{1,0:T(8,128)(2,1)S(1)} %rows_2.6.refs_0_), channel_id=1, source_target_pairs={{0,3},{1,2},{2,1},{3,0},{4,7},{5,6},{6,5},{7,4},{8,11},{9,10},{10,... | collective-permute-start | bytes 159752 | tf_op jit(solution)/shard_map/ppermute | solution.py:351
  90.8 5.1 %collective-permute-start.31 = (bf16[16,1664]{1,0:T(8,128)(2,1)S(1)}, bf16[16,1664]{1,0:T(8,128)(2,1)S(1)}, u32[]{:S(2)}, u32[]{:S(2)}) collective-permute-start(bf16[16,1664]{1,0:T(8,128)(2,1)S(1)} %rows_2.6.refs_0_), channel_id=1, source_target_pairs={{0,1},{1,0},{2,3},{3,2},{4,5},{5,4},{6,7},{7,6},{8,9},{9,8},{10,11... | collective-permute-start | bytes 159752 | tf_op jit(solution)/shard_map/ppermute | solution.py:351
  96.3 5.1 %collective-permute-start.33 = (bf16[16,1664]{1,0:T(8,128)(2,1)S(1)}, bf16[16,1664]{1,0:T(8,128)(2,1)S(1)}, u32[]{:S(2)}, u32[]{:S(2)}) collective-permute-start(bf16[16,1664]{1,0:T(8,128)(2,1)S(1)} %add.22.refs_0_), channel_id=1, source_target_pairs={{0,4},{1,5},{2,6},{3,7},{4,0},{5,1},{6,2},{7,3},{8,12},{9,13},{10,... | collective-permute-start | bytes 159752 | tf_op jit(solution)/shard_map/ppermute | solution.py:351
  104.4 4.7 %collective-permute-start.35 = (bf16[16,2176]{1,0:T(8,128)(2,1)S(1)}, bf16[16,2176]{1,0:T(8,128)(2,1)S(1)}, u32[]{:S(2)}, u32[]{:S(2)}) collective-permute-start(bf16[16,2176]{1,0:T(8,128)(2,1)S(1)} %add.23.refs_0_), channel_id=1, source_target_pairs={{0,16},{8,24},{16,0},{24,8},{1,17},{9,25},{17,1},{25,9},{2,18},{10... | collective-permute-start | bytes 208904 | tf_op jit(solution)/shard_map/ppermute | solution.py:351
  106.6 4.3 %collective-permute-start.37 = (bf16[16,2048]{1,0:T(8,128)(2,1)S(1)}, bf16[16,2048]{1,0:T(8,128)(2,1)S(1)}, u32[]{:S(2)}, u32[]{:S(2)}) collective-permute-start(bf16[16,2048]{1,0:T(8,128)(2,1)S(1)} %add.24.refs_0_), channel_id=1, source_target_pairs={{0,16},{8,24},{16,0},{24,8},{1,17},{9,25},{17,1},{25,9},{2,18},{10... | collective-permute-start | bytes 196616 | tf_op jit(solution)/shard_map/ppermute | solution.py:351
  113.9 5.1 %collective-permute-start.42 = (bf16[16,1664]{1,0:T(8,128)(2,1)S(1)}, bf16[16,1664]{1,0:T(8,128)(2,1)S(1)}, u32[]{:S(2)}, u32[]{:S(2)}) collective-permute-start(bf16[16,1664]{1,0:T(8,128)(2,1)S(1)} %rows_2.7.refs_0_), channel_id=1, source_target_pairs={{0,3},{1,2},{2,1},{3,0},{4,7},{5,6},{6,5},{7,4},{8,11},{9,10},{10,... | collective-permute-start | bytes 159752 | tf_op jit(solution)/shard_map/ppermute | solution.py:351
  115.9 4.3 %collective-permute-start.41 = (bf16[16,1664]{1,0:T(8,128)(2,1)S(1)}, bf16[16,1664]{1,0:T(8,128)(2,1)S(1)}, u32[]{:S(2)}, u32[]{:S(2)}) collective-permute-start(bf16[16,1664]{1,0:T(8,128)(2,1)S(1)} %rows_2.7.refs_0_), channel_id=1, source_target_pairs={{0,1},{1,0},{2,3},{3,2},{4,5},{5,4},{6,7},{7,6},{8,9},{9,8},{10,11... | collective-permute-start | bytes 159752 | tf_op jit(solution)/shard_map/ppermute | solution.py:351
  121.2 5.5 %collective-permute-start.43 = (bf16[16,1664]{1,0:T(8,128)(2,1)S(1)}, bf16[16,1664]{1,0:T(8,128)(2,1)S(1)}, u32[]{:S(2)}, u32[]{:S(2)}) collective-permute-start(bf16[16,1664]{1,0:T(8,128)(2,1)S(1)} %add.25.refs_0_), channel_id=1, source_target_pairs={{0,4},{1,5},{2,6},{3,7},{4,0},{5,1},{6,2},{7,3},{8,12},{9,13},{10,... | collective-permute-start | bytes 159752 | tf_op jit(solution)/shard_map/ppermute | solution.py:351
  (35 other events, 225.0 us)

commit v4 on v3

--- a/solution.py
+++ b/solution.py
@@ -62,7 +62,7 @@
 def load_kernel(x_hbm, w_hbm, x_ref, xt_ref, w_ref, l_ref, sems, w_sem, *, step, ahead):
     rows, columns = x_ref.shape
     chunks = rows // step
-    block = math.gcd(columns, 512)
+    block = math.gcd(columns, 1024)
 
     def rows_of(i):
         return pl.ds(pl.multiple_of(i * step, step), step)

time: 132 us -> 132 us (level)
  no operation moved by 1% of the time
where the time goes in v4:
time: 132 us
  starting transfers between devices  43.8 us (33%)
  waiting for transfers between devices  43.8 us (33%)
  Pallas kernels  43.6 us (33%)
    ppermute x47, starting transfers between devices, swap(): return lax.ppermute(value, axis, [(i, i ^ bit) for i in range(size)])  43.8 us
    ppermute x47, waiting for transfers between devices, swap(): return lax.ppermute(value, axis, [(i, i ^ bit) for i in range(size)])  43.8 us
    pallas_call x52, Pallas kernels, call(): pl.pallas_call(body, out_shape=tuple((out_space(shape, dtype) for shape,...  43.6 us
  transfers between devices with their start and end apart: 47, of which 34 were waited for; matrix products, arithmetic and copies ran while one was open for 0% of the time, Pallas kernels for 17%

profile of v4, /device:TPU:0, one launch (start us, length us, event | category | flops | bytes accessed | tf_op | source)
XLA Modules:
  0.0 132.3 jit_solution(3395523863746687293)
XLA Ops:
  0.6 10.2 %load.1 = (bf16[1536,8192]{1,0:T(8,128)(2,1)S(1)}, bf16[8192,1536]{1,0:T(8,128)(2,1)S(1)}, f32[16,8192]{1,0:T(8,128)S(1)}, f32[16,1536]{1,0:T(8,128)S(1)}) custom-call(bf16[1536,8192]{1,0:T(8,128)(2,1)} %refs_0_.1, f32[16,8192]{1,0:T(8,128)} %refs_1_.1), custom_call_target="tpu_custom_call" | custom-call | tf_op jit(solution)/shard_map/load/pallas_call | solution.py:335
  10.8 4.0 %collective-permute-start.2 = (f32[16,1536]{1,0:T(8,128)S(1)}, f32[16,1536]{1,0:T(8,128)S(1)}, u32[]{:S(2)}, u32[]{:S(2)}) collective-permute-start(f32[16,1536]{1,0:T(8,128)S(1)} %get-tuple-element.52.refs_0_), channel_id=1, source_target_pairs={{0,3},{1,2},{2,1},{3,0},{4,7},{5,6},{6,5},{7,4},{8,11},{9,10},{10,... | collective-permute-start | bytes 294920 | tf_op jit(solution)/shard_map/ppermute | solution.py:351
  15.5 2.5 %collective-permute-done.2.refs_3_ = f32[16,1536]{1,0:T(8,128)S(1)} collective-permute-done((f32[16,1536]{1,0:T(8,128)S(1)}, f32[16,1536]{1,0:T(8,128)S(1)}, u32[]{:S(2)}, u32[]{:S(2)}) %collective-permute-start.2) | collective-permute-done | bytes 98336 | tf_op jit(solution)/shard_map/ppermute | solution.py:351
  18.1 1.7 %collective-permute-done.1.refs_2_ = f32[16,1536]{1,0:T(8,128)S(1)} collective-permute-done((f32[16,1536]{1,0:T(8,128)S(1)}, f32[16,1536]{1,0:T(8,128)S(1)}, u32[]{:S(2)}, u32[]{:S(2)}) %collective-permute-start.1) | collective-permute-done | bytes 98336 | tf_op jit(solution)/shard_map/ppermute | solution.py:351
  20.0 2.7 %collective-permute-start.3 = (f32[16,1536]{1,0:T(8,128)S(1)}, f32[16,1536]{1,0:T(8,128)S(1)}, u32[]{:S(2)}, u32[]{:S(2)}) collective-permute-start(f32[16,1536]{1,0:T(8,128)S(1)} %add.13.refs_0_), channel_id=1, source_target_pairs={{0,4},{1,5},{2,6},{3,7},{4,0},{5,1},{6,2},{7,3},{8,12},{9,13},{10,... | collective-permute-start | bytes 294920 | tf_op jit(solution)/shard_map/ppermute | solution.py:351
  22.7 4.9 %collective-permute-done.3.refs_1_ = f32[16,1536]{1,0:T(8,128)S(1)} collective-permute-done((f32[16,1536]{1,0:T(8,128)S(1)}, f32[16,1536]{1,0:T(8,128)S(1)}, u32[]{:S(2)}, u32[]{:S(2)}) %collective-permute-start.3) | collective-permute-done | bytes 98336 | tf_op jit(solution)/shard_map/ppermute | solution.py:351
  38.0 1.7 %rows_1.4.refs_0_ = f32[16,1536]{1,0:T(8,128)S(1)} custom-call(f32[16,1536]{1,0:T(8,128)S(1)} %rows_0.4.refs_7_.refs_0_, bf16[16,2176]{1,0:T(8,128)(2,1)S(1)} %get-tuple-element.61.refs_1_, bf16[16,2048]{1,0:T(8,128)(2,1)S(1)} %collective-permute-done.8.refs_8_.refs_2_, ...), custom_call_target="tpu_custom_call" | custom-call | tf_op jit(solution)/shard_map/rows_1/pallas_call | solution.py:335
  42.5 1.7 %collective-permute-start.10 = (bf16[16,1664]{1,0:T(8,128)(2,1)S(1)}, bf16[16,1664]{1,0:T(8,128)(2,1)S(1)}, u32[]{:S(2)}, u32[]{:S(2)}) collective-permute-start(bf16[16,1664]{1,0:T(8,128)(2,1)S(1)} %rows_2.4.refs_0_), channel_id=1, source_target_pairs={{0,2},{1,3},{2,0},{3,1},{4,6},{5,7},{6,4},{7,5},{8,10},{9,11},{10,... | collective-permute-start | bytes 159752 | tf_op jit(solution)/shard_map/ppermute | solution.py:351
  44.2 2.0 %collective-permute-done.12.refs_3_ = bf16[16,1664]{1,0:T(8,128)(2,1)S(1)} collective-permute-done((bf16[16,1664]{1,0:T(8,128)(2,1)S(1)}, bf16[16,1664]{1,0:T(8,128)(2,1)S(1)}, u32[]{:S(2)}, u32[]{:S(2)}) %collective-permute-start.12) | collective-permute-done | bytes 53280 | tf_op jit(solution)/shard_map/ppermute | solution.py:351
  46.7 3.4 %collective-permute-start.13 = (bf16[16,1664]{1,0:T(8,128)(2,1)S(1)}, bf16[16,1664]{1,0:T(8,128)(2,1)S(1)}, u32[]{:S(2)}, u32[]{:S(2)}) collective-permute-start(bf16[16,1664]{1,0:T(8,128)(2,1)S(1)} %add.16.refs_0_), channel_id=1, source_target_pairs={{0,4},{1,5},{2,6},{3,7},{4,0},{5,1},{6,2},{7,3},{8,12},{9,13},{10,... | collective-permute-start | bytes 159752 | tf_op jit(solution)/shard_map/ppermute | solution.py:351
  50.1 2.1 %collective-permute-done.13.refs_1_ = bf16[16,1664]{1,0:T(8,128)(2,1)S(1)} collective-permute-done((bf16[16,1664]{1,0:T(8,128)(2,1)S(1)}, bf16[16,1664]{1,0:T(8,128)(2,1)S(1)}, u32[]{:S(2)}, u32[]{:S(2)}) %collective-permute-start.13) | collective-permute-done | bytes 53280 | tf_op jit(solution)/shard_map/ppermute | solution.py:351
  61.9 1.7 %rows_1.5.refs_0_ = f32[16,1536]{1,0:T(8,128)S(1)} custom-call(f32[16,1536]{1,0:T(8,128)S(1)} %rows_0.5.refs_9_.refs_0_, bf16[16,2176]{1,0:T(8,128)(2,1)S(1)} %get-tuple-element.72.refs_1_, bf16[16,2048]{1,0:T(8,128)(2,1)S(1)} %collective-permute-done.18.refs_10_.refs_2_, ...), custom_call_target="tpu_custom_call" | custom-call | tf_op jit(solution)/shard_map/rows_1/pallas_call | solution.py:335
  64.6 1.7 %collective-permute-start.22 = (bf16[16,1664]{1,0:T(8,128)(2,1)S(1)}, bf16[16,1664]{1,0:T(8,128)(2,1)S(1)}, u32[]{:S(2)}, u32[]{:S(2)}) collective-permute-start(bf16[16,1664]{1,0:T(8,128)(2,1)S(1)} %rows_2.5.refs_0_), channel_id=1, source_target_pairs={{0,3},{1,2},{2,1},{3,0},{4,7},{5,6},{6,5},{7,4},{8,11},{9,10},{10,... | collective-permute-start | bytes 159752 | tf_op jit(solution)/shard_map/ppermute | solution.py:351
  68.3 1.7 %collective-permute-done.22.refs_3_ = bf16[16,1664]{1,0:T(8,128)(2,1)S(1)} collective-permute-done((bf16[16,1664]{1,0:T(8,128)(2,1)S(1)}, bf16[16,1664]{1,0:T(8,128)(2,1)S(1)}, u32[]{:S(2)}, u32[]{:S(2)}) %collective-permute-start.22) | collective-permute-done | bytes 53280 | tf_op jit(solution)/shard_map/ppermute | solution.py:351
  71.6 1.8 %collective-permute-start.23 = (bf16[16,1664]{1,0:T(8,128)(2,1)S(1)}, bf16[16,1664]{1,0:T(8,128)(2,1)S(1)}, u32[]{:S(2)}, u32[]{:S(2)}) collective-permute-start(bf16[16,1664]{1,0:T(8,128)(2,1)S(1)} %add.19.refs_0_), channel_id=1, source_target_pairs={{0,4},{1,5},{2,6},{3,7},{4,0},{5,1},{6,2},{7,3},{8,12},{9,13},{10,... | collective-permute-start | bytes 159752 | tf_op jit(solution)/shard_map/ppermute | solution.py:351
  73.5 3.8 %collective-permute-done.23.refs_1_ = bf16[16,1664]{1,0:T(8,128)(2,1)S(1)} collective-permute-done((bf16[16,1664]{1,0:T(8,128)(2,1)S(1)}, bf16[16,1664]{1,0:T(8,128)(2,1)S(1)}, u32[]{:S(2)}, u32[]{:S(2)}) %collective-permute-start.23) | collective-permute-done | bytes 53280 | tf_op jit(solution)/shard_map/ppermute | solution.py:351
  87.6 1.7 %rows_1.6.refs_0_ = f32[16,1536]{1,0:T(8,128)S(1)} custom-call(f32[16,1536]{1,0:T(8,128)S(1)} %rows_0.6.refs_12_.refs_0_, bf16[16,2176]{1,0:T(8,128)(2,1)S(1)} %get-tuple-element.84.refs_1_, bf16[16,2048]{1,0:T(8,128)(2,1)S(1)} %collective-permute-done.28.refs_13_.refs_2_, ...), custom_call_target="tpu_custom_call" | custom-call | tf_op jit(solution)/shard_map/rows_1/pallas_call | solution.py:335
  92.1 1.7 %collective-permute-start.30 = (bf16[16,1664]{1,0:T(8,128)(2,1)S(1)}, bf16[16,1664]{1,0:T(8,128)(2,1)S(1)}, u32[]{:S(2)}, u32[]{:S(2)}) collective-permute-start(bf16[16,1664]{1,0:T(8,128)(2,1)S(1)} %rows_2.6.refs_0_), channel_id=1, source_target_pairs={{0,2},{1,3},{2,0},{3,1},{4,6},{5,7},{6,4},{7,5},{8,10},{9,11},{10,... | collective-permute-start | bytes 159752 | tf_op jit(solution)/shard_map/ppermute | solution.py:351
  93.8 2.0 %collective-permute-done.32.refs_3_ = bf16[16,1664]{1,0:T(8,128)(2,1)S(1)} collective-permute-done((bf16[16,1664]{1,0:T(8,128)(2,1)S(1)}, bf16[16,1664]{1,0:T(8,128)(2,1)S(1)}, u32[]{:S(2)}, u32[]{:S(2)}) %collective-permute-start.32) | collective-permute-done | bytes 53280 | tf_op jit(solution)/shard_map/ppermute | solution.py:351
  96.3 3.0 %collective-permute-start.33 = (bf16[16,1664]{1,0:T(8,128)(2,1)S(1)}, bf16[16,1664]{1,0:T(8,128)(2,1)S(1)}, u32[]{:S(2)}, u32[]{:S(2)}) collective-permute-start(bf16[16,1664]{1,0:T(8,128)(2,1)S(1)} %add.22.refs_0_), channel_id=1, source_target_pairs={{0,4},{1,5},{2,6},{3,7},{4,0},{5,1},{6,2},{7,3},{8,12},{9,13},{10,... | collective-permute-start | bytes 159752 | tf_op jit(solution)/shard_map/ppermute | solution.py:351
  99.3 2.1 %collective-permute-done.33.refs_1_ = bf16[16,1664]{1,0:T(8,128)(2,1)S(1)} collective-permute-done((bf16[16,1664]{1,0:T(8,128)(2,1)S(1)}, bf16[16,1664]{1,0:T(8,128)(2,1)S(1)}, u32[]{:S(2)}, u32[]{:S(2)}) %collective-permute-start.33) | collective-permute-done | bytes 53280 | tf_op jit(solution)/shard_map/ppermute | solution.py:351
  111.2 1.7 %rows_1.7.refs_0_ = f32[16,1536]{1,0:T(8,128)S(1)} custom-call(f32[16,1536]{1,0:T(8,128)S(1)} %rows_0.7.refs_12_.refs_0_, bf16[16,2176]{1,0:T(8,128)(2,1)S(1)} %update_1.5.refs_1_, bf16[16,2048]{1,0:T(8,128)(2,1)S(1)} %collective-permute-done.38.refs_13_.refs_2_, ...), custom_call_target="tpu_custom_call" | custom-call | tf_op jit(solution)/shard_map/rows_1/pallas_call | solution.py:335
  113.9 2.0 %collective-permute-start.42 = (bf16[16,1664]{1,0:T(8,128)(2,1)S(1)}, bf16[16,1664]{1,0:T(8,128)(2,1)S(1)}, u32[]{:S(2)}, u32[]{:S(2)}) collective-permute-start(bf16[16,1664]{1,0:T(8,128)(2,1)S(1)} %rows_2.7.refs_0_), channel_id=1, source_target_pairs={{0,3},{1,2},{2,1},{3,0},{4,7},{5,6},{6,5},{7,4},{8,11},{9,10},{10,... | collective-permute-start | bytes 159752 | tf_op jit(solution)/shard_map/ppermute | solution.py:351
  122.8 3.9 %collective-permute-done.43.refs_1_ = bf16[16,1664]{1,0:T(8,128)(2,1)S(1)} collective-permute-done((bf16[16,1664]{1,0:T(8,128)(2,1)S(1)}, bf16[16,1664]{1,0:T(8,128)(2,1)S(1)}, u32[]{:S(2)}, u32[]{:S(2)}) %collective-permute-start.43) | collective-permute-done | bytes 53280 | tf_op jit(solution)/shard_map/ppermute | solution.py:351
  (146 shorter events, 65.3 us)
Async XLA Ops:
  10.8 7.2 %collective-permute-start.2 = (f32[16,1536]{1,0:T(8,128)S(1)}, f32[16,1536]{1,0:T(8,128)S(1)}, u32[]{:S(2)}, u32[]{:S(2)}) collective-permute-start(f32[16,1536]{1,0:T(8,128)S(1)} %get-tuple-element.52.refs_0_), channel_id=1, source_target_pairs={{0,3},{1,2},{2,1},{3,0},{4,7},{5,6},{6,5},{7,4},{8,11},{9,10},{10,... | collective-permute-start | bytes 294920 | tf_op jit(solution)/shard_map/ppermute | solution.py:351
  14.9 4.9 %collective-permute-start.1 = (f32[16,1536]{1,0:T(8,128)S(1)}, f32[16,1536]{1,0:T(8,128)S(1)}, u32[]{:S(2)}, u32[]{:S(2)}) collective-permute-start(f32[16,1536]{1,0:T(8,128)S(1)} %get-tuple-element.52.refs_0_), channel_id=1, source_target_pairs={{0,1},{1,0},{2,3},{3,2},{4,5},{5,4},{6,7},{7,6},{8,9},{9,8},{10,11... | collective-permute-start | bytes 294920 | tf_op jit(solution)/shard_map/ppermute | solution.py:351
  15.4 4.6 %collective-permute-start = (f32[16,1536]{1,0:T(8,128)S(1)}, f32[16,1536]{1,0:T(8,128)S(1)}, u32[]{:S(2)}, u32[]{:S(2)}) collective-permute-start(f32[16,1536]{1,0:T(8,128)S(1)} %get-tuple-element.52.refs_0_), channel_id=1, source_target_pairs={{0,2},{1,3},{2,0},{3,1},{4,6},{5,7},{6,4},{7,5},{8,10},{9,11},{10,... | collective-permute-start | bytes 294920 | tf_op jit(solution)/shard_map/ppermute | solution.py:351
  20.0 7.5 %collective-permute-start.3 = (f32[16,1536]{1,0:T(8,128)S(1)}, f32[16,1536]{1,0:T(8,128)S(1)}, u32[]{:S(2)}, u32[]{:S(2)}) collective-permute-start(f32[16,1536]{1,0:T(8,128)S(1)} %add.13.refs_0_), channel_id=1, source_target_pairs={{0,4},{1,5},{2,6},{3,7},{4,0},{5,1},{6,2},{7,3},{8,12},{9,13},{10,... | collective-permute-start | bytes 294920 | tf_op jit(solution)/shard_map/ppermute | solution.py:351
  30.5 4.6 %collective-permute-start.5 = (bf16[16,2176]{1,0:T(8,128)(2,1)S(1)}, bf16[16,2176]{1,0:T(8,128)(2,1)S(1)}, u32[]{:S(2)}, u32[]{:S(2)}) collective-permute-start(bf16[16,2176]{1,0:T(8,128)(2,1)S(1)} %add.14.refs_0_), channel_id=1, source_target_pairs={{0,16},{8,24},{16,0},{24,8},{1,17},{9,25},{17,1},{25,9},{2,18},{10... | collective-permute-start | bytes 208904 | tf_op jit(solution)/shard_map/ppermute | solution.py:351
  33.3 4.3 %collective-permute-start.7 = (bf16[16,2048]{1,0:T(8,128)(2,1)S(1)}, bf16[16,2048]{1,0:T(8,128)(2,1)S(1)}, u32[]{:S(2)}, u32[]{:S(2)}) collective-permute-start(bf16[16,2048]{1,0:T(8,128)(2,1)S(1)} %add.15.refs_0_), channel_id=1, source_target_pairs={{0,16},{8,24},{16,0},{24,8},{1,17},{9,25},{17,1},{25,9},{2,18},{10... | collective-permute-start | bytes 196616 | tf_op jit(solution)/shard_map/ppermute | solution.py:351
  40.7 5.5 %collective-permute-start.12 = (bf16[16,1664]{1,0:T(8,128)(2,1)S(1)}, bf16[16,1664]{1,0:T(8,128)(2,1)S(1)}, u32[]{:S(2)}, u32[]{:S(2)}) collective-permute-start(bf16[16,1664]{1,0:T(8,128)(2,1)S(1)} %rows_2.4.refs_0_), channel_id=1, source_target_pairs={{0,3},{1,2},{2,1},{3,0},{4,7},{5,6},{6,5},{7,4},{8,11},{9,10},{10,... | collective-permute-start | bytes 159752 | tf_op jit(solution)/shard_map/ppermute | solution.py:351
  41.2 5.1 %collective-permute-start.11 = (bf16[16,1664]{1,0:T(8,128)(2,1)S(1)}, bf16[16,1664]{1,0:T(8,128)(2,1)S(1)}, u32[]{:S(2)}, u32[]{:S(2)}) collective-permute-start(bf16[16,1664]{1,0:T(8,128)(2,1)S(1)} %rows_2.4.refs_0_), channel_id=1, source_target_pairs={{0,1},{1,0},{2,3},{3,2},{4,5},{5,4},{6,7},{7,6},{8,9},{9,8},{10,11... | collective-permute-start | bytes 159752 | tf_op jit(solution)/shard_map/ppermute | solution.py:351
  46.7 5.6 %collective-permute-start.13 = (bf16[16,1664]{1,0:T(8,128)(2,1)S(1)}, bf16[16,1664]{1,0:T(8,128)(2,1)S(1)}, u32[]{:S(2)}, u32[]{:S(2)}) collective-permute-start(bf16[16,1664]{1,0:T(8,128)(2,1)S(1)} %add.16.refs_0_), channel_id=1, source_target_pairs={{0,4},{1,5},{2,6},{3,7},{4,0},{5,1},{6,2},{7,3},{8,12},{9,13},{10,... | collective-permute-start | bytes 159752 | tf_op jit(solution)/shard_map/ppermute | solution.py:351
  55.1 4.6 %collective-permute-start.15 = (bf16[16,2176]{1,0:T(8,128)(2,1)S(1)}, bf16[16,2176]{1,0:T(8,128)(2,1)S(1)}, u32[]{:S(2)}, u32[]{:S(2)}) collective-permute-start(bf16[16,2176]{1,0:T(8,128)(2,1)S(1)} %add.17.refs_0_), channel_id=1, source_target_pairs={{0,16},{8,24},{16,0},{24,8},{1,17},{9,25},{17,1},{25,9},{2,18},{10... | collective-permute-start | bytes 208904 | tf_op jit(solution)/shard_map/ppermute | solution.py:351
  57.2 4.3 %collective-permute-start.17 = (bf16[16,2048]{1,0:T(8,128)(2,1)S(1)}, bf16[16,2048]{1,0:T(8,128)(2,1)S(1)}, u32[]{:S(2)}, u32[]{:S(2)}) collective-permute-start(bf16[16,2048]{1,0:T(8,128)(2,1)S(1)} %add.18.refs_0_), channel_id=1, source_target_pairs={{0,16},{8,24},{16,0},{24,8},{1,17},{9,25},{17,1},{25,9},{2,18},{10... | collective-permute-start | bytes 196616 | tf_op jit(solution)/shard_map/ppermute | solution.py:351
  64.6 5.3 %collective-permute-start.22 = (bf16[16,1664]{1,0:T(8,128)(2,1)S(1)}, bf16[16,1664]{1,0:T(8,128)(2,1)S(1)}, u32[]{:S(2)}, u32[]{:S(2)}) collective-permute-start(bf16[16,1664]{1,0:T(8,128)(2,1)S(1)} %rows_2.5.refs_0_), channel_id=1, source_target_pairs={{0,3},{1,2},{2,1},{3,0},{4,7},{5,6},{6,5},{7,4},{8,11},{9,10},{10,... | collective-permute-start | bytes 159752 | tf_op jit(solution)/shard_map/ppermute | solution.py:351
  66.3 4.7 %collective-permute-start.21 = (bf16[16,1664]{1,0:T(8,128)(2,1)S(1)}, bf16[16,1664]{1,0:T(8,128)(2,1)S(1)}, u32[]{:S(2)}, u32[]{:S(2)}) collective-permute-start(bf16[16,1664]{1,0:T(8,128)(2,1)S(1)} %rows_2.5.refs_0_), channel_id=1, source_target_pairs={{0,1},{1,0},{2,3},{3,2},{4,5},{5,4},{6,7},{7,6},{8,9},{9,8},{10,11... | collective-permute-start | bytes 159752 | tf_op jit(solution)/shard_map/ppermute | solution.py:351
  71.6 5.7 %collective-permute-start.23 = (bf16[16,1664]{1,0:T(8,128)(2,1)S(1)}, bf16[16,1664]{1,0:T(8,128)(2,1)S(1)}, u32[]{:S(2)}, u32[]{:S(2)}) collective-permute-start(bf16[16,1664]{1,0:T(8,128)(2,1)S(1)} %add.19.refs_0_), channel_id=1, source_target_pairs={{0,4},{1,5},{2,6},{3,7},{4,0},{5,1},{6,2},{7,3},{8,12},{9,13},{10,... | collective-permute-start | bytes 159752 | tf_op jit(solution)/shard_map/ppermute | solution.py:351
  80.3 4.7 %collective-permute-start.25 = (bf16[16,2176]{1,0:T(8,128)(2,1)S(1)}, bf16[16,2176]{1,0:T(8,128)(2,1)S(1)}, u32[]{:S(2)}, u32[]{:S(2)}) collective-permute-start(bf16[16,2176]{1,0:T(8,128)(2,1)S(1)} %add.20.refs_0_), channel_id=1, source_target_pairs={{0,16},{8,24},{16,0},{24,8},{1,17},{9,25},{17,1},{25,9},{2,18},{10... | collective-permute-start | bytes 208904 | tf_op jit(solution)/shard_map/ppermute | solution.py:351
  82.9 4.3 %collective-permute-start.27 = (bf16[16,2048]{1,0:T(8,128)(2,1)S(1)}, bf16[16,2048]{1,0:T(8,128)(2,1)S(1)}, u32[]{:S(2)}, u32[]{:S(2)}) collective-permute-start(bf16[16,2048]{1,0:T(8,128)(2,1)S(1)} %add.21.refs_0_), channel_id=1, source_target_pairs={{0,16},{8,24},{16,0},{24,8},{1,17},{9,25},{17,1},{25,9},{2,18},{10... | collective-permute-start | bytes 196616 | tf_op jit(solution)/shard_map/ppermute | solution.py:351
  90.3 5.5 %collective-permute-start.32 = (bf16[16,1664]{1,0:T(8,128)(2,1)S(1)}, bf16[16,1664]{1,0:T(8,128)(2,1)S(1)}, u32[]{:S(2)}, u32[]{:S(2)}) collective-permute-start(bf16[16,1664]{1,0:T(8,128)(2,1)S(1)} %rows_2.6.refs_0_), channel_id=1, source_target_pairs={{0,3},{1,2},{2,1},{3,0},{4,7},{5,6},{6,5},{7,4},{8,11},{9,10},{10,... | collective-permute-start | bytes 159752 | tf_op jit(solution)/shard_map/ppermute | solution.py:351
  90.8 5.1 %collective-permute-start.31 = (bf16[16,1664]{1,0:T(8,128)(2,1)S(1)}, bf16[16,1664]{1,0:T(8,128)(2,1)S(1)}, u32[]{:S(2)}, u32[]{:S(2)}) collective-permute-start(bf16[16,1664]{1,0:T(8,128)(2,1)S(1)} %rows_2.6.refs_0_), channel_id=1, source_target_pairs={{0,1},{1,0},{2,3},{3,2},{4,5},{5,4},{6,7},{7,6},{8,9},{9,8},{10,11... | collective-permute-start | bytes 159752 | tf_op jit(solution)/shard_map/ppermute | solution.py:351
  96.3 5.1 %collective-permute-start.33 = (bf16[16,1664]{1,0:T(8,128)(2,1)S(1)}, bf16[16,1664]{1,0:T(8,128)(2,1)S(1)}, u32[]{:S(2)}, u32[]{:S(2)}) collective-permute-start(bf16[16,1664]{1,0:T(8,128)(2,1)S(1)} %add.22.refs_0_), channel_id=1, source_target_pairs={{0,4},{1,5},{2,6},{3,7},{4,0},{5,1},{6,2},{7,3},{8,12},{9,13},{10,... | collective-permute-start | bytes 159752 | tf_op jit(solution)/shard_map/ppermute | solution.py:351
  104.4 4.7 %collective-permute-start.35 = (bf16[16,2176]{1,0:T(8,128)(2,1)S(1)}, bf16[16,2176]{1,0:T(8,128)(2,1)S(1)}, u32[]{:S(2)}, u32[]{:S(2)}) collective-permute-start(bf16[16,2176]{1,0:T(8,128)(2,1)S(1)} %add.23.refs_0_), channel_id=1, source_target_pairs={{0,16},{8,24},{16,0},{24,8},{1,17},{9,25},{17,1},{25,9},{2,18},{10... | collective-permute-start | bytes 208904 | tf_op jit(solution)/shard_map/ppermute | solution.py:351
  106.6 4.3 %collective-permute-start.37 = (bf16[16,2048]{1,0:T(8,128)(2,1)S(1)}, bf16[16,2048]{1,0:T(8,128)(2,1)S(1)}, u32[]{:S(2)}, u32[]{:S(2)}) collective-permute-start(bf16[16,2048]{1,0:T(8,128)(2,1)S(1)} %add.24.refs_0_), channel_id=1, source_target_pairs={{0,16},{8,24},{16,0},{24,8},{1,17},{9,25},{17,1},{25,9},{2,18},{10... | collective-permute-start | bytes 196616 | tf_op jit(solution)/shard_map/ppermute | solution.py:351
  113.9 5.1 %collective-permute-start.42 = (bf16[16,1664]{1,0:T(8,128)(2,1)S(1)}, bf16[16,1664]{1,0:T(8,128)(2,1)S(1)}, u32[]{:S(2)}, u32[]{:S(2)}) collective-permute-start(bf16[16,1664]{1,0:T(8,128)(2,1)S(1)} %rows_2.7.refs_0_), channel_id=1, source_target_pairs={{0,3},{1,2},{2,1},{3,0},{4,7},{5,6},{6,5},{7,4},{8,11},{9,10},{10,... | collective-permute-start | bytes 159752 | tf_op jit(solution)/shard_map/ppermute | solution.py:351
  115.9 4.3 %collective-permute-start.41 = (bf16[16,1664]{1,0:T(8,128)(2,1)S(1)}, bf16[16,1664]{1,0:T(8,128)(2,1)S(1)}, u32[]{:S(2)}, u32[]{:S(2)}) collective-permute-start(bf16[16,1664]{1,0:T(8,128)(2,1)S(1)} %rows_2.7.refs_0_), channel_id=1, source_target_pairs={{0,1},{1,0},{2,3},{3,2},{4,5},{5,4},{6,7},{7,6},{8,9},{9,8},{10,11... | collective-permute-start | bytes 159752 | tf_op jit(solution)/shard_map/ppermute | solution.py:351
  121.2 5.5 %collective-permute-start.43 = (bf16[16,1664]{1,0:T(8,128)(2,1)S(1)}, bf16[16,1664]{1,0:T(8,128)(2,1)S(1)}, u32[]{:S(2)}, u32[]{:S(2)}) collective-permute-start(bf16[16,1664]{1,0:T(8,128)(2,1)S(1)} %add.25.refs_0_), channel_id=1, source_target_pairs={{0,4},{1,5},{2,6},{3,7},{4,0},{5,1},{6,2},{7,3},{8,12},{9,13},{10,... | collective-permute-start | bytes 159752 | tf_op jit(solution)/shard_map/ppermute | solution.py:351
  (35 other events, 225.0 us)
